TPU v7x, 256 devices: a whole 4x4x8 slice. The times are simulated.
256 devices in a mesh: section: 8 (over y, core), fsdp: 32 (over x, z).
Axes of the slice: x: 4, y: 4, z: 8, core: 2. Of those that a mesh axis runs over, the one named last changes fastest.
Arguments:
- grad: bfloat16 [12288, 8192], P(('section', 'fsdp')), parts along dimension 0, may hold values from -40 to 40
- momentum: float32 [12288, 8192], P(('section', 'fsdp')), parts along dimension 0, may hold values from -3 to 3
- left_stat: float32 [24, 32, 256, 512], P('section', 'fsdp'), parts along dimension 0, may hold values from -6 to 6
- right_stat: float32 [24, 32, 256, 512], P('section', 'fsdp'), parts along dimension 0, may hold values from -6 to 6
- left_root: bfloat16 [24, 32, 256, 512], P('section', 'fsdp'), parts along dimension 0, may hold values from -0.25 to 0.25
- right_root: bfloat16 [24, 32, 512, 256], P('section', 'fsdp'), parts along dimension 0, may hold values from -0.25 to 0.25
Outputs:
- new_momentum: float32 [12288, 8192], P(('section', 'fsdp')), parts along dimension 0
- new_left: float32 [24, 32, 256, 512], P('section', 'fsdp'), parts along dimension 0
- new_right: float32 [24, 32, 256, 512], P('section', 'fsdp'), parts along dimension 0
There are 8 independent parts, one for each index of `section`. A program takes and returns all parts, laid end to end along the dimension named above; each array names one. Nothing has to cross between parts.
All inputs are finite; a program needn't handle non-finite values.
Results may differ from a plain program's by a relative error of at most 0.003.
Values may be sent and summed in bfloat16 or wider, within the bound.
No kernel may reach another device: no remote copies, remote signals or barrier semaphores. Data moves between devices by JAX's collectives and lax.ppermute only.
A program may use at most 64 MiB of HBM per device.

v0:
```python
import math

import jax
import jax.numpy as jnp
from jax import lax
from jax.sharding import PartitionSpec as P

decay_stat = 0.95
momentum_rate = 0.9
epsilon = 1e-06


def from_partner(block, axis, bit):
    count = lax.axis_size(axis)
    route = []
    for low in range(count):
        high = low | 1 << bit
        if high != low and high < count:
            route += [(low, high), (high, low)]
    return lax.ppermute(block, axis, route)


def join_halves(own_part, partner, parity, axis):
    first = jnp.concatenate([own_part, partner], axis=axis)
    second = jnp.concatenate([partner, own_part], axis=axis)
    return jnp.where(parity == 0, first, second)


def local(grad, momentum, left_stat, right_stat, left_root, right_root):
    owners = lax.axis_size("fsdp")
    parity = lax.axis_index("fsdp") % 2
    rows_dev, all_cols = grad.shape
    row_blocks, _, half_width, block_size = left_stat.shape
    all_rows = rows_dev * owners
    clip_limit = 0.5 * math.sqrt(all_rows * all_cols)
    grad_wide = grad.astype(jnp.float32)
    total_sq = lax.psum(jnp.sum(grad_wide * grad_wide), "fsdp")
    pieces = grad.reshape(rows_dev, owners // 2, 1, block_size)
    pieces = jnp.broadcast_to(pieces, (rows_dev, owners // 2, 2, block_size))
    pieces = pieces.reshape(rows_dev, owners, block_size)
    column_block = lax.all_to_all(pieces, "fsdp", split_axis=1, concat_axis=0, tiled=True).reshape(
        all_rows, block_size
    )
    own_half = lax.dynamic_slice_in_dim(column_block, parity * half_width, half_width, 1)
    clip_factor = jnp.minimum(
        jnp.float32(1.0), jnp.float32(clip_limit) / (jnp.sqrt(total_sq) + epsilon)
    )
    grad_blocks = column_block.reshape(row_blocks, block_size, block_size)
    row_half = lax.dynamic_slice_in_dim(grad_blocks, parity * half_width, half_width, 1)
    col_half = own_half.reshape(row_blocks, block_size, half_width)
    left_gram = jnp.einsum(
        "rik,rjk->rij", row_half, grad_blocks, preferred_element_type=jnp.float32
    )
    right_gram = jnp.einsum(
        "rki,rkj->rij", col_half, grad_blocks, preferred_element_type=jnp.float32
    )
    coeff = (1.0 - decay_stat) * clip_factor * clip_factor
    new_left = decay_stat * left_stat + coeff * left_gram[:, None]
    new_right = decay_stat * right_stat + coeff * right_gram[:, None]
    left_apply = jnp.einsum(
        "rik,rkj->rij", left_root[:, 0], grad_blocks, preferred_element_type=jnp.float32
    ).astype(jnp.bfloat16)
    partner_apply = from_partner(left_apply, "fsdp", 0)
    applied = join_halves(left_apply, partner_apply, parity, 1)
    precond = jnp.einsum(
        "rik,rkj->rij", applied, right_root[:, 0], preferred_element_type=jnp.float32
    )
    blocks_wide = grad_blocks.astype(jnp.float32)
    gnorm = jnp.sum(blocks_wide * blocks_wide, axis=(1, 2))
    pnorm_own = jnp.sum(precond * precond, axis=(1, 2))
    pnorm = pnorm_own + from_partner(pnorm_own, "fsdp", 0)
    scale = clip_factor * jnp.sqrt(gnorm) / (jnp.sqrt(pnorm) + epsilon)
    update = (scale[:, None, None] * precond).astype(jnp.bfloat16).reshape(all_rows, half_width)
    returned = lax.all_to_all(update, "fsdp", split_axis=0, concat_axis=1, tiled=True)
    new_momentum = momentum_rate * momentum + returned.astype(jnp.float32)
    return (new_momentum, new_left, new_right)


def solution(mesh):
    return jax.shard_map(
        local,
        mesh=mesh,
        in_specs=(
            P(("section", "fsdp"), None),
            P(("section", "fsdp"), None),
            P("section", "fsdp", None, None),
            P("section", "fsdp", None, None),
            P("section", "fsdp", None, None),
            P("section", "fsdp", None, None),
        ),
        out_specs=(
            P(("section", "fsdp"), None),
            P("section", "fsdp", None, None),
            P("section", "fsdp", None, None),
        ),
        check_vma=False,
    )
```

profile of v0, /device:TPU:8, one launch (start us, length us, event | category | flops | bytes accessed | tf_op | source)
XLA Modules:
  0.0 167.2 jit_solution(15288381892562948768)
XLA Ops:
  0.6 0.0 copy-start
  0.6 1.3 copy.33
  1.9 0.2 broadcast_in_dim.5
  2.1 0.0 copy-start.5
  2.1 50.6 %all_to_all.28 = bf16[48,32,512]{2,0,1:T(8,128)(2,1)S(1)} all-to-all(bf16[48,32,512]{2,0,1:T(8,128)(2,1)S(1)} %bitcast.55), channel_id=1, replica_groups=mesh['section'=8,'fsdp'=32] {'fsdp'}, dimensions={1} | all-to-all | bytes 3145728 | tf_op jit(solution)/shard_map/all_to_all | solution.py:41
  52.7 0.0 copy-done.5
  52.7 0.0 copy-start.1
  52.7 0.6 convolution_convert_fusion
  53.3 2.6 %collective-permute-start = (bf16[3,256,512]{2,1,0:T(8,128)(2,1)S(1)}, bf16[3,256,512]{2,1,0:T(8,128)(2,1)}, u32[]{:S(2)}, u32[]{:S(2)}) collective-permute-start(bf16[3,256,512]{2,1,0:T(8,128)(2,1)S(1)} %convolution_convert_fusion), channel_id=1, source_target_pairs={{0,1},{1,0},{2,3},{3,2},{4,5},{5,4},{6,7},{7,6},{8,9},{9,8},{10,11... | collective-permute-start | bytes 2359304 | tf_op jit(solution)/shard_map/ppermute | solution.py:20
  55.9 0.0 copy-done.1
  55.9 1.0 multiply_reduce_fusion.2
  56.9 79.5 %psum.7 = f32[]{:T(128)} all-reduce(f32[]{:T(128)} %multiply_reduce_fusion.2), channel_id=1, replica_groups=mesh['section'=8,'fsdp'=32] {'fsdp'}, use_global_device_ids=true, to_apply=%region_1.2 | all-reduce | flops 1 | bytes 8 | tf_op jit(solution)/shard_map/psum | solution.py:37
  137.2 0.4 multiply_reduce_fusion
  137.6 0.1 reduce_sum.36
  137.7 0.1 reduce_sum.37
  137.8 0.0 collective-permute-done
  137.8 0.0 copy-done
  137.8 2.1 %multiply_reduce_fusion.1 = (f32[3]{0:T(128)S(1)}, f32[3,512,256]{2,1,0:T(8,128)S(1)}) fusion(bf16[3,1,512,256]{3,2,1,0:T(8,128)(2,1)S(1)} %copy-done, bf16[3,256,512]{2,1,0:T(8,128)(2,1)} %collective-permute-done, bf16[3,256,512]{2,1,0:T(8,128)(2,1)S(1)} %convolution_convert_fusion, pred[]{:T(512)S(6)} %eq.5), kind=kOutput, calls=%fused_computation.16 | convolution fusion | flops 410517504 | bytes 3932173 | tf_op jit(solution)/shard_map/rik,rkj->rij/dot_general | solution.py:65
  139.9 0.0 collective-permute-start.1
  139.9 3.5 %collective-permute-done.1 = f32[3]{0:T(128)S(1)} collective-permute-done((f32[3]{0:T(128)S(1)}, f32[3]{0:T(128)S(1)}, u32[]{:S(2)}, u32[]{:S(2)}) %collective-permute-start.1) | collective-permute-done | bytes 44 | tf_op jit(solution)/shard_map/ppermute | solution.py:20
  143.5 1.1 multiply_convert_fusion
  144.6 3.9 %all-to-all-start.1 = ((bf16[32,48,256]{2,1,0:T(8,128)(2,1)}), bf16[32,48,256]{2,1,0:T(8,128)(2,1)S(1)}, u32[]{:S(2)}, u32[]{:S(2)}) async-start(bf16[32,48,256]{2,1,0:T(8,128)(2,1)} %bitcast.7), calls=%async_computation.1 | async-start | bytes 1572864 | tf_op jit(solution)/shard_map/all_to_all | solution.py:74
  148.5 0.0 copy-start.2
  148.5 0.1 constant_dynamic-slice_fusion
  148.6 1.3 copy-done.2
  149.9 0.0 copy-start.3
  149.9 1.8 %fusion.7 = f32[3,1,256,512]{3,2,1,0:T(8,128)} fusion(f32[3,1,256,512]{3,2,1,0:T(8,128)S(1)} %copy-done.2, bf16[3,512,512]{2,1,0:T(8,128)(2,1)S(1)} %bitcast.53, s32[]{:T(128)S(6)} %select_n.22, f32[]{:T(128)S(6)} %mul.69), kind=kOutput, calls=%fused_computation.12 | convolution fusion | flops 403832832 | bytes 5505032 | tf_op jit(solution)/shard_map/rik,rjk->rij/dot_general | solution.py:51
  151.7 0.0 copy-done.3
  151.7 1.8 %fusion.6 = f32[3,1,256,512]{3,2,1,0:T(8,128)} fusion(f32[3,1,256,512]{3,2,1,0:T(8,128)S(1)} %copy-done.3, bf16[3,512,256]{2,1,0:T(8,128)(2,1)S(1)} %bitcast.59, bf16[3,512,512]{2,1,0:T(8,128)(2,1)S(1)} %bitcast.54, f32[]{:T(128)S(6)} %mul.69), kind=kOutput, calls=%fused_computation.9 | convolution fusion | flops 403832832 | bytes 5505028 | tf_op jit(solution)/shard_map/rki,rkj->rij/dot_general | solution.py:54
  153.5 10.8 %all-to-all-done.1 = bf16[32,48,256]{2,1,0:T(8,128)(2,1)S(1)} async-done(((bf16[32,48,256]{2,1,0:T(8,128)(2,1)}), bf16[32,48,256]{2,1,0:T(8,128)(2,1)S(1)}, u32[]{:S(2)}, u32[]{:S(2)}) %all-to-all-start.1) | async-done | bytes 786464 | tf_op jit(solution)/shard_map/all_to_all | solution.py:74
  164.3 0.2 convert_bitcast_fusion
  164.5 0.0 copy-start.4
  164.5 0.1 copy.31
  164.6 1.3 copy-done.4
  165.9 1.3 multiply_add_fusion
  (1 shorter events, 0.0 us)
Async XLA Ops:
  0.6 137.2 %copy-start = (bf16[3,1,512,256]{3,2,1,0:T(8,128)(2,1)S(1)}, bf16[3,1,512,256]{3,2,1,0:T(8,128)(2,1)}, u32[]{:S(2)}) copy-start(bf16[3,1,512,256]{3,2,1,0:T(8,128)(2,1)} %param.11) | copy-start | bytes 2359300
  2.1 50.6 %copy-start.5 = (bf16[3,1,256,512]{3,2,1,0:T(8,128)(2,1)S(1)}, bf16[3,1,256,512]{3,2,1,0:T(8,128)(2,1)}, u32[]{:S(2)}) copy-start(bf16[3,1,256,512]{3,2,1,0:T(8,128)(2,1)} %param.10) | copy-start | bytes 2359300
  52.7 3.2 %copy-start.1 = (bf16[48,8192]{1,0:T(8,128)(2,1)S(1)}, bf16[48,8192]{1,0:T(8,128)(2,1)}, u32[]{:S(2)}) copy-start(bf16[48,8192]{1,0:T(8,128)(2,1)} %param.6) | copy-start | bytes 2359300
  53.3 84.5 %collective-permute-start = (bf16[3,256,512]{2,1,0:T(8,128)(2,1)S(1)}, bf16[3,256,512]{2,1,0:T(8,128)(2,1)}, u32[]{:S(2)}, u32[]{:S(2)}) collective-permute-start(bf16[3,256,512]{2,1,0:T(8,128)(2,1)S(1)} %convolution_convert_fusion), channel_id=1, source_target_pairs={{0,1},{1,0},{2,3},{3,2},{4,5},{5,4},{6,7},{7,6},{8,9},{9,8},{10,11... | collective-permute-start | bytes 2359304 | tf_op jit(solution)/shard_map/ppermute | solution.py:20
  139.9 3.6 %collective-permute-start.1 = (f32[3]{0:T(128)S(1)}, f32[3]{0:T(128)S(1)}, u32[]{:S(2)}, u32[]{:S(2)}) collective-permute-start(f32[3]{0:T(128)S(1)} %get-tuple-element.12), channel_id=1, source_target_pairs={{0,1},{1,0},{2,3},{3,2},{4,5},{5,4},{6,7},{7,6},{8,9},{9,8},{10,11... | collective-permute-start | bytes 44 | tf_op jit(solution)/shard_map/ppermute | solution.py:20
  144.6 19.7 %all-to-all-start.1 = ((bf16[32,48,256]{2,1,0:T(8,128)(2,1)}), bf16[32,48,256]{2,1,0:T(8,128)(2,1)S(1)}, u32[]{:S(2)}, u32[]{:S(2)}) async-start(bf16[32,48,256]{2,1,0:T(8,128)(2,1)} %bitcast.7), calls=%async_computation.1 | async-start | bytes 1572864 | tf_op jit(solution)/shard_map/all_to_all | solution.py:74
  148.5 1.4 copy-start.2
  149.9 1.8 %copy-start.3 = (f32[3,1,256,512]{3,2,1,0:T(8,128)S(1)}, f32[3,1,256,512]{3,2,1,0:T(8,128)}, u32[]{:S(2)}) copy-start(f32[3,1,256,512]{3,2,1,0:T(8,128)} %param.9) | copy-start | bytes 4718596
  164.5 1.4 copy-start.4
where the time goes:
time: 168 us; the launch traced here: 167 us
  blocking collectives  130 us (77%)
  waiting for transfers between devices  14.4 us (9%)
  starting transfers between devices  6.57 us (4%)
  matrix products  6.2 us (4%)
  local copies, waits for them, and re-layouts  4.35 us (3%)
  other arithmetic  4.1 us (2%)
    psum x1, blocking collectives, local(): total_sq = lax.psum(jnp.sum(grad_wide * grad_wide), 'fsdp')  79.5 us
    all_to_all x1, blocking collectives, local(): lax.all_to_all(pieces, 'fsdp', split_axis=1, concat_axis=0, tiled=True)  50.6 us
    all_to_all x1, waiting for transfers between devices, local(): lax.all_to_all(update, 'fsdp', split_axis=0, concat_axis=1, tiled=True)  10.8 us
    all_to_all x1, starting transfers between devices, local(): lax.all_to_all(update, 'fsdp', split_axis=0, concat_axis=1, tiled=True)  3.91 us
    ppermute x2, waiting for transfers between devices, from_partner(): return lax.ppermute(block, axis, route)  3.53 us
  transfers between devices with their start and end apart: 3, of which 2 were waited for; matrix products, arithmetic and copies ran while one was open for 3% of the time, Pallas kernels for 0%

commit v1 on v0

v1 whole, which is shorter than its diff:
```python
import functools
import math

import jax
import jax.numpy as jnp
from jax import lax
from jax.experimental import pallas as pl
from jax.experimental.pallas import tpu as pltpu
from jax.sharding import PartitionSpec as P

decay_stat = 0.95
momentum_rate = 0.9
epsilon = 1e-06
lanes = 128
extra_rows = 8
ring_x = 4
ring_z = 8
pairs = ring_z // 2
origins = (0, -1, -2, -3, 1, 2, 3, 4)


def shifted(block, step_x, step_z):
    route = []
    for x in range(ring_x):
        for z in range(ring_z):
            there = (x + step_x) % ring_x * ring_z + (z + step_z(z)) % ring_z
            route.append((x * ring_z + z, there))
    return lax.ppermute(block, "fsdp", route)


def toward(block, steps):
    return shifted(block, 0, lambda z: steps if z % 2 else -steps)


def scalar_sum(value):
    return jnp.sum(jnp.sum(value, axis=0, keepdims=True), axis=1, keepdims=True)


def aligned(index, multiple):
    return pl.multiple_of(index * multiple, multiple)


def cut_kernel(place, grad, *rest):
    *slabs, sem = rest
    x = place[0] // ring_z
    width = slabs[0].shape[1]
    copies = []
    for i, slab in enumerate(slabs):
        at = pl.ds(aligned((x + 1 + i) % ring_x, width), width)
        copies.append(pltpu.make_async_copy(grad.at[:, at], slab, sem.at[i]))
        copies[-1].start()
    for copy in copies:
        copy.wait()


def pick_kernel(place, *rest):
    slabs, outs = rest[:ring_x], rest[ring_x:]
    z = place[0] % ring_z
    pair, parity = z // 2, z % 2
    width = outs[0].shape[2]
    for out, step in zip(outs, (2, 1 - 2 * parity, 2 * parity - 1, 0)):
        column = (pair + pairs + step) % pairs
        for d in range(ring_x):
            out[d] = slabs[d][:, pl.ds(aligned(column, width), width)]


def apply_kernel(place, *refs):
    groups, (own_root, partner_root, right_root) = refs[:8], refs[8:11]
    blocks, payload, root_v, right_v, sem = refs[11:]
    bring = pltpu.make_async_copy(right_root, right_v, sem)
    bring.start()
    me = place[0]
    x, z = me // ring_z, me % ring_z
    parity = z % 2
    sign = 1 - 2 * parity
    rows_dev = groups[0].shape[1]
    row_blocks, half, block_size = own_root.shape
    owners, length, _ = payload.shape
    body = length - extra_rows

    for group, origin in zip(groups, origins):
        for d in range(ring_x):
            source = (x + ring_x - d) % ring_x * ring_z + (z + ring_z + sign * origin) % ring_z
            blocks[pl.ds(aligned(source, rows_dev), rows_dev), :] = group[d]
    for root, side in ((own_root, parity), (partner_root, 1 - parity)):
        for r in range(row_blocks):
            root_v[r, pl.ds(aligned(side, half), half), :] = root[r]
    bring.wait()

    lane = lax.broadcasted_iota(jnp.int32, (8, lanes), 1)
    total = jnp.zeros((8, lanes), jnp.float32)
    for r in range(row_blocks):
        begin, end = r * block_size, (r + 1) * block_size
        block = blocks[begin:end, :]
        applied = jnp.dot(root_v[r], block, preferred_element_type=jnp.float32)
        precond = jnp.dot(
            applied.astype(jnp.bfloat16), right_v[r], preferred_element_type=jnp.float32
        )
        rounded = precond.astype(jnp.bfloat16)
        for f in range(begin // rows_dev, -(-end // rows_dev)):
            low, high = max(begin, f * rows_dev), min(end, (f + 1) * rows_dev)
            for c in range(half // lanes):
                at = c * rows_dev - f * rows_dev
                payload[f, at + low : at + high, :] = rounded[
                    low - begin : high - begin, c * lanes : (c + 1) * lanes
                ]
        wide = block.astype(jnp.float32)
        total += jnp.where(lane == r, scalar_sum(precond * precond), 0.0)
        total += jnp.where(lane == r + row_blocks, scalar_sum(wide * wide), 0.0)

    high = total.astype(jnp.bfloat16).astype(jnp.float32)
    middle = (total - high).astype(jnp.bfloat16).astype(jnp.float32)
    low = total - high - middle
    row = lax.broadcasted_iota(jnp.int32, (8, lanes), 0)
    parts = jnp.where(row == 0, high, jnp.where(row == 1, middle, jnp.where(row == 2, low, 0.0)))
    parts = parts.astype(jnp.bfloat16)
    for f in range(owners):
        payload[f, body : body + extra_rows, :] = parts


def gram_kernel(
    place, blocks, left_stat, right_stat, momentum,
    left_gram, right_gram, left_near, right_near, momentum_near, sem,
):
    bring = []
    for i, (far, near) in enumerate(
        ((left_stat, left_near), (right_stat, right_near), (momentum, momentum_near))
    ):
        bring.append(pltpu.make_async_copy(far, near, sem.at[i]))
        bring[-1].start()
    row_blocks, half, block_size = left_gram.shape
    parity = place[0] % 2
    for r in range(row_blocks):
        block = blocks[r * block_size : (r + 1) * block_size, :]
        rows = blocks[pl.ds(pl.multiple_of(r * block_size + parity * half, half), half), :]
        left_gram[r] = lax.dot_general(
            rows, block, (((1,), (1,)), ((), ())), preferred_element_type=jnp.float32
        )
    for side in range(2):

        @pl.when(parity == side)
        def _():
            for r in range(row_blocks):
                block = blocks[r * block_size : (r + 1) * block_size, :]
                right_gram[r] = lax.dot_general(
                    block[:, side * half : (side + 1) * half], block,
                    (((0,), (0,)), ((), ())), preferred_element_type=jnp.float32,
                )
    for copy in bring:
        copy.wait()


def finish_kernel(
    clip_limit, block_size, place,
    back, momentum, left_stat, right_stat, left_gram, right_gram,
    new_momentum, new_left, new_right, momentum_v, stat_v, out_sem, stat_out_sem,
):
    me = place[0]
    rows_dev, all_cols = momentum.shape
    owners, length, _ = back.shape
    row_blocks, half, _ = left_stat.shape
    pieces = out_sem.shape[0]
    width = all_cols // pieces
    share = owners // pieces
    columns = all_cols // owners
    body = length - extra_rows

    parts = back[:, body : body + extra_rows, :].astype(jnp.float32)
    values = parts[:, 0, :] + parts[:, 1, :] + parts[:, 2, :]
    lane = lax.broadcasted_iota(jnp.int32, values.shape, 1)
    source = lax.broadcasted_iota(jnp.int32, values.shape, 0)
    even = source % 2 == 0
    paired = jnp.where(even, pltpu.roll(values, owners - 1, 0), pltpu.roll(values, 1, 0))
    pnorm = values + paired
    gnorm = pltpu.roll(values, lanes - row_blocks, 1)
    total_sq = scalar_sum(jnp.where(even & (lane < row_blocks), gnorm, 0.0))
    clip_factor = jnp.minimum(1.0, clip_limit / (jnp.sqrt(total_sq) + epsilon))
    coeff = (1.0 - decay_stat) * clip_factor * clip_factor
    puts = []
    for side, (stat, gram, out) in enumerate(
        ((left_stat, left_gram, new_left), (right_stat, right_gram, new_right))
    ):
        for r in range(row_blocks):
            i = side * row_blocks + r
            stat_v[i] = decay_stat * stat[r] + coeff * gram[r]
            puts.append(pltpu.make_async_copy(stat_v.at[i], out.at[r], stat_out_sem.at[i]))
            puts[-1].start()

    scale = clip_factor * jnp.sqrt(gnorm) / (jnp.sqrt(pnorm) + epsilon)
    first = me * rows_dev // block_size
    until = (first + 1) * block_size - me * rows_dev
    upper = jnp.sum(jnp.where(lane == first, scale, 0.0), axis=1, keepdims=True)
    lower = jnp.sum(
        jnp.where((lane == first + 1) & (lane < row_blocks), scale, 0.0), axis=1, keepdims=True
    )
    in_upper = lax.broadcasted_iota(jnp.int32, (rows_dev, lanes), 0) < until
    for q in range(pieces):
        for s in range(q * share, (q + 1) * share):
            row_scale = jnp.where(in_upper, upper[s : s + 1], lower[s : s + 1])
            for c in range(columns // lanes):
                at = pl.ds(s * columns + c * lanes, lanes)
                moved = back[s, c * rows_dev : (c + 1) * rows_dev, :].astype(jnp.float32)
                momentum_v[:, at] = momentum_rate * momentum[:, at] + row_scale * moved
        part = pl.ds(q * width, width)
        puts.append(
            pltpu.make_async_copy(momentum_v.at[:, part], new_momentum.at[:, part], out_sem.at[q])
        )
        puts[-1].start()
    for copy in puts:
        copy.wait()


def keep_in_hbm(array):
    return pltpu.with_memory_space_constraint(array, pltpu.HBM)


def local(grad, momentum, left_stat, right_stat, left_root, right_root):
    owners = ring_x * ring_z
    me = lax.axis_index("fsdp")
    place = me.astype(jnp.int32).reshape(1)
    rows_dev, all_cols = grad.shape
    row_blocks, _, half, block_size = left_stat.shape
    all_rows = rows_dev * owners
    clip_limit = 0.5 * math.sqrt(all_rows * all_cols)
    length = rows_dev * half // lanes + extra_rows
    slab_width = all_cols // ring_x
    smem = pl.BlockSpec(memory_space=pltpu.SMEM)
    in_hbm = pl.BlockSpec(memory_space=pltpu.HBM)
    in_vmem = pl.BlockSpec(memory_space=pltpu.VMEM)
    some_vmem = pltpu.CompilerParams(vmem_limit_bytes=16 << 20)
    flops = row_blocks * 2 * half * block_size * block_size
    dma = pltpu.SemaphoreType.DMA

    def cost(flops, megabytes):
        return pl.CostEstimate(flops=flops, bytes_accessed=megabytes << 20, transcendentals=0)

    def array(*shape, dtype=jnp.bfloat16):
        return jax.ShapeDtypeStruct(shape, dtype)

    left_root = left_root.reshape(row_blocks, half, block_size)
    right_root = right_root.reshape(row_blocks, block_size, half)
    left_stat = left_stat.reshape(row_blocks, half, block_size)
    right_stat = right_stat.reshape(row_blocks, half, block_size)

    *slabs, own_slab = pl.pallas_call(
        cut_kernel,
        out_shape=[array(rows_dev, slab_width)] * ring_x,
        in_specs=[smem, in_hbm],
        out_specs=[in_vmem] * ring_x,
        scratch_shapes=[dma((ring_x,))],
        cost_estimate=cost(0, 1),
        name="cut",
    )(place, keep_in_hbm(grad))
    slabs = [shifted(slab, d + 1, lambda z: 0) for d, slab in enumerate(slabs)]
    swap = functools.partial(
        lax.ppermute, axis_name="fsdp", perm=[(i, i ^ 1) for i in range(owners)]
    )
    left_partner = swap(left_root)
    far, same, cross, own = pl.pallas_call(
        pick_kernel,
        out_shape=[array(ring_x, rows_dev, block_size)] * 4,
        in_specs=[smem] + [in_vmem] * ring_x,
        out_specs=[in_vmem] * 4,
        cost_estimate=cost(0, 2),
        name="pick",
    )(place, own_slab, *slabs)
    far = toward(far, 3)
    same = toward(same, -2)
    cross = toward(cross, 1)
    groups = [own, cross, same, far]
    groups += [swap(group) for group in groups]

    blocks, payload = pl.pallas_call(
        apply_kernel,
        out_shape=[array(all_rows, block_size), array(owners, length, lanes)],
        in_specs=[smem] + [in_vmem] * 10 + [in_hbm],
        out_specs=[in_vmem] * 2,
        scratch_shapes=[
            pltpu.VMEM((row_blocks, block_size, block_size), jnp.bfloat16),
            pltpu.VMEM((row_blocks, block_size, half), jnp.bfloat16),
            dma,
        ],
        compiler_params=some_vmem,
        cost_estimate=cost(3 * flops, 6),
        name="apply",
    )(place, *groups, left_root, left_partner, keep_in_hbm(right_root))
    back = lax.all_to_all(payload, "fsdp", split_axis=0, concat_axis=0, tiled=True)

    stat = array(row_blocks, half, block_size, dtype=jnp.float32)
    wide = array(rows_dev, all_cols, dtype=jnp.float32)
    grams = pl.pallas_call(
        gram_kernel,
        out_shape=[stat] * 4 + [wide],
        in_specs=[smem, in_vmem] + [in_hbm] * 3,
        out_specs=[in_vmem] * 5,
        scratch_shapes=[dma((3,))],
        compiler_params=some_vmem,
        cost_estimate=cost(2 * flops, 8),
        name="grams",
    )(place, blocks, *map(keep_in_hbm, (left_stat, right_stat, momentum)))
    left_gram, right_gram, left_near, right_near, momentum_near = grams

    quarters = 4
    new_momentum, new_left, new_right = pl.pallas_call(
        functools.partial(finish_kernel, clip_limit, block_size),
        out_shape=[wide, stat, stat],
        in_specs=[smem] + [in_vmem] * 6,
        out_specs=[in_hbm] * 3,
        scratch_shapes=[
            pltpu.VMEM((rows_dev, all_cols), jnp.float32),
            pltpu.VMEM((2 * row_blocks, half, block_size), jnp.float32),
            dma((quarters,)),
            dma((2 * row_blocks,)),
        ],
        compiler_params=some_vmem,
        cost_estimate=cost(1 << 22, 10),
        name="finish",
    )(place, back, momentum_near, left_near, right_near, left_gram, right_gram)
    shape = (row_blocks, 1, half, block_size)
    return (new_momentum, new_left.reshape(shape), new_right.reshape(shape))


def solution(mesh):
    return jax.shard_map(
        local,
        mesh=mesh,
        in_specs=(
            P(("section", "fsdp"), None),
            P(("section", "fsdp"), None),
            P("section", "fsdp", None, None),
            P("section", "fsdp", None, None),
            P("section", "fsdp", None, None),
            P("section", "fsdp", None, None),
        ),
        out_specs=(
            P(("section", "fsdp"), None),
            P("section", "fsdp", None, None),
            P("section", "fsdp", None, None),
        ),
        check_vma=False,
    )
```

time: 168 us -> 101 us (0.60)
  blocking collectives: 130 us -> 0 us
  waiting for transfers between devices: 14.4 us -> 40.2 us
  starting transfers between devices: 6.57 us -> 31.7 us
  Pallas kernels: 0 us -> 13.1 us
  local copies, waits for them, and re-layouts: 4.35 us -> 14.5 us
  matrix products: 6.2 us -> 0 us
  other arithmetic: 4.1 us -> 0 us
    psum x1 -> x0, blocking collectives: 79.5 us -> none  [local(): total_sq = lax.psum(jnp.sum(grad_wide * grad_wide), 'fsdp')]
    all_to_all x1 -> x0, blocking collectives: 50.6 us -> none  [local(): lax.all_to_all(pieces, 'fsdp', split_axis=1, concat_axis=0, tiled=True)]
    ppermute x2 -> x11, waiting for transfers between devices: 3.53 us -> 24.5 us  [the longest x6 16.7 us: shifted(): return lax.ppermute(block, 'fsdp', route)]
    ppermute x2 -> x11, starting transfers between devices: 2.66 us -> 21.9 us  [the longest x6 15.3 us: shifted(): return lax.ppermute(block, 'fsdp', route)]
    pallas_call x0 -> x5, Pallas kernels: none -> 13.1 us  [the longest x1 3.72 us: local(): pl.pallas_call(apply_kernel, out_shape=[array(all_rows, block_size), arra...]
    unnamed x12 -> x30, local copies, waits for them, and re-layouts: 2.63 us -> 14.5 us
    dot_general x4 -> x0, matrix products: 6.2 us -> none  [the longest x1 2.08 us: local(): jnp.einsum('rik,rkj->rij', applied, right_root[:, 0], preferred_element_t...]
    all_to_all x1, starting transfers between devices: 3.91 us -> 9.84 us  [local(): lax.all_to_all(payload, 'fsdp', split_axis=0, concat_axis=0, tiled=True)]
  transfers between devices with their start and end apart: 3 -> 12, of which waited for: 2 -> 8; matrix products, arithmetic and copies ran while one was open for 3% -> 0% of each run, Pallas kernels for 0% -> 7%
where the time goes in v1:
time: 101 us; the launch traced here: 100 us
  waiting for transfers between devices  40.2 us (40%)
  starting transfers between devices  31.7 us (31%)
  local copies, waits for them, and re-layouts  14.5 us (14%)
  Pallas kernels  13.1 us (13%)
    ppermute x6, waiting for transfers between devices, shifted(): return lax.ppermute(block, 'fsdp', route)  16.7 us
    all_to_all x1, waiting for transfers between devices, local(): lax.all_to_all(payload, 'fsdp', split_axis=0, concat_axis=0, tiled=True)  15.7 us
    ppermute x6, starting transfers between devices, shifted(): return lax.ppermute(block, 'fsdp', route)  15.3 us
    unnamed x30, local copies, waits for them, and re-layouts  14.5 us
    all_to_all x1, starting transfers between devices, local(): lax.all_to_all(payload, 'fsdp', split_axis=0, concat_axis=0, tiled=True)  9.84 us
    ppermute x4, waiting for transfers between devices, local(): groups += [swap(group) for group in groups]  7.81 us
    ppermute x4, starting transfers between devices, local(): groups += [swap(group) for group in groups]  4.63 us
    pallas_call x1, Pallas kernels, local(): pl.pallas_call(apply_kernel, out_shape=[array(all_rows, block_size), arra...  3.72 us
  transfers between devices with their start and end apart: 12, of which 8 were waited for; matrix products, arithmetic and copies ran while one was open for 0% of the time, Pallas kernels for 7%

profile of v1, /device:TPU:8, one launch (start us, length us, event | category | flops | bytes accessed | tf_op | source)
XLA Modules:
  0.0 100.1 jit_solution(15368378031234676181)
XLA Ops:
  0.6 0.0 copy-start.10
  0.6 2.0 %collective-permute-start.10 = (bf16[3,256,512]{2,1,0:T(8,128)(2,1)}, bf16[3,256,512]{2,1,0:T(8,128)(2,1)S(1)}, u32[]{:S(2)}, u32[]{:S(2)}) collective-permute-start(bf16[3,256,512]{2,1,0:T(8,128)(2,1)} %bitcast.11), channel_id=1, source_target_pairs={{0,1},{1,0},{2,3},{3,2},{4,5},{5,4},{6,7},{7,6},{8,9},{9,8},{10,11... | collective-permute-start | bytes 2359304 | tf_op jit(solution)/shard_map/ppermute | solution.py:258
  2.6 2.1 %cut.1 = (bf16[48,2048]{1,0:T(8,128)(2,1)}, bf16[48,2048]{1,0:T(8,128)(2,1)}, bf16[48,2048]{1,0:T(8,128)(2,1)}, bf16[48,2048]{1,0:T(8,128)(2,1)}) custom-call(s32[1]{0:T(128)} %bitcast.place, bf16[48,8192]{1,0:T(8,128)(2,1)} %grad.1), custom_call_target="tpu_custom_call" | custom-call | bytes 1048576 | tf_op jit(solution)/shard_map/cut/pallas_call | solution.py:245
  4.8 1.6 %collective-permute-start = (bf16[48,2048]{1,0:T(8,128)(2,1)}, bf16[48,2048]{1,0:T(8,128)(2,1)S(1)}, u32[]{:S(2)}, u32[]{:S(2)}) collective-permute-start(bf16[48,2048]{1,0:T(8,128)(2,1)} %get-tuple-element.22), channel_id=1, source_target_pairs={{0,8},{1,9},{2,10},{3,11},{4,12},{5,13},{6,14},{7,15},{8,16},{9,17... | collective-permute-start | bytes 589832 | tf_op jit(solution)/shard_map/ppermute | solution.py:28
  6.3 2.7 %collective-permute-start.1 = (bf16[48,2048]{1,0:T(8,128)(2,1)}, bf16[48,2048]{1,0:T(8,128)(2,1)S(1)}, u32[]{:S(2)}, u32[]{:S(2)}) collective-permute-start(bf16[48,2048]{1,0:T(8,128)(2,1)} %get-tuple-element.23), channel_id=1, source_target_pairs={{0,16},{1,17},{2,18},{3,19},{4,20},{5,21},{6,22},{7,23},{8,24},{9,... | collective-permute-start | bytes 589832 | tf_op jit(solution)/shard_map/ppermute | solution.py:28
  9.1 1.4 %collective-permute-start.2 = (bf16[48,2048]{1,0:T(8,128)(2,1)}, bf16[48,2048]{1,0:T(8,128)(2,1)S(1)}, u32[]{:S(2)}, u32[]{:S(2)}) collective-permute-start(bf16[48,2048]{1,0:T(8,128)(2,1)} %get-tuple-element.24), channel_id=1, source_target_pairs={{0,24},{1,25},{2,26},{3,27},{4,28},{5,29},{6,30},{7,31},{8,0},{9,1... | collective-permute-start | bytes 589832 | tf_op jit(solution)/shard_map/ppermute | solution.py:28
  10.5 2.6 %collective-permute-done.rest_1_ = bf16[48,2048]{1,0:T(8,128)(2,1)S(1)} collective-permute-done((bf16[48,2048]{1,0:T(8,128)(2,1)}, bf16[48,2048]{1,0:T(8,128)(2,1)S(1)}, u32[]{:S(2)}, u32[]{:S(2)}) %collective-permute-start) | collective-permute-done | bytes 196640 | tf_op jit(solution)/shard_map/ppermute | solution.py:28
  13.1 0.0 copy-start.12
  13.1 4.7 %collective-permute-done.1.rest_2_ = bf16[48,2048]{1,0:T(8,128)(2,1)S(1)} collective-permute-done((bf16[48,2048]{1,0:T(8,128)(2,1)}, bf16[48,2048]{1,0:T(8,128)(2,1)S(1)}, u32[]{:S(2)}, u32[]{:S(2)}) %collective-permute-start.1) | collective-permute-done | bytes 196640 | tf_op jit(solution)/shard_map/ppermute | solution.py:28
  17.8 0.0 copy-start.13
  17.8 0.0 collective-permute-done.2.rest_3_
  17.8 0.0 copy-start.14
  17.8 0.0 copy-done.12
  17.8 0.7 copy-done.13
  18.5 0.1 copy-done.14
  18.6 2.2 %pick.1 = (bf16[4,48,512]{2,1,0:T(8,128)(2,1)}, bf16[4,48,512]{2,1,0:T(8,128)(2,1)}, bf16[4,48,512]{2,1,0:T(8,128)(2,1)}, bf16[4,48,512]{2,1,0:T(8,128)(2,1)}) custom-call(s32[1]{0:T(128)} %bitcast.place, bf16[48,2048]{1,0:T(8,128)(2,1)} %get-tuple-element.21.rest_0_, bf16[48,2048]{1,0:T(8,128)(2,1)} %copy-done.12, bf16[48,2048]{1,0:T(8,128)(2,1)} %copy-done.13, ...), custom_call_target="tpu_custom_call" | custom-call | bytes 2097152 | tf_op jit(solution)/shard_map/pick/pallas_call | solution.py:259
  20.8 4.9 %collective-permute-start.3 = (bf16[4,48,512]{2,1,0:T(8,128)(2,1)}, bf16[4,48,512]{2,1,0:T(8,128)(2,1)S(1)}, u32[]{:S(2)}, u32[]{:S(2)}) collective-permute-start(bf16[4,48,512]{2,1,0:T(8,128)(2,1)} %get-tuple-element.26), channel_id=1, source_target_pairs={{0,7},{1,2},{2,1},{3,4},{4,3},{5,6},{6,5},{7,0},{8,15},{9,10},{10,... | collective-permute-start | bytes 589832 | tf_op jit(solution)/shard_map/ppermute | solution.py:28
  25.7 0.0 collective-permute-start.4
  25.7 4.6 %collective-permute-start.5 = (bf16[4,48,512]{2,1,0:T(8,128)(2,1)}, bf16[4,48,512]{2,1,0:T(8,128)(2,1)S(1)}, u32[]{:S(2)}, u32[]{:S(2)}) collective-permute-start(bf16[4,48,512]{2,1,0:T(8,128)(2,1)} %get-tuple-element.28), channel_id=1, source_target_pairs={{0,5},{1,4},{2,7},{3,6},{4,1},{5,0},{6,3},{7,2},{8,13},{9,12},{10,... | collective-permute-start | bytes 589832 | tf_op jit(solution)/shard_map/ppermute | solution.py:28
  30.3 0.0 collective-permute-start.6
  30.3 8.2 %collective-permute-done.3.refs_1_ = bf16[4,48,512]{2,1,0:T(8,128)(2,1)S(1)} collective-permute-done((bf16[4,48,512]{2,1,0:T(8,128)(2,1)}, bf16[4,48,512]{2,1,0:T(8,128)(2,1)S(1)}, u32[]{:S(2)}, u32[]{:S(2)}) %collective-permute-start.3) | collective-permute-done | bytes 196640 | tf_op jit(solution)/shard_map/ppermute | solution.py:28
  38.5 0.0 collective-permute-start.7
  38.5 0.0 collective-permute-done.4.refs_2_
  38.5 2.0 %collective-permute-start.8 = (bf16[4,48,512]{2,1,0:T(8,128)(2,1)S(1)}, bf16[4,48,512]{2,1,0:T(8,128)(2,1)S(1)}, u32[]{:S(2)}, u32[]{:S(2)}) collective-permute-start(bf16[4,48,512]{2,1,0:T(8,128)(2,1)S(1)} %collective-permute-done.4.refs_2_), channel_id=1, source_target_pairs={{0,1},{1,0},{2,3},{3,2},{4,5},{5,4},{6,7},{7,6},{8,9},{9,8},{10,11... | collective-permute-start | bytes 589832 | tf_op jit(solution)/shard_map/ppermute | solution.py:271
  40.5 1.2 %collective-permute-done.5.refs_3_ = bf16[4,48,512]{2,1,0:T(8,128)(2,1)S(1)} collective-permute-done((bf16[4,48,512]{2,1,0:T(8,128)(2,1)}, bf16[4,48,512]{2,1,0:T(8,128)(2,1)S(1)}, u32[]{:S(2)}, u32[]{:S(2)}) %collective-permute-start.5) | collective-permute-done | bytes 196640 | tf_op jit(solution)/shard_map/ppermute | solution.py:28
  41.7 2.6 %collective-permute-start.9 = (bf16[4,48,512]{2,1,0:T(8,128)(2,1)S(1)}, bf16[4,48,512]{2,1,0:T(8,128)(2,1)S(1)}, u32[]{:S(2)}, u32[]{:S(2)}) collective-permute-start(bf16[4,48,512]{2,1,0:T(8,128)(2,1)S(1)} %collective-permute-done.5.refs_3_), channel_id=1, source_target_pairs={{0,1},{1,0},{2,3},{3,2},{4,5},{5,4},{6,7},{7,6},{8,9},{9,8},{10,11... | collective-permute-start | bytes 589832 | tf_op jit(solution)/shard_map/ppermute | solution.py:271
  44.3 0.0 collective-permute-done.6.refs_4_
  44.3 2.0 %collective-permute-done.7.refs_5_ = bf16[4,48,512]{2,1,0:T(8,128)(2,1)S(1)} collective-permute-done((bf16[4,48,512]{2,1,0:T(8,128)(2,1)S(1)}, bf16[4,48,512]{2,1,0:T(8,128)(2,1)S(1)}, u32[]{:S(2)}, u32[]{:S(2)}) %collective-permute-start.7) | collective-permute-done | bytes 196640 | tf_op jit(solution)/shard_map/ppermute | solution.py:271
  46.3 3.7 %collective-permute-done.8.refs_6_ = bf16[4,48,512]{2,1,0:T(8,128)(2,1)S(1)} collective-permute-done((bf16[4,48,512]{2,1,0:T(8,128)(2,1)S(1)}, bf16[4,48,512]{2,1,0:T(8,128)(2,1)S(1)}, u32[]{:S(2)}, u32[]{:S(2)}) %collective-permute-start.8) | collective-permute-done | bytes 196640 | tf_op jit(solution)/shard_map/ppermute | solution.py:271
  50.0 2.1 %collective-permute-done.9.refs_7_ = bf16[4,48,512]{2,1,0:T(8,128)(2,1)S(1)} collective-permute-done((bf16[4,48,512]{2,1,0:T(8,128)(2,1)S(1)}, bf16[4,48,512]{2,1,0:T(8,128)(2,1)S(1)}, u32[]{:S(2)}, u32[]{:S(2)}) %collective-permute-start.9) | collective-permute-done | bytes 196640 | tf_op jit(solution)/shard_map/ppermute | solution.py:271
  52.1 0.0 collective-permute-done.10.refs_9_
  52.1 0.0 copy-done.10
  52.1 0.0 copy-start.11
  52.1 0.9 copy-done.11
  53.0 3.7 %apply.1 = (bf16[1536,512]{1,0:T(8,128)(2,1)S(1)}, bf16[32,104,128]{2,1,0:T(8,128)(2,1)}) custom-call(s32[1]{0:T(128)} %bitcast.place, bf16[4,48,512]{2,1,0:T(8,128)(2,1)S(1)} %copy-done.11, bf16[4,48,512]{2,1,0:T(8,128)(2,1)S(1)} %collective-permute-done.3.refs_1_, bf16[4,48,512]{2,1,0:T(8,128)(2,1)S(1)} %collective-permute-done.4.refs_2_, ...), custom_call_target="tpu_custom_call" | custom-call | flops 1207959552 | bytes 6291456 | tf_op jit(solution)/shard_map/apply/pallas_call | solution.py:273
  56.8 9.8 %all-to-all-start = ((bf16[32,104,128]{2,1,0:T(8,128)(2,1)}), bf16[32,104,128]{2,1,0:T(8,128)(2,1)S(1)}, u32[]{:S(2)}, u32[]{:S(2)}) async-start(bf16[32,104,128]{2,1,0:T(8,128)(2,1)} %get-tuple-element.29), calls=%async_computation | async-start | bytes 1703936 | tf_op jit(solution)/shard_map/all_to_all | solution.py:287
  66.6 2.5 %grams.1 = (f32[3,256,512]{2,1,0:T(8,128)S(1)}, f32[3,256,512]{2,1,0:T(8,128)S(1)}, f32[3,256,512]{2,1,0:T(8,128)S(1)}, f32[3,256,512]{2,1,0:T(8,128)S(1)}, f32[48,8192]{1,0:T(8,128)S(1)}) custom-call(s32[1]{0:T(128)} %bitcast.place, bf16[1536,512]{1,0:T(8,128)(2,1)S(1)} %get-tuple-element.30.blocks, f32[3,256,512]{2,1,0:T(8,128)} %bitcast.13, ...), custom_call_target="tpu_custom_call" | custom-call | flops 805306368 | bytes 8388608 | tf_op jit(solution)/shard_map/grams/pallas_call | solution.py:291
  69.1 0.0 copy-start
  69.1 1.2 %copy-done = f32[3,256,512]{2,1,0:T(8,128)} copy-done((f32[3,256,512]{2,1,0:T(8,128)}, f32[3,256,512]{2,1,0:T(8,128)S(1)}, u32[]{:S(2)}) %copy-start) | copy-done | bytes 1572888
  70.3 0.0 copy-start.2
  70.3 1.1 %copy-done.2 = f32[3,256,512]{2,1,0:T(8,128)} copy-done((f32[3,256,512]{2,1,0:T(8,128)}, f32[3,256,512]{2,1,0:T(8,128)S(1)}, u32[]{:S(2)}) %copy-start.2) | copy-done | bytes 1572888
  71.4 0.0 copy-start.4
  71.5 1.1 %copy-done.4 = f32[3,256,512]{2,1,0:T(8,128)} copy-done((f32[3,256,512]{2,1,0:T(8,128)}, f32[3,256,512]{2,1,0:T(8,128)S(1)}, u32[]{:S(2)}) %copy-start.4) | copy-done | bytes 1572888
  72.6 0.0 copy-start.6
  72.6 1.1 %copy-done.6 = f32[3,256,512]{2,1,0:T(8,128)} copy-done((f32[3,256,512]{2,1,0:T(8,128)}, f32[3,256,512]{2,1,0:T(8,128)S(1)}, u32[]{:S(2)}) %copy-start.6) | copy-done | bytes 1572888
  73.7 0.0 copy-start.8
  73.7 1.1 %copy-done.8 = f32[48,8192]{1,0:T(8,128)} copy-done((f32[48,8192]{1,0:T(8,128)}, f32[48,8192]{1,0:T(8,128)S(1)}, u32[]{:S(2)}) %copy-start.8) | copy-done | bytes 1572888
  74.9 15.7 %all-to-all-done.back = bf16[32,104,128]{2,1,0:T(8,128)(2,1)S(1)} async-done(((bf16[32,104,128]{2,1,0:T(8,128)(2,1)}), bf16[32,104,128]{2,1,0:T(8,128)(2,1)S(1)}, u32[]{:S(2)}, u32[]{:S(2)}) %all-to-all-start) | async-done | bytes 852000 | tf_op jit(solution)/shard_map/all_to_all | solution.py:287
  90.5 0.0 copy-start.1
  90.5 1.4 %copy-done.1 = f32[3,256,512]{2,1,0:T(8,128)S(1)} copy-done((f32[3,256,512]{2,1,0:T(8,128)S(1)}, f32[3,256,512]{2,1,0:T(8,128)}, u32[]{:S(2)}) %copy-start.1) | copy-done | bytes 1572888
  91.9 0.0 copy-start.3
  92.0 1.4 %copy-done.3 = f32[3,256,512]{2,1,0:T(8,128)S(1)} copy-done((f32[3,256,512]{2,1,0:T(8,128)S(1)}, f32[3,256,512]{2,1,0:T(8,128)}, u32[]{:S(2)}) %copy-start.3) | copy-done | bytes 1572888
  93.4 0.0 copy-start.5
  93.4 1.4 %copy-done.5 = f32[3,256,512]{2,1,0:T(8,128)S(1)} copy-done((f32[3,256,512]{2,1,0:T(8,128)S(1)}, f32[3,256,512]{2,1,0:T(8,128)}, u32[]{:S(2)}) %copy-start.5) | copy-done | bytes 1572888
  94.8 0.0 copy-start.7
  94.8 1.4 %copy-done.7 = f32[3,256,512]{2,1,0:T(8,128)S(1)} copy-done((f32[3,256,512]{2,1,0:T(8,128)S(1)}, f32[3,256,512]{2,1,0:T(8,128)}, u32[]{:S(2)}) %copy-start.7) | copy-done | bytes 1572888
  96.2 0.0 copy-start.9
  96.2 1.4 %copy-done.9 = f32[48,8192]{1,0:T(8,128)S(1)} copy-done((f32[48,8192]{1,0:T(8,128)S(1)}, f32[48,8192]{1,0:T(8,128)}, u32[]{:S(2)}) %copy-start.9) | copy-done | bytes 1572888
  97.6 2.5 %finish.1 = (f32[48,8192]{1,0:T(8,128)}, f32[3,256,512]{2,1,0:T(8,128)}, f32[3,256,512]{2,1,0:T(8,128)}) custom-call(s32[1]{0:T(128)} %bitcast.place, bf16[32,104,128]{2,1,0:T(8,128)(2,1)S(1)} %all-to-all-done.back, f32[48,8192]{1,0:T(8,128)S(1)} %copy-done.9, f32[3,256,512]{2,1,0:T(8,128)S(1)} %copy-done.5, f32[3,256,512]{2,1,0:T(8,128)S(1)} %copy-done.7, ...), custom_call_target="tpu_custom_call" | custom-call | flops 4194304 | bytes 10485760 | tf_op jit(solution)/shard_map/finish/pallas_call | solution.py:304
Async XLA Ops:
  0.6 51.5 %copy-start.10 = (bf16[3,1,256,512]{3,2,1,0:T(8,128)(2,1)S(1)}, bf16[3,1,256,512]{3,2,1,0:T(8,128)(2,1)}, u32[]{:S(2)}) copy-start(bf16[3,1,256,512]{3,2,1,0:T(8,128)(2,1)} %param.10) | copy-start | bytes 2359300
  0.6 51.5 %collective-permute-start.10 = (bf16[3,256,512]{2,1,0:T(8,128)(2,1)}, bf16[3,256,512]{2,1,0:T(8,128)(2,1)S(1)}, u32[]{:S(2)}, u32[]{:S(2)}) collective-permute-start(bf16[3,256,512]{2,1,0:T(8,128)(2,1)} %bitcast.11), channel_id=1, source_target_pairs={{0,1},{1,0},{2,3},{3,2},{4,5},{5,4},{6,7},{7,6},{8,9},{9,8},{10,11... | collective-permute-start | bytes 2359304 | tf_op jit(solution)/shard_map/ppermute | solution.py:258
  4.8 8.3 %collective-permute-start = (bf16[48,2048]{1,0:T(8,128)(2,1)}, bf16[48,2048]{1,0:T(8,128)(2,1)S(1)}, u32[]{:S(2)}, u32[]{:S(2)}) collective-permute-start(bf16[48,2048]{1,0:T(8,128)(2,1)} %get-tuple-element.22), channel_id=1, source_target_pairs={{0,8},{1,9},{2,10},{3,11},{4,12},{5,13},{6,14},{7,15},{8,16},{9,17... | collective-permute-start | bytes 589832 | tf_op jit(solution)/shard_map/ppermute | solution.py:28
  6.3 11.5 %collective-permute-start.1 = (bf16[48,2048]{1,0:T(8,128)(2,1)}, bf16[48,2048]{1,0:T(8,128)(2,1)S(1)}, u32[]{:S(2)}, u32[]{:S(2)}) collective-permute-start(bf16[48,2048]{1,0:T(8,128)(2,1)} %get-tuple-element.23), channel_id=1, source_target_pairs={{0,16},{1,17},{2,18},{3,19},{4,20},{5,21},{6,22},{7,23},{8,24},{9,... | collective-permute-start | bytes 589832 | tf_op jit(solution)/shard_map/ppermute | solution.py:28
  9.1 8.8 %collective-permute-start.2 = (bf16[48,2048]{1,0:T(8,128)(2,1)}, bf16[48,2048]{1,0:T(8,128)(2,1)S(1)}, u32[]{:S(2)}, u32[]{:S(2)}) collective-permute-start(bf16[48,2048]{1,0:T(8,128)(2,1)} %get-tuple-element.24), channel_id=1, source_target_pairs={{0,24},{1,25},{2,26},{3,27},{4,28},{5,29},{6,30},{7,31},{8,0},{9,1... | collective-permute-start | bytes 589832 | tf_op jit(solution)/shard_map/ppermute | solution.py:28
  13.1 4.7 %copy-start.12 = (bf16[48,2048]{1,0:T(8,128)(2,1)}, bf16[48,2048]{1,0:T(8,128)(2,1)S(1)}, u32[]{:S(2)}) copy-start(bf16[48,2048]{1,0:T(8,128)(2,1)S(1)} %collective-permute-done.rest_1_) | copy-start | bytes 589828
  17.8 0.7 copy-start.13
  17.8 0.7 copy-start.14
  20.8 17.7 %collective-permute-start.3 = (bf16[4,48,512]{2,1,0:T(8,128)(2,1)}, bf16[4,48,512]{2,1,0:T(8,128)(2,1)S(1)}, u32[]{:S(2)}, u32[]{:S(2)}) collective-permute-start(bf16[4,48,512]{2,1,0:T(8,128)(2,1)} %get-tuple-element.26), channel_id=1, source_target_pairs={{0,7},{1,2},{2,1},{3,4},{4,3},{5,6},{6,5},{7,0},{8,15},{9,10},{10,... | collective-permute-start | bytes 589832 | tf_op jit(solution)/shard_map/ppermute | solution.py:28
  25.7 12.8 %collective-permute-start.4 = (bf16[4,48,512]{2,1,0:T(8,128)(2,1)}, bf16[4,48,512]{2,1,0:T(8,128)(2,1)S(1)}, u32[]{:S(2)}, u32[]{:S(2)}) collective-permute-start(bf16[4,48,512]{2,1,0:T(8,128)(2,1)} %get-tuple-element.27), channel_id=1, source_target_pairs={{0,2},{1,7},{2,4},{3,1},{4,6},{5,3},{6,0},{7,5},{8,10},{9,15},{10,... | collective-permute-start | bytes 589832 | tf_op jit(solution)/shard_map/ppermute | solution.py:28
  25.7 16.0 %collective-permute-start.5 = (bf16[4,48,512]{2,1,0:T(8,128)(2,1)}, bf16[4,48,512]{2,1,0:T(8,128)(2,1)S(1)}, u32[]{:S(2)}, u32[]{:S(2)}) collective-permute-start(bf16[4,48,512]{2,1,0:T(8,128)(2,1)} %get-tuple-element.28), channel_id=1, source_target_pairs={{0,5},{1,4},{2,7},{3,6},{4,1},{5,0},{6,3},{7,2},{8,13},{9,12},{10,... | collective-permute-start | bytes 589832 | tf_op jit(solution)/shard_map/ppermute | solution.py:28
  30.3 14.0 %collective-permute-start.6 = (bf16[4,48,512]{2,1,0:T(8,128)(2,1)}, bf16[4,48,512]{2,1,0:T(8,128)(2,1)S(1)}, u32[]{:S(2)}, u32[]{:S(2)}) collective-permute-start(bf16[4,48,512]{2,1,0:T(8,128)(2,1)} %get-tuple-element.25.refs_0_), channel_id=1, source_target_pairs={{0,1},{1,0},{2,3},{3,2},{4,5},{5,4},{6,7},{7,6},{8,9},{9,8},{10,11... | collective-permute-start | bytes 589832 | tf_op jit(solution)/shard_map/ppermute | solution.py:271
  38.5 7.8 %collective-permute-start.7 = (bf16[4,48,512]{2,1,0:T(8,128)(2,1)S(1)}, bf16[4,48,512]{2,1,0:T(8,128)(2,1)S(1)}, u32[]{:S(2)}, u32[]{:S(2)}) collective-permute-start(bf16[4,48,512]{2,1,0:T(8,128)(2,1)S(1)} %collective-permute-done.3.refs_1_), channel_id=1, source_target_pairs={{0,1},{1,0},{2,3},{3,2},{4,5},{5,4},{6,7},{7,6},{8,9},{9,8},{10,11... | collective-permute-start | bytes 589832 | tf_op jit(solution)/shard_map/ppermute | solution.py:271
  38.5 11.5 %collective-permute-start.8 = (bf16[4,48,512]{2,1,0:T(8,128)(2,1)S(1)}, bf16[4,48,512]{2,1,0:T(8,128)(2,1)S(1)}, u32[]{:S(2)}, u32[]{:S(2)}) collective-permute-start(bf16[4,48,512]{2,1,0:T(8,128)(2,1)S(1)} %collective-permute-done.4.refs_2_), channel_id=1, source_target_pairs={{0,1},{1,0},{2,3},{3,2},{4,5},{5,4},{6,7},{7,6},{8,9},{9,8},{10,11... | collective-permute-start | bytes 589832 | tf_op jit(solution)/shard_map/ppermute | solution.py:271
  41.7 10.4 %collective-permute-start.9 = (bf16[4,48,512]{2,1,0:T(8,128)(2,1)S(1)}, bf16[4,48,512]{2,1,0:T(8,128)(2,1)S(1)}, u32[]{:S(2)}, u32[]{:S(2)}) collective-permute-start(bf16[4,48,512]{2,1,0:T(8,128)(2,1)S(1)} %collective-permute-done.5.refs_3_), channel_id=1, source_target_pairs={{0,1},{1,0},{2,3},{3,2},{4,5},{5,4},{6,7},{7,6},{8,9},{9,8},{10,11... | collective-permute-start | bytes 589832 | tf_op jit(solution)/shard_map/ppermute | solution.py:271
  52.1 0.9 copy-start.11
  56.8 33.8 %all-to-all-start = ((bf16[32,104,128]{2,1,0:T(8,128)(2,1)}), bf16[32,104,128]{2,1,0:T(8,128)(2,1)S(1)}, u32[]{:S(2)}, u32[]{:S(2)}) async-start(bf16[32,104,128]{2,1,0:T(8,128)(2,1)} %get-tuple-element.29), calls=%async_computation | async-start | bytes 1703936 | tf_op jit(solution)/shard_map/all_to_all | solution.py:287
  69.1 1.2 %copy-start = (f32[3,256,512]{2,1,0:T(8,128)}, f32[3,256,512]{2,1,0:T(8,128)S(1)}, u32[]{:S(2)}) copy-start(f32[3,256,512]{2,1,0:T(8,128)S(1)} %get-tuple-element.34.left_gram) | copy-start | bytes 4718596
  70.3 1.1 %copy-start.2 = (f32[3,256,512]{2,1,0:T(8,128)}, f32[3,256,512]{2,1,0:T(8,128)S(1)}, u32[]{:S(2)}) copy-start(f32[3,256,512]{2,1,0:T(8,128)S(1)} %get-tuple-element.35.right_gram) | copy-start | bytes 4718596
  71.4 1.1 %copy-start.4 = (f32[3,256,512]{2,1,0:T(8,128)}, f32[3,256,512]{2,1,0:T(8,128)S(1)}, u32[]{:S(2)}) copy-start(f32[3,256,512]{2,1,0:T(8,128)S(1)} %get-tuple-element.32.left_stat) | copy-start | bytes 4718596
  72.6 1.1 %copy-start.6 = (f32[3,256,512]{2,1,0:T(8,128)}, f32[3,256,512]{2,1,0:T(8,128)S(1)}, u32[]{:S(2)}) copy-start(f32[3,256,512]{2,1,0:T(8,128)S(1)} %get-tuple-element.33.right_stat) | copy-start | bytes 4718596
  73.7 1.1 %copy-start.8 = (f32[48,8192]{1,0:T(8,128)}, f32[48,8192]{1,0:T(8,128)S(1)}, u32[]{:S(2)}) copy-start(f32[48,8192]{1,0:T(8,128)S(1)} %get-tuple-element.31.momentum) | copy-start | bytes 4718596
  90.5 1.4 %copy-start.1 = (f32[3,256,512]{2,1,0:T(8,128)S(1)}, f32[3,256,512]{2,1,0:T(8,128)}, u32[]{:S(2)}) copy-start(f32[3,256,512]{2,1,0:T(8,128)} %copy-done) | copy-start | bytes 4718596
  91.9 1.4 %copy-start.3 = (f32[3,256,512]{2,1,0:T(8,128)S(1)}, f32[3,256,512]{2,1,0:T(8,128)}, u32[]{:S(2)}) copy-start(f32[3,256,512]{2,1,0:T(8,128)} %copy-done.2) | copy-start | bytes 4718596
  93.4 1.4 %copy-start.5 = (f32[3,256,512]{2,1,0:T(8,128)S(1)}, f32[3,256,512]{2,1,0:T(8,128)}, u32[]{:S(2)}) copy-start(f32[3,256,512]{2,1,0:T(8,128)} %copy-done.4) | copy-start | bytes 4718596
  94.8 1.4 %copy-start.7 = (f32[3,256,512]{2,1,0:T(8,128)S(1)}, f32[3,256,512]{2,1,0:T(8,128)}, u32[]{:S(2)}) copy-start(f32[3,256,512]{2,1,0:T(8,128)} %copy-done.6) | copy-start | bytes 4718596
  96.2 1.4 %copy-start.9 = (f32[48,8192]{1,0:T(8,128)S(1)}, f32[48,8192]{1,0:T(8,128)}, u32[]{:S(2)}) copy-start(f32[48,8192]{1,0:T(8,128)} %copy-done.8) | copy-start | bytes 4718596

commit v2 on v1

--- a/solution.py
+++ b/solution.py
@@ -13,10 +13,11 @@
 epsilon = 1e-06
 lanes = 128
 extra_rows = 8
+row_parts = 3
 ring_x = 4
 ring_z = 8
 pairs = ring_z // 2
-origins = (0, -1, -2, -3, 1, 2, 3, 4)
+origins = (-3, -2, -1, 0, 4, 3, 2, 1)
 
 
 def shifted(block, step_x, step_z):
@@ -40,52 +41,73 @@
     return pl.multiple_of(index * multiple, multiple)
 
 
-def cut_kernel(place, grad, *rest):
-    *slabs, sem = rest
-    x = place[0] // ring_z
-    width = slabs[0].shape[1]
+def role_steps(parity):
+    return 2, 1 - 2 * parity, 2 * parity - 1, 0
+
+
+def cut_kernel(place, grad, slabs, *rest):
+    nears, sem = rest[:-1], rest[-1]
+    x, z = place[0] // ring_z, place[0] % ring_z
+    pair, parity = z // 2, z % 2
+    _, rows_dev, width = slabs.shape
+    block_size = nears[0].shape[1]
+    wanted = [(slabs.at[i], pl.ds(i * width, width)) for i in range(ring_x)]
+    for near, step in zip(nears, role_steps(parity)):
+        at = x * pairs + (pair + pairs + step) % pairs
+        wanted.append((near, pl.ds(aligned(at, block_size), block_size)))
     copies = []
-    for i, slab in enumerate(slabs):
-        at = pl.ds(aligned((x + 1 + i) % ring_x, width), width)
-        copies.append(pltpu.make_async_copy(grad.at[:, at], slab, sem.at[i]))
-        copies[-1].start()
+    for out, at in wanted:
+        for part in range(row_parts):
+            rows = pl.ds(part * rows_dev // row_parts, rows_dev // row_parts)
+            copies.append(
+                pltpu.make_async_copy(grad.at[rows, at], out.at[rows], sem.at[len(copies)])
+            )
+            copies[-1].start()
     for copy in copies:
         copy.wait()
 
 
-def pick_kernel(place, *rest):
-    slabs, outs = rest[:ring_x], rest[ring_x:]
-    z = place[0] % ring_z
+def pick_kernel(place, slabs, *rest):
+    outs, sem = rest[:-1], rest[-1]
+    x, z = place[0] // ring_z, place[0] % ring_z
     pair, parity = z // 2, z % 2
     width = outs[0].shape[2]
-    for out, step in zip(outs, (2, 1 - 2 * parity, 2 * parity - 1, 0)):
-        column = (pair + pairs + step) % pairs
-        for d in range(ring_x):
-            out[d] = slabs[d][:, pl.ds(aligned(column, width), width)]
+    copies = []
+    for out, step in zip(outs, role_steps(parity)):
+        at = pl.ds(aligned((pair + pairs + step) % pairs, width), width)
+        for d in range(1, ring_x):
+            block = slabs.at[(x + ring_x - d) % ring_x, :, at]
+            copies.append(pltpu.make_async_copy(block, out.at[d - 1], sem.at[len(copies)]))
+            copies[-1].start()
+    for copy in copies:
+        copy.wait()
 
 
 def apply_kernel(place, *refs):
-    groups, (own_root, partner_root, right_root) = refs[:8], refs[8:11]
-    blocks, payload, root_v, right_v, sem = refs[11:]
-    bring = pltpu.make_async_copy(right_root, right_v, sem)
-    bring.start()
+    nears, swapped, fars = refs[:4], refs[4], refs[5:13]
+    own_root, partner_root, right_root, blocks, payload, root_v, right_v, sem = refs[13:]
     me = place[0]
     x, z = me // ring_z, me % ring_z
     parity = z % 2
     sign = 1 - 2 * parity
-    rows_dev = groups[0].shape[1]
+    rows_dev = nears[0].shape[0]
     row_blocks, half, block_size = own_root.shape
     owners, length, _ = payload.shape
     body = length - extra_rows
 
-    for group, origin in zip(groups, origins):
+    bring = [pltpu.make_async_copy(right_root, right_v, sem.at[2])]
+    for i, (root, side) in enumerate(((own_root, parity), (partner_root, 1 - parity))):
+        rows = pl.ds(aligned(side, half), half)
+        bring.append(pltpu.make_async_copy(root, root_v.at[:, rows], sem.at[i]))
+    for copy in bring[::-1]:
+        copy.start()
+    for i, origin in enumerate(origins):
         for d in range(ring_x):
             source = (x + ring_x - d) % ring_x * ring_z + (z + ring_z + sign * origin) % ring_z
-            blocks[pl.ds(aligned(source, rows_dev), rows_dev), :] = group[d]
-    for root, side in ((own_root, parity), (partner_root, 1 - parity)):
-        for r in range(row_blocks):
-            root_v[r, pl.ds(aligned(side, half), half), :] = root[r]
-    bring.wait()
+            group = fars[i][d - 1] if d else nears[i][...] if i < 4 else swapped[i - 4]
+            blocks[pl.ds(aligned(source, rows_dev), rows_dev), :] = group
+    for copy in bring:
+        copy.wait()
 
     lane = lax.broadcasted_iota(jnp.int32, (8, lanes), 1)
     total = jnp.zeros((8, lanes), jnp.float32)
@@ -118,16 +140,7 @@
         payload[f, body : body + extra_rows, :] = parts
 
 
-def gram_kernel(
-    place, blocks, left_stat, right_stat, momentum,
-    left_gram, right_gram, left_near, right_near, momentum_near, sem,
-):
-    bring = []
-    for i, (far, near) in enumerate(
-        ((left_stat, left_near), (right_stat, right_near), (momentum, momentum_near))
-    ):
-        bring.append(pltpu.make_async_copy(far, near, sem.at[i]))
-        bring[-1].start()
+def gram_kernel(place, blocks, left_gram, right_gram):
     row_blocks, half, block_size = left_gram.shape
     parity = place[0] % 2
     for r in range(row_blocks):
@@ -146,14 +159,13 @@
                     block[:, side * half : (side + 1) * half], block,
                     (((0,), (0,)), ((), ())), preferred_element_type=jnp.float32,
                 )
-    for copy in bring:
-        copy.wait()
 
 
 def finish_kernel(
     clip_limit, block_size, place,
     back, momentum, left_stat, right_stat, left_gram, right_gram,
-    new_momentum, new_left, new_right, momentum_v, stat_v, out_sem, stat_out_sem,
+    new_momentum, new_left, new_right,
+    back_v, momentum_v, stat_v, gram_v, back_sem, in_sem, stat_sem, gram_sem, out_sem, stat_out_sem,
 ):
     me = place[0]
     rows_dev, all_cols = momentum.shape
@@ -165,7 +177,35 @@
     columns = all_cols // owners
     body = length - extra_rows
 
-    parts = back[:, body : body + extra_rows, :].astype(jnp.float32)
+    get_back, get_momentum, put_momentum = [], [], []
+    get_stat, get_gram, put_stat = [], [], []
+    for q in range(pieces):
+        some = pl.ds(q * share, share)
+        get_back.append(pltpu.make_async_copy(back.at[some], back_v.at[some], back_sem.at[q]))
+        get_back[-1].start()
+    for side, (stat, gram, out) in enumerate(
+        ((left_stat, left_gram, new_left), (right_stat, right_gram, new_right))
+    ):
+        for r in range(row_blocks):
+            i = side * row_blocks + r
+            get_stat.append(pltpu.make_async_copy(stat.at[r], stat_v.at[i], stat_sem.at[i]))
+            get_gram.append(pltpu.make_async_copy(gram.at[r], gram_v.at[i], gram_sem.at[i]))
+            put_stat.append(pltpu.make_async_copy(stat_v.at[i], out.at[r], stat_out_sem.at[i]))
+            get_stat[-1].start()
+            get_gram[-1].start()
+    for q in range(pieces):
+        part = pl.ds(q * width, width)
+        get_momentum.append(
+            pltpu.make_async_copy(momentum.at[:, part], momentum_v.at[:, part], in_sem.at[q])
+        )
+        put_momentum.append(
+            pltpu.make_async_copy(momentum_v.at[:, part], new_momentum.at[:, part], out_sem.at[q])
+        )
+        get_momentum[-1].start()
+
+    for copy in get_back:
+        copy.wait()
+    parts = back_v[:, body : body + extra_rows, :].astype(jnp.float32)
     values = parts[:, 0, :] + parts[:, 1, :] + parts[:, 2, :]
     lane = lax.broadcasted_iota(jnp.int32, values.shape, 1)
     source = lax.broadcasted_iota(jnp.int32, values.shape, 0)
@@ -176,15 +216,11 @@
     total_sq = scalar_sum(jnp.where(even & (lane < row_blocks), gnorm, 0.0))
     clip_factor = jnp.minimum(1.0, clip_limit / (jnp.sqrt(total_sq) + epsilon))
     coeff = (1.0 - decay_stat) * clip_factor * clip_factor
-    puts = []
-    for side, (stat, gram, out) in enumerate(
-        ((left_stat, left_gram, new_left), (right_stat, right_gram, new_right))
-    ):
-        for r in range(row_blocks):
-            i = side * row_blocks + r
-            stat_v[i] = decay_stat * stat[r] + coeff * gram[r]
-            puts.append(pltpu.make_async_copy(stat_v.at[i], out.at[r], stat_out_sem.at[i]))
-            puts[-1].start()
+    for i in range(2 * row_blocks):
+        get_stat[i].wait()
+        get_gram[i].wait()
+        stat_v[i] = decay_stat * stat_v[i] + coeff * gram_v[i]
+        put_stat[i].start()
 
     scale = clip_factor * jnp.sqrt(gnorm) / (jnp.sqrt(pnorm) + epsilon)
     first = me * rows_dev // block_size
@@ -195,18 +231,15 @@
     )
     in_upper = lax.broadcasted_iota(jnp.int32, (rows_dev, lanes), 0) < until
     for q in range(pieces):
+        get_momentum[q].wait()
         for s in range(q * share, (q + 1) * share):
             row_scale = jnp.where(in_upper, upper[s : s + 1], lower[s : s + 1])
             for c in range(columns // lanes):
                 at = pl.ds(s * columns + c * lanes, lanes)
-                moved = back[s, c * rows_dev : (c + 1) * rows_dev, :].astype(jnp.float32)
-                momentum_v[:, at] = momentum_rate * momentum[:, at] + row_scale * moved
-        part = pl.ds(q * width, width)
-        puts.append(
-            pltpu.make_async_copy(momentum_v.at[:, part], new_momentum.at[:, part], out_sem.at[q])
-        )
-        puts[-1].start()
-    for copy in puts:
+                moved = back_v[s, c * rows_dev : (c + 1) * rows_dev, :].astype(jnp.float32)
+                momentum_v[:, at] = momentum_rate * momentum_v[:, at] + row_scale * moved
+        put_momentum[q].start()
+    for copy in put_stat + put_momentum:
         copy.wait()
 
 
@@ -242,80 +275,88 @@
     left_stat = left_stat.reshape(row_blocks, half, block_size)
     right_stat = right_stat.reshape(row_blocks, half, block_size)
 
-    *slabs, own_slab = pl.pallas_call(
+    slabs, *nears = pl.pallas_call(
         cut_kernel,
-        out_shape=[array(rows_dev, slab_width)] * ring_x,
+        out_shape=[array(ring_x, rows_dev, slab_width)] + [array(rows_dev, block_size)] * 4,
         in_specs=[smem, in_hbm],
-        out_specs=[in_vmem] * ring_x,
-        scratch_shapes=[dma((ring_x,))],
+        out_specs=[in_vmem] * 5,
+        scratch_shapes=[dma(((ring_x + 4) * row_parts,))],
         cost_estimate=cost(0, 1),
         name="cut",
     )(place, keep_in_hbm(grad))
-    slabs = [shifted(slab, d + 1, lambda z: 0) for d, slab in enumerate(slabs)]
+    slabs = lax.all_to_all(
+        slabs, "fsdp", split_axis=0, concat_axis=0, tiled=True,
+        axis_index_groups=[[i * ring_z + z for i in range(ring_x)] for z in range(ring_z)],
+    )
+    steps = (3, -2, 1)
+    nears = [toward(near, step) for near, step in zip(nears, steps)] + nears[3:]
     swap = functools.partial(
         lax.ppermute, axis_name="fsdp", perm=[(i, i ^ 1) for i in range(owners)]
     )
     left_partner = swap(left_root)
-    far, same, cross, own = pl.pallas_call(
+    fars = pl.pallas_call(
         pick_kernel,
-        out_shape=[array(ring_x, rows_dev, block_size)] * 4,
-        in_specs=[smem] + [in_vmem] * ring_x,
+        out_shape=[array(ring_x - 1, rows_dev, block_size)] * 4,
+        in_specs=[smem, in_hbm],
         out_specs=[in_vmem] * 4,
+        scratch_shapes=[dma((4 * (ring_x - 1),))],
         cost_estimate=cost(0, 2),
         name="pick",
-    )(place, own_slab, *slabs)
-    far = toward(far, 3)
-    same = toward(same, -2)
-    cross = toward(cross, 1)
-    groups = [own, cross, same, far]
-    groups += [swap(group) for group in groups]
+    )(place, slabs)
+    fars = [toward(far, step) for far, step in zip(fars, steps)] + [fars[3]]
+    swapped = swap(jnp.stack(nears))
+    fars += [swap(far) for far in fars]
 
     blocks, payload = pl.pallas_call(
         apply_kernel,
         out_shape=[array(all_rows, block_size), array(owners, length, lanes)],
-        in_specs=[smem] + [in_vmem] * 10 + [in_hbm],
+        in_specs=[smem] + [in_vmem] * 13 + [in_hbm] * 3,
         out_specs=[in_vmem] * 2,
         scratch_shapes=[
             pltpu.VMEM((row_blocks, block_size, block_size), jnp.bfloat16),
             pltpu.VMEM((row_blocks, block_size, half), jnp.bfloat16),
-            dma,
+            dma((3,)),
         ],
         compiler_params=some_vmem,
         cost_estimate=cost(3 * flops, 6),
         name="apply",
-    )(place, *groups, left_root, left_partner, keep_in_hbm(right_root))
+    )(place, *nears, swapped, *fars, keep_in_hbm(left_root), left_partner, keep_in_hbm(right_root))
     back = lax.all_to_all(payload, "fsdp", split_axis=0, concat_axis=0, tiled=True)
 
     stat = array(row_blocks, half, block_size, dtype=jnp.float32)
     wide = array(rows_dev, all_cols, dtype=jnp.float32)
     grams = pl.pallas_call(
         gram_kernel,
-        out_shape=[stat] * 4 + [wide],
-        in_specs=[smem, in_vmem] + [in_hbm] * 3,
-        out_specs=[in_vmem] * 5,
-        scratch_shapes=[dma((3,))],
+        out_shape=[stat] * 2,
+        in_specs=[smem, in_vmem],
+        out_specs=[in_vmem] * 2,
         compiler_params=some_vmem,
-        cost_estimate=cost(2 * flops, 8),
+        cost_estimate=cost(2 * flops, 5),
         name="grams",
-    )(place, blocks, *map(keep_in_hbm, (left_stat, right_stat, momentum)))
-    left_gram, right_gram, left_near, right_near, momentum_near = grams
+    )(place, blocks)
 
     quarters = 4
     new_momentum, new_left, new_right = pl.pallas_call(
         functools.partial(finish_kernel, clip_limit, block_size),
         out_shape=[wide, stat, stat],
-        in_specs=[smem] + [in_vmem] * 6,
+        in_specs=[smem] + [in_hbm] * 6,
         out_specs=[in_hbm] * 3,
         scratch_shapes=[
+            pltpu.VMEM((owners, length, lanes), jnp.bfloat16),
             pltpu.VMEM((rows_dev, all_cols), jnp.float32),
             pltpu.VMEM((2 * row_blocks, half, block_size), jnp.float32),
+            pltpu.VMEM((2 * row_blocks, half, block_size), jnp.float32),
+            dma((quarters,)),
+            dma((quarters,)),
+            dma((2 * row_blocks,)),
+            dma((2 * row_blocks,)),
             dma((quarters,)),
             dma((2 * row_blocks,)),
         ],
         compiler_params=some_vmem,
-        cost_estimate=cost(1 << 22, 10),
+        cost_estimate=cost(1 << 22, 14),
         name="finish",
-    )(place, back, momentum_near, left_near, right_near, left_gram, right_gram)
+    )(place, back, *map(keep_in_hbm, (momentum, left_stat, right_stat, *grams)))
     shape = (row_blocks, 1, half, block_size)
     return (new_momentum, new_left.reshape(shape), new_right.reshape(shape))
 

time: 101 us -> 103 us (1.020)
  waiting for transfers between devices: 40.2 us -> 51 us
  local copies, waits for them, and re-layouts: 14.5 us -> 4.13 us
  Pallas kernels: 13.1 us -> 16.3 us
  starting transfers between devices: 31.7 us -> 30.3 us
    unnamed x30 -> x18, local copies, waits for them, and re-layouts: 14.5 us -> 4.13 us
    ppermute x6, waiting for transfers between devices: 16.7 us -> 24.7 us  [shifted(): return lax.ppermute(block, 'fsdp', route)]
    all_to_all x0 -> x1, starting transfers between devices: none -> 4.44 us  [local(): lax.all_to_all(slabs, 'fsdp', split_axis=0, concat_axis=0, tiled=True, ax...]
    pallas_call x1, Pallas kernels: 2.55 us -> 6.61 us  [local(): pl.pallas_call(functools.partial(finish_kernel, clip_limit, block_size),...]
    all_to_all x1, starting transfers between devices: 9.84 us -> 5.94 us  [local(): lax.all_to_all(payload, 'fsdp', split_axis=0, concat_axis=0, tiled=True)]
    all_to_all x1, waiting for transfers between devices: 15.7 us -> 18.9 us  [local(): lax.all_to_all(payload, 'fsdp', split_axis=0, concat_axis=0, tiled=True)]
    ppermute x6, starting transfers between devices: 15.3 us -> 13 us  [shifted(): return lax.ppermute(block, 'fsdp', route)]
    pallas_call x3, Pallas kernels: 6.81 us -> 5.54 us  [the longest x1 2.39 us: local(): pl.pallas_call(cut_kernel, out_shape=[array(ring_x, rows_dev, slab_width)...]
  transfers between devices with their start and end apart: 12 -> 14, of which waited for: 8 -> 8; matrix products, arithmetic and copies ran while one was open for 0% -> 0% of each run, Pallas kernels for 7% -> 3%
where the time goes in v2:
time: 103 us
  waiting for transfers between devices  51 us (50%)
  starting transfers between devices  30.3 us (29%)
  Pallas kernels  16.3 us (16%)
  local copies, waits for them, and re-layouts  4.13 us (4%)
    ppermute x6, waiting for transfers between devices, shifted(): return lax.ppermute(block, 'fsdp', route)  24.7 us
    all_to_all x1, waiting for transfers between devices, local(): lax.all_to_all(payload, 'fsdp', split_axis=0, concat_axis=0, tiled=True)  18.9 us
    ppermute x6, starting transfers between devices, shifted(): return lax.ppermute(block, 'fsdp', route)  13 us
    ppermute x4, waiting for transfers between devices, local(): fars += [swap(far) for far in fars]  7.39 us
    pallas_call x1, Pallas kernels, local(): pl.pallas_call(functools.partial(finish_kernel, clip_limit, block_size),...  6.61 us
    all_to_all x1, starting transfers between devices, local(): lax.all_to_all(payload, 'fsdp', split_axis=0, concat_axis=0, tiled=True)  5.94 us
    ppermute x4, starting transfers between devices, local(): fars += [swap(far) for far in fars]  4.95 us
    all_to_all x1, starting transfers between devices, local(): lax.all_to_all(slabs, 'fsdp', split_axis=0, concat_axis=0, tiled=True, ax...  4.44 us
  transfers between devices with their start and end apart: 14, of which 8 were waited for; matrix products, arithmetic and copies ran while one was open for 0% of the time, Pallas kernels for 3%

profile of v2, /device:TPU:8, one launch (start us, length us, event | category | flops | bytes accessed | tf_op | source)
XLA Modules:
  0.0 102.5 jit_solution(17705739474139158499)
XLA Ops:
  0.6 0.0 copy-start.5
  0.6 2.4 %cut.1 = (bf16[4,48,2048]{2,1,0:T(8,128)(2,1)}, bf16[48,512]{1,0:T(8,128)(2,1)}, bf16[48,512]{1,0:T(8,128)(2,1)}, bf16[48,512]{1,0:T(8,128)(2,1)}, bf16[48,512]{1,0:T(8,128)(2,1)}) custom-call(s32[1]{0:T(128)} %bitcast.place, bf16[48,8192]{1,0:T(8,128)(2,1)} %grad.1), custom_call_target="tpu_custom_call" | custom-call | bytes 1048576 | tf_op jit(solution)/shard_map/cut/pallas_call | solution.py:278
  3.0 0.0 copy-start.8
  3.1 0.0 copy-start.7
  3.1 0.0 copy-start.6
  3.1 0.0 copy-start.2
  3.1 4.4 %all-to-all-start = ((bf16[4,48,2048]{2,1,0:T(8,128)(2,1)}), bf16[4,48,2048]{2,1,0:T(8,128)(2,1)S(1)}, u32[]{:S(2)}, u32[]{:S(2)}) async-start(bf16[4,48,2048]{2,1,0:T(8,128)(2,1)} %get-tuple-element.23), calls=%async_computation | async-start | bytes 1572864 | tf_op jit(solution)/shard_map/all_to_all | solution.py:287
  7.5 0.0 copy-done.5
  7.5 1.9 %collective-permute-start.11 = (bf16[3,256,512]{2,1,0:T(8,128)(2,1)S(1)}, bf16[3,256,512]{2,1,0:T(8,128)(2,1)S(1)}, u32[]{:S(2)}, u32[]{:S(2)}) collective-permute-start(bf16[3,256,512]{2,1,0:T(8,128)(2,1)S(1)} %bitcast.24), channel_id=1, source_target_pairs={{0,1},{1,0},{2,3},{3,2},{4,5},{5,4},{6,7},{7,6},{8,9},{9,8},{10,11... | collective-permute-start | bytes 2359304 | tf_op jit(solution)/shard_map/ppermute | solution.py:296
  9.4 0.0 copy-done.8
  9.4 5.8 %collective-permute-start = (bf16[48,512]{1,0:T(8,128)(2,1)S(1)}, bf16[48,512]{1,0:T(8,128)(2,1)S(1)}, u32[]{:S(2)}, u32[]{:S(2)}) collective-permute-start(bf16[48,512]{1,0:T(8,128)(2,1)S(1)} %copy-done.8), channel_id=1, source_target_pairs={{0,5},{1,4},{2,7},{3,6},{4,1},{5,0},{6,3},{7,2},{8,13},{9,12},{10,... | collective-permute-start | bytes 147464 | tf_op jit(solution)/shard_map/ppermute | solution.py:29
  15.3 0.0 copy-done.7
  15.3 1.5 %collective-permute-start.1 = (bf16[48,512]{1,0:T(8,128)(2,1)S(1)}, bf16[48,512]{1,0:T(8,128)(2,1)S(1)}, u32[]{:S(2)}, u32[]{:S(2)}) collective-permute-start(bf16[48,512]{1,0:T(8,128)(2,1)S(1)} %copy-done.7), channel_id=1, source_target_pairs={{0,2},{1,7},{2,4},{3,1},{4,6},{5,3},{6,0},{7,5},{8,10},{9,15},{10,... | collective-permute-start | bytes 147464 | tf_op jit(solution)/shard_map/ppermute | solution.py:29
  16.8 0.0 copy-done.6
  16.8 0.0 collective-permute-start.2
  16.8 0.7 collective-permute-done.refs_0_
  17.5 16.5 %collective-permute-done.1.refs_1_ = bf16[48,512]{1,0:T(8,128)(2,1)S(1)} collective-permute-done((bf16[48,512]{1,0:T(8,128)(2,1)S(1)}, bf16[48,512]{1,0:T(8,128)(2,1)S(1)}, u32[]{:S(2)}, u32[]{:S(2)}) %collective-permute-start.1) | collective-permute-done | bytes 49184 | tf_op jit(solution)/shard_map/ppermute | solution.py:29
  33.9 0.0 collective-permute-done.2.refs_2_
  33.9 0.0 copy-done.2
  34.0 0.1 collective-permute-start.3
  34.1 0.0 all-to-all-done.slabs
  34.1 0.0 copy-start.4
  34.1 0.9 copy-done.4
  35.0 2.0 %pick.1 = (bf16[3,48,512]{2,1,0:T(8,128)(2,1)}, bf16[3,48,512]{2,1,0:T(8,128)(2,1)}, bf16[3,48,512]{2,1,0:T(8,128)(2,1)}, bf16[3,48,512]{2,1,0:T(8,128)(2,1)}) custom-call(s32[1]{0:T(128)} %bitcast.place, bf16[4,48,2048]{2,1,0:T(8,128)(2,1)} %copy-done.4), custom_call_target="tpu_custom_call" | custom-call | bytes 2097152 | tf_op jit(solution)/shard_map/pick/pallas_call | solution.py:297
  36.9 2.1 %collective-permute-start.4 = (bf16[3,48,512]{2,1,0:T(8,128)(2,1)}, bf16[3,48,512]{2,1,0:T(8,128)(2,1)S(1)}, u32[]{:S(2)}, u32[]{:S(2)}) collective-permute-start(bf16[3,48,512]{2,1,0:T(8,128)(2,1)} %get-tuple-element.24), channel_id=1, source_target_pairs={{0,5},{1,4},{2,7},{3,6},{4,1},{5,0},{6,3},{7,2},{8,13},{9,12},{10,... | collective-permute-start | bytes 442376 | tf_op jit(solution)/shard_map/ppermute | solution.py:29
  39.0 2.4 %collective-permute-start.5 = (bf16[3,48,512]{2,1,0:T(8,128)(2,1)}, bf16[3,48,512]{2,1,0:T(8,128)(2,1)S(1)}, u32[]{:S(2)}, u32[]{:S(2)}) collective-permute-start(bf16[3,48,512]{2,1,0:T(8,128)(2,1)} %get-tuple-element.25), channel_id=1, source_target_pairs={{0,2},{1,7},{2,4},{3,1},{4,6},{5,3},{6,0},{7,5},{8,10},{9,15},{10,... | collective-permute-start | bytes 442376 | tf_op jit(solution)/shard_map/ppermute | solution.py:29
  41.4 1.2 %collective-permute-start.6 = (bf16[3,48,512]{2,1,0:T(8,128)(2,1)}, bf16[3,48,512]{2,1,0:T(8,128)(2,1)S(1)}, u32[]{:S(2)}, u32[]{:S(2)}) collective-permute-start(bf16[3,48,512]{2,1,0:T(8,128)(2,1)} %get-tuple-element.26), channel_id=1, source_target_pairs={{0,7},{1,2},{2,1},{3,4},{4,3},{5,6},{6,5},{7,0},{8,15},{9,10},{10,... | collective-permute-start | bytes 442376 | tf_op jit(solution)/shard_map/ppermute | solution.py:29
  42.6 0.0 collective-permute-done.3.refs_4_
  42.6 2.0 %collective-permute-start.10 = (bf16[3,48,512]{2,1,0:T(8,128)(2,1)}, bf16[3,48,512]{2,1,0:T(8,128)(2,1)S(1)}, u32[]{:S(2)}, u32[]{:S(2)}) collective-permute-start(bf16[3,48,512]{2,1,0:T(8,128)(2,1)} %get-tuple-element.27.refs_8_), channel_id=1, source_target_pairs={{0,1},{1,0},{2,3},{3,2},{4,5},{5,4},{6,7},{7,6},{8,9},{9,8},{10,11... | collective-permute-start | bytes 442376 | tf_op jit(solution)/shard_map/ppermute | solution.py:308
  44.6 7.0 %collective-permute-done.4.refs_5_ = bf16[3,48,512]{2,1,0:T(8,128)(2,1)S(1)} collective-permute-done((bf16[3,48,512]{2,1,0:T(8,128)(2,1)}, bf16[3,48,512]{2,1,0:T(8,128)(2,1)S(1)}, u32[]{:S(2)}, u32[]{:S(2)}) %collective-permute-start.4) | collective-permute-done | bytes 147488 | tf_op jit(solution)/shard_map/ppermute | solution.py:29
  51.6 1.4 %collective-permute-start.7 = (bf16[3,48,512]{2,1,0:T(8,128)(2,1)S(1)}, bf16[3,48,512]{2,1,0:T(8,128)(2,1)S(1)}, u32[]{:S(2)}, u32[]{:S(2)}) collective-permute-start(bf16[3,48,512]{2,1,0:T(8,128)(2,1)S(1)} %collective-permute-done.4.refs_5_), channel_id=1, source_target_pairs={{0,1},{1,0},{2,3},{3,2},{4,5},{5,4},{6,7},{7,6},{8,9},{9,8},{10,11... | collective-permute-start | bytes 442376 | tf_op jit(solution)/shard_map/ppermute | solution.py:308
  53.0 0.0 collective-permute-done.5.refs_6_
  53.0 0.6 collective-permute-start.8
  53.6 0.5 collective-permute-done.6.refs_7_
  54.2 0.9 collective-permute-start.9
  55.1 0.0 collective-permute-done.10.refs_12_
  55.1 0.0 collective-permute-done.11.refs_14_
  55.1 3.3 %collective-permute-done.7.refs_9_ = bf16[3,48,512]{2,1,0:T(8,128)(2,1)S(1)} collective-permute-done((bf16[3,48,512]{2,1,0:T(8,128)(2,1)S(1)}, bf16[3,48,512]{2,1,0:T(8,128)(2,1)S(1)}, u32[]{:S(2)}, u32[]{:S(2)}) %collective-permute-start.7) | collective-permute-done | bytes 147488 | tf_op jit(solution)/shard_map/ppermute | solution.py:308
  58.4 2.5 %collective-permute-done.8.refs_10_ = bf16[3,48,512]{2,1,0:T(8,128)(2,1)S(1)} collective-permute-done((bf16[3,48,512]{2,1,0:T(8,128)(2,1)S(1)}, bf16[3,48,512]{2,1,0:T(8,128)(2,1)S(1)}, u32[]{:S(2)}, u32[]{:S(2)}) %collective-permute-start.8) | collective-permute-done | bytes 147488 | tf_op jit(solution)/shard_map/ppermute | solution.py:308
  60.9 1.6 %collective-permute-done.9.refs_11_ = bf16[3,48,512]{2,1,0:T(8,128)(2,1)S(1)} collective-permute-done((bf16[3,48,512]{2,1,0:T(8,128)(2,1)S(1)}, bf16[3,48,512]{2,1,0:T(8,128)(2,1)S(1)}, u32[]{:S(2)}, u32[]{:S(2)}) %collective-permute-start.9) | collective-permute-done | bytes 147488 | tf_op jit(solution)/shard_map/ppermute | solution.py:308
  62.5 0.0 copy-start.3
  62.5 0.9 copy-done.3
  63.4 4.1 %apply.1 = (bf16[1536,512]{1,0:T(8,128)(2,1)S(1)}, bf16[32,104,128]{2,1,0:T(8,128)(2,1)}) custom-call(s32[1]{0:T(128)} %bitcast.place, bf16[48,512]{1,0:T(8,128)(2,1)S(1)} %collective-permute-done.refs_0_, bf16[48,512]{1,0:T(8,128)(2,1)S(1)} %collective-permute-done.1.refs_1_, bf16[48,512]{1,0:T(8,128)(2,1)S(1)} %collective-permute-done.2.refs_2_, ...), custom_call_target="tpu_custom_call" | custom-call | flops 1207959552 | bytes 6291456 | tf_op jit(solution)/shard_map/apply/pallas_call | solution.py:310
  67.5 5.9 %all-to-all-start.1 = ((bf16[32,104,128]{2,1,0:T(8,128)(2,1)}), bf16[32,104,128]{2,1,0:T(8,128)(2,1)S(1)}, u32[]{:S(2)}, u32[]{:S(2)}) async-start(bf16[32,104,128]{2,1,0:T(8,128)(2,1)} %get-tuple-element.28), calls=%async_computation.1 | async-start | bytes 1703936 | tf_op jit(solution)/shard_map/all_to_all | solution.py:324
  73.5 1.2 %grams.1 = (f32[3,256,512]{2,1,0:T(8,128)S(1)}, f32[3,256,512]{2,1,0:T(8,128)S(1)}) custom-call(s32[1]{0:T(128)} %bitcast.place, bf16[1536,512]{1,0:T(8,128)(2,1)S(1)} %get-tuple-element.29.blocks), custom_call_target="tpu_custom_call" | custom-call | flops 805306368 | bytes 5242880 | tf_op jit(solution)/shard_map/grams/pallas_call | solution.py:328
  74.6 0.0 copy-start
  74.7 1.2 %copy-done = f32[3,256,512]{2,1,0:T(8,128)} copy-done((f32[3,256,512]{2,1,0:T(8,128)}, f32[3,256,512]{2,1,0:T(8,128)S(1)}, u32[]{:S(2)}) %copy-start) | copy-done | bytes 1572888
  75.8 0.0 copy-start.1
  75.8 1.1 %copy-done.1 = f32[3,256,512]{2,1,0:T(8,128)} copy-done((f32[3,256,512]{2,1,0:T(8,128)}, f32[3,256,512]{2,1,0:T(8,128)S(1)}, u32[]{:S(2)}) %copy-start.1) | copy-done | bytes 1572888
  77.0 18.9 %all-to-all-done.1.back = bf16[32,104,128]{2,1,0:T(8,128)(2,1)S(1)} async-done(((bf16[32,104,128]{2,1,0:T(8,128)(2,1)}), bf16[32,104,128]{2,1,0:T(8,128)(2,1)S(1)}, u32[]{:S(2)}, u32[]{:S(2)}) %all-to-all-start.1) | async-done | bytes 852000 | tf_op jit(solution)/shard_map/all_to_all | solution.py:324
  95.9 6.6 %finish.1 = (f32[48,8192]{1,0:T(8,128)}, f32[3,256,512]{2,1,0:T(8,128)}, f32[3,256,512]{2,1,0:T(8,128)}) custom-call(s32[1]{0:T(128)} %bitcast.place, bf16[32,104,128]{2,1,0:T(8,128)(2,1)S(1)} %all-to-all-done.1.back, f32[48,8192]{1,0:T(8,128)} %momentum.1, f32[3,256,512]{2,1,0:T(8,128)} %bitcast.19, f32[3,256,512]{2,1,0:T(8,128)} %bitcast.20, ...), custom_call_target="tpu_custom_call" | custom-call | flops 4194304 | bytes 14680064 | tf_op jit(solution)/shard_map/finish/pallas_call | solution.py:339
  (1 shorter events, 0.0 us)
Async XLA Ops:
  0.6 6.9 %copy-start.5 = (bf16[3,1,256,512]{3,2,1,0:T(8,128)(2,1)S(1)}, bf16[3,1,256,512]{3,2,1,0:T(8,128)(2,1)}, u32[]{:S(2)}) copy-start(bf16[3,1,256,512]{3,2,1,0:T(8,128)(2,1)} %param.10) | copy-start | bytes 2359300
  3.0 6.4 %copy-start.8 = (bf16[48,512]{1,0:T(8,128)(2,1)S(1)}, bf16[48,512]{1,0:T(8,128)(2,1)}, u32[]{:S(2)}) copy-start(bf16[48,512]{1,0:T(8,128)(2,1)} %get-tuple-element.19) | copy-start | bytes 147460
  3.1 12.2 %copy-start.7 = (bf16[48,512]{1,0:T(8,128)(2,1)S(1)}, bf16[48,512]{1,0:T(8,128)(2,1)}, u32[]{:S(2)}) copy-start(bf16[48,512]{1,0:T(8,128)(2,1)} %get-tuple-element.20) | copy-start | bytes 147460
  3.1 13.7 %copy-start.6 = (bf16[48,512]{1,0:T(8,128)(2,1)S(1)}, bf16[48,512]{1,0:T(8,128)(2,1)}, u32[]{:S(2)}) copy-start(bf16[48,512]{1,0:T(8,128)(2,1)} %get-tuple-element.21) | copy-start | bytes 147460
  3.1 30.9 %copy-start.2 = (bf16[48,512]{1,0:T(8,128)(2,1)S(1)}, bf16[48,512]{1,0:T(8,128)(2,1)}, u32[]{:S(2)}) copy-start(bf16[48,512]{1,0:T(8,128)(2,1)} %get-tuple-element.22.refs_3_) | copy-start | bytes 147460
  3.1 31.0 %all-to-all-start = ((bf16[4,48,2048]{2,1,0:T(8,128)(2,1)}), bf16[4,48,2048]{2,1,0:T(8,128)(2,1)S(1)}, u32[]{:S(2)}, u32[]{:S(2)}) async-start(bf16[4,48,2048]{2,1,0:T(8,128)(2,1)} %get-tuple-element.23), calls=%async_computation | async-start | bytes 1572864 | tf_op jit(solution)/shard_map/all_to_all | solution.py:287
  7.5 47.6 %collective-permute-start.11 = (bf16[3,256,512]{2,1,0:T(8,128)(2,1)S(1)}, bf16[3,256,512]{2,1,0:T(8,128)(2,1)S(1)}, u32[]{:S(2)}, u32[]{:S(2)}) collective-permute-start(bf16[3,256,512]{2,1,0:T(8,128)(2,1)S(1)} %bitcast.24), channel_id=1, source_target_pairs={{0,1},{1,0},{2,3},{3,2},{4,5},{5,4},{6,7},{7,6},{8,9},{9,8},{10,11... | collective-permute-start | bytes 2359304 | tf_op jit(solution)/shard_map/ppermute | solution.py:296
  9.4 8.0 %collective-permute-start = (bf16[48,512]{1,0:T(8,128)(2,1)S(1)}, bf16[48,512]{1,0:T(8,128)(2,1)S(1)}, u32[]{:S(2)}, u32[]{:S(2)}) collective-permute-start(bf16[48,512]{1,0:T(8,128)(2,1)S(1)} %copy-done.8), channel_id=1, source_target_pairs={{0,5},{1,4},{2,7},{3,6},{4,1},{5,0},{6,3},{7,2},{8,13},{9,12},{10,... | collective-permute-start | bytes 147464 | tf_op jit(solution)/shard_map/ppermute | solution.py:29
  15.3 18.6 %collective-permute-start.1 = (bf16[48,512]{1,0:T(8,128)(2,1)S(1)}, bf16[48,512]{1,0:T(8,128)(2,1)S(1)}, u32[]{:S(2)}, u32[]{:S(2)}) collective-permute-start(bf16[48,512]{1,0:T(8,128)(2,1)S(1)} %copy-done.7), channel_id=1, source_target_pairs={{0,2},{1,7},{2,4},{3,1},{4,6},{5,3},{6,0},{7,5},{8,10},{9,15},{10,... | collective-permute-start | bytes 147464 | tf_op jit(solution)/shard_map/ppermute | solution.py:29
  16.8 17.2 %collective-permute-start.2 = (bf16[48,512]{1,0:T(8,128)(2,1)S(1)}, bf16[48,512]{1,0:T(8,128)(2,1)S(1)}, u32[]{:S(2)}, u32[]{:S(2)}) collective-permute-start(bf16[48,512]{1,0:T(8,128)(2,1)S(1)} %copy-done.6), channel_id=1, source_target_pairs={{0,7},{1,2},{2,1},{3,4},{4,3},{5,6},{6,5},{7,0},{8,15},{9,10},{10,... | collective-permute-start | bytes 147464 | tf_op jit(solution)/shard_map/ppermute | solution.py:29
  34.0 8.7 %collective-permute-start.3 = (bf16[4,48,512]{2,1,0:T(8,128)(2,1)S(1)}, bf16[4,48,512]{2,1,0:T(8,128)(2,1)S(1)}, u32[]{:S(2)}, u32[]{:S(2)}) collective-permute-start(bf16[4,48,512]{2,1,0:T(8,128)(2,1)S(1)} %pad_maximum_fusion), channel_id=1, source_target_pairs={{0,1},{1,0},{2,3},{3,2},{4,5},{5,4},{6,7},{7,6},{8,9},{9,8},{10,11... | collective-permute-start | bytes 589832 | tf_op jit(solution)/shard_map/ppermute | solution.py:307
  34.1 0.9 copy-start.4
  36.9 14.7 %collective-permute-start.4 = (bf16[3,48,512]{2,1,0:T(8,128)(2,1)}, bf16[3,48,512]{2,1,0:T(8,128)(2,1)S(1)}, u32[]{:S(2)}, u32[]{:S(2)}) collective-permute-start(bf16[3,48,512]{2,1,0:T(8,128)(2,1)} %get-tuple-element.24), channel_id=1, source_target_pairs={{0,5},{1,4},{2,7},{3,6},{4,1},{5,0},{6,3},{7,2},{8,13},{9,12},{10,... | collective-permute-start | bytes 442376 | tf_op jit(solution)/shard_map/ppermute | solution.py:29
  39.0 14.0 %collective-permute-start.5 = (bf16[3,48,512]{2,1,0:T(8,128)(2,1)}, bf16[3,48,512]{2,1,0:T(8,128)(2,1)S(1)}, u32[]{:S(2)}, u32[]{:S(2)}) collective-permute-start(bf16[3,48,512]{2,1,0:T(8,128)(2,1)} %get-tuple-element.25), channel_id=1, source_target_pairs={{0,2},{1,7},{2,4},{3,1},{4,6},{5,3},{6,0},{7,5},{8,10},{9,15},{10,... | collective-permute-start | bytes 442376 | tf_op jit(solution)/shard_map/ppermute | solution.py:29
  41.4 12.8 %collective-permute-start.6 = (bf16[3,48,512]{2,1,0:T(8,128)(2,1)}, bf16[3,48,512]{2,1,0:T(8,128)(2,1)S(1)}, u32[]{:S(2)}, u32[]{:S(2)}) collective-permute-start(bf16[3,48,512]{2,1,0:T(8,128)(2,1)} %get-tuple-element.26), channel_id=1, source_target_pairs={{0,7},{1,2},{2,1},{3,4},{4,3},{5,6},{6,5},{7,0},{8,15},{9,10},{10,... | collective-permute-start | bytes 442376 | tf_op jit(solution)/shard_map/ppermute | solution.py:29
  42.6 12.4 %collective-permute-start.10 = (bf16[3,48,512]{2,1,0:T(8,128)(2,1)}, bf16[3,48,512]{2,1,0:T(8,128)(2,1)S(1)}, u32[]{:S(2)}, u32[]{:S(2)}) collective-permute-start(bf16[3,48,512]{2,1,0:T(8,128)(2,1)} %get-tuple-element.27.refs_8_), channel_id=1, source_target_pairs={{0,1},{1,0},{2,3},{3,2},{4,5},{5,4},{6,7},{7,6},{8,9},{9,8},{10,11... | collective-permute-start | bytes 442376 | tf_op jit(solution)/shard_map/ppermute | solution.py:308
  51.6 6.8 %collective-permute-start.7 = (bf16[3,48,512]{2,1,0:T(8,128)(2,1)S(1)}, bf16[3,48,512]{2,1,0:T(8,128)(2,1)S(1)}, u32[]{:S(2)}, u32[]{:S(2)}) collective-permute-start(bf16[3,48,512]{2,1,0:T(8,128)(2,1)S(1)} %collective-permute-done.4.refs_5_), channel_id=1, source_target_pairs={{0,1},{1,0},{2,3},{3,2},{4,5},{5,4},{6,7},{7,6},{8,9},{9,8},{10,11... | collective-permute-start | bytes 442376 | tf_op jit(solution)/shard_map/ppermute | solution.py:308
  53.0 7.8 %collective-permute-start.8 = (bf16[3,48,512]{2,1,0:T(8,128)(2,1)S(1)}, bf16[3,48,512]{2,1,0:T(8,128)(2,1)S(1)}, u32[]{:S(2)}, u32[]{:S(2)}) collective-permute-start(bf16[3,48,512]{2,1,0:T(8,128)(2,1)S(1)} %collective-permute-done.5.refs_6_), channel_id=1, source_target_pairs={{0,1},{1,0},{2,3},{3,2},{4,5},{5,4},{6,7},{7,6},{8,9},{9,8},{10,11... | collective-permute-start | bytes 442376 | tf_op jit(solution)/shard_map/ppermute | solution.py:308
  54.2 8.3 %collective-permute-start.9 = (bf16[3,48,512]{2,1,0:T(8,128)(2,1)S(1)}, bf16[3,48,512]{2,1,0:T(8,128)(2,1)S(1)}, u32[]{:S(2)}, u32[]{:S(2)}) collective-permute-start(bf16[3,48,512]{2,1,0:T(8,128)(2,1)S(1)} %collective-permute-done.6.refs_7_), channel_id=1, source_target_pairs={{0,1},{1,0},{2,3},{3,2},{4,5},{5,4},{6,7},{7,6},{8,9},{9,8},{10,11... | collective-permute-start | bytes 442376 | tf_op jit(solution)/shard_map/ppermute | solution.py:308
  62.5 0.9 copy-start.3
  67.5 28.4 %all-to-all-start.1 = ((bf16[32,104,128]{2,1,0:T(8,128)(2,1)}), bf16[32,104,128]{2,1,0:T(8,128)(2,1)S(1)}, u32[]{:S(2)}, u32[]{:S(2)}) async-start(bf16[32,104,128]{2,1,0:T(8,128)(2,1)} %get-tuple-element.28), calls=%async_computation.1 | async-start | bytes 1703936 | tf_op jit(solution)/shard_map/all_to_all | solution.py:324
  74.6 1.2 %copy-start = (f32[3,256,512]{2,1,0:T(8,128)}, f32[3,256,512]{2,1,0:T(8,128)S(1)}, u32[]{:S(2)}) copy-start(f32[3,256,512]{2,1,0:T(8,128)S(1)} %get-tuple-element.30.left_gram) | copy-start | bytes 4718596
  75.8 1.1 %copy-start.1 = (f32[3,256,512]{2,1,0:T(8,128)}, f32[3,256,512]{2,1,0:T(8,128)S(1)}, u32[]{:S(2)}) copy-start(f32[3,256,512]{2,1,0:T(8,128)S(1)} %get-tuple-element.31.right_gram) | copy-start | bytes 4718596

commit v3 on v2

v3 whole, which is shorter than its diff:
```python
import functools
import math

import jax
import jax.numpy as jnp
from jax import lax
from jax.experimental import pallas as pl
from jax.experimental.pallas import tpu as pltpu
from jax.sharding import PartitionSpec as P

decay_stat = 0.95
momentum_rate = 0.9
epsilon = 1e-06
lanes = 128
extra_rows = 8
ring_x = 4
ring_z = 8
pairs = ring_z // 2
roles = 4
origins = (-3, -2, -1, 0, 4, 3, 2, 1)


def shifted(block, step_x, step_z):
    route = []
    for x in range(ring_x):
        for z in range(ring_z):
            there = (x + step_x) % ring_x * ring_z + (z + step_z(z)) % ring_z
            route.append((x * ring_z + z, there))
    return lax.ppermute(block, "fsdp", route)


def outward(steps):
    return lambda z: steps if z % 2 else -steps


def scalar_sum(value):
    return jnp.sum(jnp.sum(value, axis=0, keepdims=True), axis=1, keepdims=True)


def aligned(index, multiple):
    return pl.multiple_of(index * multiple, multiple)


def in_parts(value):
    value = jnp.broadcast_to(value, (extra_rows, value.shape[1]))
    high = value.astype(jnp.bfloat16).astype(jnp.float32)
    middle = (value - high).astype(jnp.bfloat16).astype(jnp.float32)
    low = value - high - middle
    row = lax.broadcasted_iota(jnp.int32, value.shape, 0)
    parts = jnp.where(row == 0, high, jnp.where(row == 1, middle, jnp.where(row == 2, low, 0.0)))
    return parts.astype(jnp.bfloat16)


def from_parts(rows):
    wide = rows.astype(jnp.float32)
    return jnp.sum(wide, axis=0, keepdims=True)


def cut_kernel(place, grad, *rest):
    outs, sem = rest[:-1], rest[-1]
    pair, parity = place[0] % ring_z // 2, place[0] % 2
    rows_dev = grad.shape[0]
    width = outs[0].shape[1]
    body = ring_x * rows_dev
    copies = []
    for out, step in zip(outs, (2, 1 - 2 * parity, 2 * parity - 1, 0)):
        column = (pair + pairs + step) % pairs
        for x in range(ring_x):
            at = pl.ds(aligned(x * pairs + column, width), width)
            rows = pl.ds(x * rows_dev, rows_dev)
            copies.append(pltpu.make_async_copy(grad.at[:, at], out.at[rows], sem.at[len(copies)]))
            copies[-1].start()
    square = jnp.zeros((8, width), jnp.float32)
    for i, copy in enumerate(copies):
        copy.wait()
        first = i % ring_x * rows_dev
        for row in range(first, first + rows_dev, 16):
            wide = outs[i // ring_x][row : row + 16, :].astype(jnp.float32)
            square += wide[:8] * wide[:8] + wide[8:] * wide[8:]
    parts = in_parts(jnp.broadcast_to(scalar_sum(square), (1, width)))
    for out in outs:
        out[body : body + extra_rows, :] = parts


def hold_kernel(root, earlier, out, sem):
    last = out.shape[0]
    copy = pltpu.make_async_copy(root.at[pl.ds(root.shape[0] - last, last)], out, sem)
    copy.start()
    copy.wait()


def pick_kernel(place, *refs):
    groups, outs = refs[:roles], refs[roles:]
    x = place[0] // ring_z
    body = groups[0].shape[0] - extra_rows
    rows_dev = body // ring_x
    total = sum(from_parts(group[body : body + extra_rows, :]) for group in groups)
    parts = in_parts(total)
    for d, out in enumerate(outs):
        rows = pl.ds(aligned((x + d) % ring_x, rows_dev), rows_dev)
        for i, group in enumerate(groups):
            out[i * rows_dev : (i + 1) * rows_dev, :] = group[rows, :]
        out[body : body + extra_rows, :] = parts


def apply_kernel(clip_limit, place, *refs):
    groups = refs[: 2 * ring_x]
    own_root, partner_first, partner_last, right_root = refs[8:12]
    blocks, payload, clip, root_v, right_v, sem = refs[12:]
    me = place[0]
    x, z = me // ring_z, me % ring_z
    parity = z % 2
    sign = 1 - 2 * parity
    row_blocks, half, block_size = own_root.shape
    owners, length, _ = payload.shape
    body = length - extra_rows
    group_body = groups[0].shape[0] - extra_rows
    rows_dev = group_body // roles

    own_rows, partner_rows = (pl.ds(aligned(side, half), half) for side in (parity, 1 - parity))
    early = partner_first.shape[0]
    first, last = pl.ds(0, early), pl.ds(early, row_blocks - early)
    bring = [
        pltpu.make_async_copy(own_root, root_v.at[:, own_rows], sem.at[0]),
        pltpu.make_async_copy(partner_first, root_v.at[first, partner_rows], sem.at[1]),
        pltpu.make_async_copy(partner_last, root_v.at[last, partner_rows], sem.at[3]),
        pltpu.make_async_copy(right_root, right_v, sem.at[2]),
    ]
    for copy in bring:
        copy.start()
    for i, origin in enumerate(origins):
        for d in range(ring_x):
            source = (x + ring_x - d) % ring_x * ring_z + (z + ring_z + sign * origin) % ring_z
            group = groups[i // roles * ring_x + d]
            first = i % roles * rows_dev
            blocks[pl.ds(aligned(source, rows_dev), rows_dev), :] = group[first : first + rows_dev, :]
    total_sq = sum(from_parts(group[group_body : group_body + extra_rows, :]) for group in groups)
    clip_factor = jnp.minimum(1.0, clip_limit / (jnp.sqrt(total_sq) + epsilon))
    clip[...] = jnp.broadcast_to(clip_factor[:, :lanes], clip.shape)
    for copy in bring:
        copy.wait()

    lane = lax.broadcasted_iota(jnp.int32, (1, lanes), 1)
    total = jnp.zeros((1, lanes), jnp.float32)
    for r in range(row_blocks):
        begin, end = r * block_size, (r + 1) * block_size
        block = blocks[begin:end, :]
        applied = jnp.dot(root_v[r], block, preferred_element_type=jnp.float32)
        precond = jnp.dot(
            applied.astype(jnp.bfloat16), right_v[r], preferred_element_type=jnp.float32
        )
        rounded = precond.astype(jnp.bfloat16)
        for f in range(begin // rows_dev, -(-end // rows_dev)):
            low, high = max(begin, f * rows_dev), min(end, (f + 1) * rows_dev)
            for c in range(half // lanes):
                at = c * rows_dev - f * rows_dev
                payload[f, at + low : at + high, :] = rounded[
                    low - begin : high - begin, c * lanes : (c + 1) * lanes
                ]
        wide = block.astype(jnp.float32)
        total += jnp.where(lane == r, scalar_sum(precond * precond), 0.0)
        total += jnp.where(lane == r + row_blocks, scalar_sum(wide * wide), 0.0)
    parts = in_parts(total)
    for f in range(owners):
        payload[f, body : body + extra_rows, :] = parts


def stat_kernel(
    place, clip, blocks, left_stat, right_stat, new_left, new_right, clip_out, stat_v, in_sem, out_sem
):
    row_blocks, half, block_size = left_stat.shape
    parity = place[0] % 2
    get, put = [], []
    for side, (stat, out) in enumerate(((left_stat, new_left), (right_stat, new_right))):
        for r in range(row_blocks):
            i = side * row_blocks + r
            get.append(pltpu.make_async_copy(stat.at[r], stat_v.at[i], in_sem.at[i]))
            put.append(pltpu.make_async_copy(stat_v.at[i], out.at[r], out_sem.at[i]))
            get[-1].start()
    clip_out[...] = clip[...]
    factor = clip[0:1, 0:1]
    coeff = (1.0 - decay_stat) * factor * factor
    for r in range(row_blocks):
        begin = r * block_size
        block = blocks[begin : begin + block_size, :]
        rows = blocks[pl.ds(pl.multiple_of(begin + parity * half, half), half), :]
        gram = lax.dot_general(
            rows, block, (((1,), (1,)), ((), ())), preferred_element_type=jnp.float32
        )
        get[r].wait()
        stat_v[r] = decay_stat * stat_v[r] + coeff * gram
        put[r].start()
    for r in range(row_blocks):
        i = row_blocks + r
        get[i].wait()
        for side in range(2):

            @pl.when(parity == side)
            def _():
                block = blocks[r * block_size : (r + 1) * block_size, :]
                gram = lax.dot_general(
                    block[:, side * half : (side + 1) * half], block,
                    (((0,), (0,)), ((), ())), preferred_element_type=jnp.float32,
                )
                stat_v[i] = decay_stat * stat_v[i] + coeff * gram

        put[i].start()
    for copy in put:
        copy.wait()


def finish_kernel(
    row_blocks, block_size, place, back, clip, momentum, new_momentum,
    back_v, clip_v, momentum_v, back_sem, clip_sem, in_sem, out_sem,
):
    me = place[0]
    rows_dev, all_cols = momentum.shape
    owners, length, _ = back.shape
    pieces = out_sem.shape[0]
    width = all_cols // pieces
    share = owners // pieces
    columns = all_cols // owners
    body = length - extra_rows

    get_clip = pltpu.make_async_copy(clip, clip_v, clip_sem)
    get_clip.start()
    get_back, get_momentum, put_momentum = [], [], []
    for q in range(pieces):
        some = pl.ds(q * share, share)
        get_back.append(pltpu.make_async_copy(back.at[some], back_v.at[some], back_sem.at[q]))
        get_back[-1].start()
    for q in range(pieces):
        part = pl.ds(q * width, width)
        get_momentum.append(
            pltpu.make_async_copy(momentum.at[:, part], momentum_v.at[:, part], in_sem.at[q])
        )
        put_momentum.append(
            pltpu.make_async_copy(momentum_v.at[:, part], new_momentum.at[:, part], out_sem.at[q])
        )
        get_momentum[-1].start()
    for copy in [get_clip] + get_back:
        copy.wait()

    parts = back_v[:, body : body + extra_rows, :].astype(jnp.float32)
    values = parts[:, 0, :] + parts[:, 1, :] + parts[:, 2, :]
    lane = lax.broadcasted_iota(jnp.int32, values.shape, 1)
    source = lax.broadcasted_iota(jnp.int32, values.shape, 0)
    paired = jnp.where(
        source % 2 == 0, pltpu.roll(values, owners - 1, 0), pltpu.roll(values, 1, 0)
    )
    pnorm = values + paired
    gnorm = pltpu.roll(values, lanes - row_blocks, 1)
    scale = clip_v[0:1, :] * jnp.sqrt(gnorm) / (jnp.sqrt(pnorm) + epsilon)
    first = me * rows_dev // block_size
    until = (first + 1) * block_size - me * rows_dev
    upper = jnp.sum(jnp.where(lane == first, scale, 0.0), axis=1, keepdims=True)
    lower = jnp.sum(
        jnp.where((lane == first + 1) & (lane < row_blocks), scale, 0.0), axis=1, keepdims=True
    )
    in_upper = lax.broadcasted_iota(jnp.int32, (rows_dev, lanes), 0) < until
    for q in range(pieces):
        get_momentum[q].wait()
        for s in range(q * share, (q + 1) * share):
            row_scale = jnp.where(in_upper, upper[s : s + 1], lower[s : s + 1])
            for c in range(columns // lanes):
                at = pl.ds(s * columns + c * lanes, lanes)
                moved = back_v[s, c * rows_dev : (c + 1) * rows_dev, :].astype(jnp.float32)
                momentum_v[:, at] = momentum_rate * momentum_v[:, at] + row_scale * moved
        put_momentum[q].start()
    for copy in put_momentum:
        copy.wait()


def keep_in_hbm(array):
    return pltpu.with_memory_space_constraint(array, pltpu.HBM)


def local(grad, momentum, left_stat, right_stat, left_root, right_root):
    owners = ring_x * ring_z
    place = lax.axis_index("fsdp").astype(jnp.int32).reshape(1)
    rows_dev, all_cols = grad.shape
    row_blocks, _, half, block_size = left_stat.shape
    all_rows = rows_dev * owners
    clip_limit = 0.5 * math.sqrt(all_rows * all_cols)
    length = rows_dev * half // lanes + extra_rows
    smem = pl.BlockSpec(memory_space=pltpu.SMEM)
    in_hbm = pl.BlockSpec(memory_space=pltpu.HBM)
    in_vmem = pl.BlockSpec(memory_space=pltpu.VMEM)
    some_vmem = pltpu.CompilerParams(vmem_limit_bytes=16 << 20)
    flops = row_blocks * 2 * half * block_size * block_size
    dma = pltpu.SemaphoreType.DMA

    def cost(flops, megabytes):
        return pl.CostEstimate(flops=flops, bytes_accessed=megabytes << 20, transcendentals=0)

    def array(*shape, dtype=jnp.bfloat16):
        return jax.ShapeDtypeStruct(shape, dtype)

    left_root = left_root.reshape(row_blocks, half, block_size)
    right_root = right_root.reshape(row_blocks, block_size, half)
    left_stat = left_stat.reshape(row_blocks, half, block_size)
    right_stat = right_stat.reshape(row_blocks, half, block_size)
    group = array(ring_x * rows_dev + extra_rows, block_size)
    stat = array(row_blocks, half, block_size, dtype=jnp.float32)
    wide = array(rows_dev, all_cols, dtype=jnp.float32)
    still = lambda z: 0
    to_partner = outward(-1)

    early = row_blocks - 1
    partner_first = shifted(left_root[:early], 0, to_partner)
    *sent, own = pl.pallas_call(
        cut_kernel,
        out_shape=[group] * roles,
        in_specs=[smem, in_hbm],
        out_specs=[in_vmem] * roles,
        scratch_shapes=[dma((roles * ring_x,))],
        compiler_params=some_vmem,
        cost_estimate=cost(0, 1),
        name="cut",
    )(place, keep_in_hbm(grad))
    far, same, cross = (shifted(block, 0, outward(n)) for block, n in zip(sent, (3, -2, 1)))
    last_root = pl.pallas_call(
        hold_kernel,
        out_shape=array(row_blocks - early, half, block_size),
        in_specs=[in_hbm, in_hbm],
        out_specs=in_vmem,
        scratch_shapes=[dma],
        cost_estimate=cost(0, 1),
        name="hold",
    )(keep_in_hbm(left_root), cross)
    partner_last = shifted(last_root, 0, to_partner)
    parts = pl.pallas_call(
        pick_kernel,
        out_shape=[group] * ring_x,
        in_specs=[smem] + [in_vmem] * roles,
        out_specs=[in_vmem] * ring_x,
        compiler_params=some_vmem,
        cost_estimate=cost(0, 2),
        name="pick",
    )(place, far, same, cross, own)
    near = [parts[0]] + [shifted(parts[d], d, still) for d in range(1, ring_x)]
    swapped = [shifted(parts[d], d, to_partner) for d in range(ring_x) if d != 2]
    swapped.insert(2, shifted(near[2], 0, to_partner))

    blocks, payload, clip = pl.pallas_call(
        functools.partial(apply_kernel, clip_limit),
        out_shape=[
            array(all_rows, block_size),
            array(owners, length, lanes),
            array(8, lanes, dtype=jnp.float32),
        ],
        in_specs=[smem] + [in_vmem] * (2 * ring_x) + [in_hbm] * 4,
        out_specs=[in_vmem] * 3,
        scratch_shapes=[
            pltpu.VMEM((row_blocks, block_size, block_size), jnp.bfloat16),
            pltpu.VMEM((row_blocks, block_size, half), jnp.bfloat16),
            dma((4,)),
        ],
        compiler_params=some_vmem,
        cost_estimate=cost(3 * flops, 6),
        name="apply",
    )(
        place, *near, *swapped,
        keep_in_hbm(left_root), partner_first, partner_last, keep_in_hbm(right_root),
    )
    back = lax.all_to_all(payload, "fsdp", split_axis=0, concat_axis=0, tiled=True)
    new_left, new_right, clip = pl.pallas_call(
        stat_kernel,
        out_shape=[stat] * 2 + [array(8, lanes, dtype=jnp.float32)],
        in_specs=[smem, in_vmem, in_vmem, in_hbm, in_hbm],
        out_specs=[in_hbm, in_hbm, in_vmem],
        scratch_shapes=[
            pltpu.VMEM((2 * row_blocks, half, block_size), jnp.float32),
            dma((2 * row_blocks,)),
            dma((2 * row_blocks,)),
        ],
        compiler_params=some_vmem,
        cost_estimate=cost(2 * flops, 8),
        name="statistics",
    )(place, clip, blocks, keep_in_hbm(left_stat), keep_in_hbm(right_stat))

    quarters = 4
    new_momentum = pl.pallas_call(
        functools.partial(finish_kernel, row_blocks, block_size),
        out_shape=wide,
        in_specs=[smem] + [in_hbm] * 3,
        out_specs=in_hbm,
        scratch_shapes=[
            pltpu.VMEM((owners, length, lanes), jnp.bfloat16),
            pltpu.VMEM((8, lanes), jnp.float32),
            pltpu.VMEM((rows_dev, all_cols), jnp.float32),
            dma((quarters,)),
            dma,
            dma((quarters,)),
            dma((quarters,)),
        ],
        compiler_params=some_vmem,
        cost_estimate=cost(1 << 22, 4),
        name="finish",
    )(place, back, clip, keep_in_hbm(momentum))
    shape = (row_blocks, 1, half, block_size)
    return (new_momentum, new_left.reshape(shape), new_right.reshape(shape))


def solution(mesh):
    return jax.shard_map(
        local,
        mesh=mesh,
        in_specs=(
            P(("section", "fsdp"), None),
            P(("section", "fsdp"), None),
            P("section", "fsdp", None, None),
            P("section", "fsdp", None, None),
            P("section", "fsdp", None, None),
            P("section", "fsdp", None, None),
        ),
        out_specs=(
            P(("section", "fsdp"), None),
            P("section", "fsdp", None, None),
            P("section", "fsdp", None, None),
        ),
        check_vma=False,
    )
```

time: 103 us -> 92.5 us (0.90)
  local copies, waits for them, and re-layouts: 4.13 us -> 1.08 us
  waiting for transfers between devices: 51 us -> 48.2 us
  starting transfers between devices: 30.3 us -> 28 us
  Pallas kernels: 16.3 us -> 14.2 us
    ppermute x6 -> x12, starting transfers between devices: 13 us -> 21.2 us  [shifted(): return lax.ppermute(block, 'fsdp', route)]
    ppermute x6 -> x0, waiting for transfers between devices: 7.4 us -> none  [the longest x4 7.39 us: local(): fars += [swap(far) for far in fars]]
    ppermute x6 -> x0, starting transfers between devices: 6.96 us -> none  [the longest x4 4.95 us: local(): fars += [swap(far) for far in fars]]
    all_to_all x1 -> x0, starting transfers between devices: 4.44 us -> none  [local(): lax.all_to_all(slabs, 'fsdp', split_axis=0, concat_axis=0, tiled=True, ax...]
    ppermute x6 -> x12, waiting for transfers between devices: 24.7 us -> 29 us  [shifted(): return lax.ppermute(block, 'fsdp', route)]
    unnamed x18 -> x2, local copies, waits for them, and re-layouts: 4.13 us -> 0.01 us
    pallas_call x5 -> x6, Pallas kernels: 16.3 us -> 14.2 us  [the longest x1 3.95 us: local(): pl.pallas_call(functools.partial(apply_kernel, clip_limit), out_shape=[ar...]
    slice x0 -> x1, local copies, waits for them, and re-layouts: none -> 1.08 us  [local(): partner_first = shifted(left_root[:early], 0, to_partner)]
  transfers between devices with their start and end apart: 14 -> 13, of which waited for: 8 -> 9; matrix products, arithmetic and copies ran while one was open for 0% -> 1% of each run, Pallas kernels for 3% -> 6%
where the time goes in v3:
time: 92.5 us; the launch traced here: 92.1 us
  waiting for transfers between devices  48.2 us (52%)
  starting transfers between devices  28 us (30%)
  Pallas kernels  14.2 us (15%)
  local copies, waits for them, and re-layouts  1.08 us (1%)
    ppermute x12, waiting for transfers between devices, shifted(): return lax.ppermute(block, 'fsdp', route)  29 us
    ppermute x12, starting transfers between devices, shifted(): return lax.ppermute(block, 'fsdp', route)  21.2 us
    all_to_all x1, waiting for transfers between devices, local(): lax.all_to_all(payload, 'fsdp', split_axis=0, concat_axis=0, tiled=True)  19.1 us
    all_to_all x1, starting transfers between devices, local(): lax.all_to_all(payload, 'fsdp', split_axis=0, concat_axis=0, tiled=True)  6.79 us
    pallas_call x1, Pallas kernels, local(): pl.pallas_call(functools.partial(apply_kernel, clip_limit), out_shape=[ar...  3.95 us
    pallas_call x1, Pallas kernels, local(): pl.pallas_call(stat_kernel, out_shape=[stat] * 2 + [array(8, lanes, dtype...  3.75 us
    pallas_call x1, Pallas kernels, local(): pl.pallas_call(functools.partial(finish_kernel, row_blocks, block_size),...  3.37 us
  transfers between devices with their start and end apart: 13, of which 9 were waited for; matrix products, arithmetic and copies ran while one was open for 1% of the time, Pallas kernels for 6%

profile of v3, /device:TPU:8, one launch (start us, length us, event | category | flops | bytes accessed | tf_op | source)
XLA Modules:
  0.0 92.1 jit_solution(4067768567277254429)
XLA Ops:
  0.6 1.4 %cut.1 = (bf16[200,512]{1,0:T(8,128)(2,1)S(1)}, bf16[200,512]{1,0:T(8,128)(2,1)S(1)}, bf16[200,512]{1,0:T(8,128)(2,1)S(1)}, bf16[200,512]{1,0:T(8,128)(2,1)S(1)}) custom-call(s32[1]{0:T(128)} %bitcast.place, bf16[48,8192]{1,0:T(8,128)(2,1)} %grad.1), custom_call_target="tpu_custom_call" | custom-call | bytes 1048576 | tf_op jit(solution)/shard_map/cut/pallas_call | solution.py:311
  2.0 6.8 %collective-permute-start = (bf16[200,512]{1,0:T(8,128)(2,1)S(1)}, bf16[200,512]{1,0:T(8,128)(2,1)S(1)}, u32[]{:S(2)}, u32[]{:S(2)}) collective-permute-start(bf16[200,512]{1,0:T(8,128)(2,1)S(1)} %get-tuple-element.17), channel_id=1, source_target_pairs={{0,5},{1,4},{2,7},{3,6},{4,1},{5,0},{6,3},{7,2},{8,13},{9,12},{10,... | collective-permute-start | bytes 614408 | tf_op jit(solution)/shard_map/ppermute | solution.py:29
  8.9 1.5 %collective-permute-start.1 = (bf16[200,512]{1,0:T(8,128)(2,1)S(1)}, bf16[200,512]{1,0:T(8,128)(2,1)S(1)}, u32[]{:S(2)}, u32[]{:S(2)}) collective-permute-start(bf16[200,512]{1,0:T(8,128)(2,1)S(1)} %get-tuple-element.18), channel_id=1, source_target_pairs={{0,2},{1,7},{2,4},{3,1},{4,6},{5,3},{6,0},{7,5},{8,10},{9,15},{10,... | collective-permute-start | bytes 614408 | tf_op jit(solution)/shard_map/ppermute | solution.py:29
  10.3 0.0 collective-permute-start.2
  10.3 1.1 %slice_bitcast_fusion = bf16[2,256,512]{2,1,0:T(8,128)(2,1)S(1)} fusion(bf16[3,1,256,512]{3,2,0,1:T(8,128)(2,1)} %bitcast.14), kind=kLoop, calls=%fused_computation | loop fusion | bytes 1048576 | tf_op jit(solution)/shard_map/slice | solution.py:310
  11.4 0.7 collective-permute-start.10
  12.1 10.2 %collective-permute-done.refs_0_ = bf16[200,512]{1,0:T(8,128)(2,1)S(1)} collective-permute-done((bf16[200,512]{1,0:T(8,128)(2,1)S(1)}, bf16[200,512]{1,0:T(8,128)(2,1)S(1)}, u32[]{:S(2)}, u32[]{:S(2)}) %collective-permute-start) | collective-permute-done | bytes 204832 | tf_op jit(solution)/shard_map/ppermute | solution.py:29
  22.3 0.0 collective-permute-done.1.refs_1_
  22.3 4.1 %collective-permute-done.2.refs_2_.earlier = bf16[200,512]{1,0:T(8,128)(2,1)S(1)} collective-permute-done((bf16[200,512]{1,0:T(8,128)(2,1)S(1)}, bf16[200,512]{1,0:T(8,128)(2,1)S(1)}, u32[]{:S(2)}, u32[]{:S(2)}) %collective-permute-start.2) | collective-permute-done | bytes 204832 | tf_op jit(solution)/shard_map/ppermute | solution.py:29
  26.4 0.0 copy-start
  26.4 0.1 pick.1
  26.4 3.1 %collective-permute-start.4 = (bf16[200,512]{1,0:T(8,128)(2,1)S(1)}, bf16[200,512]{1,0:T(8,128)(2,1)S(1)}, u32[]{:S(2)}, u32[]{:S(2)}) collective-permute-start(bf16[200,512]{1,0:T(8,128)(2,1)S(1)} %get-tuple-element.23), channel_id=1, source_target_pairs={{0,16},{1,17},{2,18},{3,19},{4,20},{5,21},{6,22},{7,23},{8,24},{9,... | collective-permute-start | bytes 614408 | tf_op jit(solution)/shard_map/ppermute | solution.py:29
  29.6 1.8 %collective-permute-start.6 = (bf16[200,512]{1,0:T(8,128)(2,1)S(1)}, bf16[200,512]{1,0:T(8,128)(2,1)S(1)}, u32[]{:S(2)}, u32[]{:S(2)}) collective-permute-start(bf16[200,512]{1,0:T(8,128)(2,1)S(1)} %get-tuple-element.21.refs_0_), channel_id=1, source_target_pairs={{0,1},{1,0},{2,3},{3,2},{4,5},{5,4},{6,7},{7,6},{8,9},{9,8},{10,11... | collective-permute-start | bytes 614408 | tf_op jit(solution)/shard_map/ppermute | solution.py:29
  31.3 0.3 collective-permute-start.7
  31.6 0.3 collective-permute-start.3
  31.9 0.0 copy-done
  31.9 1.7 %hold.1 = bf16[1,256,512]{2,1,0:T(8,128)(2,1)} custom-call(bf16[3,256,512]{2,1,0:T(8,128)(2,1)} %bitcast.15, bf16[200,512]{1,0:T(8,128)(2,1)} %copy-done), custom_call_target="tpu_custom_call" | custom-call | bytes 1048576 | tf_op jit(solution)/shard_map/hold/pallas_call | solution.py:322
  33.6 2.2 %collective-permute-done.4.refs_2_ = bf16[200,512]{1,0:T(8,128)(2,1)S(1)} collective-permute-done((bf16[200,512]{1,0:T(8,128)(2,1)S(1)}, bf16[200,512]{1,0:T(8,128)(2,1)S(1)}, u32[]{:S(2)}, u32[]{:S(2)}) %collective-permute-start.4) | collective-permute-done | bytes 204832 | tf_op jit(solution)/shard_map/ppermute | solution.py:29
  35.8 1.7 %collective-permute-start.11 = (bf16[1,256,512]{2,1,0:T(8,128)(2,1)}, bf16[1,256,512]{2,1,0:T(8,128)(2,1)S(1)}, u32[]{:S(2)}, u32[]{:S(2)}) collective-permute-start(bf16[1,256,512]{2,1,0:T(8,128)(2,1)} %hold.1), channel_id=1, source_target_pairs={{0,1},{1,0},{2,3},{3,2},{4,5},{5,4},{6,7},{7,6},{8,9},{9,8},{10,11... | collective-permute-start | bytes 786440 | tf_op jit(solution)/shard_map/ppermute | solution.py:29
  37.5 0.1 collective-permute-done.6.refs_4_
  37.5 2.3 %collective-permute-start.9 = (bf16[200,512]{1,0:T(8,128)(2,1)S(1)}, bf16[200,512]{1,0:T(8,128)(2,1)S(1)}, u32[]{:S(2)}, u32[]{:S(2)}) collective-permute-start(bf16[200,512]{1,0:T(8,128)(2,1)S(1)} %get-tuple-element.24), channel_id=1, source_target_pairs={{0,25},{1,24},{2,27},{3,26},{4,29},{5,28},{6,31},{7,30},{8,1},{9,0... | collective-permute-start | bytes 614408 | tf_op jit(solution)/shard_map/ppermute | solution.py:29
  39.9 2.7 %collective-permute-done.7.refs_5_ = bf16[200,512]{1,0:T(8,128)(2,1)S(1)} collective-permute-done((bf16[200,512]{1,0:T(8,128)(2,1)S(1)}, bf16[200,512]{1,0:T(8,128)(2,1)S(1)}, u32[]{:S(2)}, u32[]{:S(2)}) %collective-permute-start.7) | collective-permute-done | bytes 204832 | tf_op jit(solution)/shard_map/ppermute | solution.py:29
  42.6 0.6 collective-permute-start.5
  43.2 0.2 collective-permute-done.3.refs_1_
  43.4 2.2 %collective-permute-start.8 = (bf16[200,512]{1,0:T(8,128)(2,1)S(1)}, bf16[200,512]{1,0:T(8,128)(2,1)S(1)}, u32[]{:S(2)}, u32[]{:S(2)}) collective-permute-start(bf16[200,512]{1,0:T(8,128)(2,1)S(1)} %collective-permute-done.4.refs_2_), channel_id=1, source_target_pairs={{0,1},{1,0},{2,3},{3,2},{4,5},{5,4},{6,7},{7,6},{8,9},{9,8},{10,11... | collective-permute-start | bytes 614408 | tf_op jit(solution)/shard_map/ppermute | solution.py:29
  45.5 6.6 %collective-permute-done.9.refs_7_ = bf16[200,512]{1,0:T(8,128)(2,1)S(1)} collective-permute-done((bf16[200,512]{1,0:T(8,128)(2,1)S(1)}, bf16[200,512]{1,0:T(8,128)(2,1)S(1)}, u32[]{:S(2)}, u32[]{:S(2)}) %collective-permute-start.9) | collective-permute-done | bytes 204832 | tf_op jit(solution)/shard_map/ppermute | solution.py:29
  52.1 0.0 collective-permute-done.5.refs_3_
  52.2 0.0 collective-permute-done.11.refs_10_
  52.2 0.0 collective-permute-done.10.refs_9_
  52.2 2.9 %collective-permute-done.8.refs_6_ = bf16[200,512]{1,0:T(8,128)(2,1)S(1)} collective-permute-done((bf16[200,512]{1,0:T(8,128)(2,1)S(1)}, bf16[200,512]{1,0:T(8,128)(2,1)S(1)}, u32[]{:S(2)}, u32[]{:S(2)}) %collective-permute-start.8) | collective-permute-done | bytes 204832 | tf_op jit(solution)/shard_map/ppermute | solution.py:29
  55.1 3.9 %apply.1 = (bf16[1536,512]{1,0:T(8,128)(2,1)S(1)}, bf16[32,104,128]{2,1,0:T(8,128)(2,1)}, f32[8,128]{1,0:T(8,128)S(1)}) custom-call(s32[1]{0:T(128)} %bitcast.place, bf16[200,512]{1,0:T(8,128)(2,1)S(1)} %get-tuple-element.21.refs_0_, bf16[200,512]{1,0:T(8,128)(2,1)S(1)} %collective-permute-done.3.refs_1_, ...), custom_call_target="tpu_custom_call" | custom-call | flops 1207959552 | bytes 6291456 | tf_op jit(solution)/shard_map/apply/pallas_call | solution.py:345
  59.1 6.8 %all-to-all-start = ((bf16[32,104,128]{2,1,0:T(8,128)(2,1)}), bf16[32,104,128]{2,1,0:T(8,128)(2,1)S(1)}, u32[]{:S(2)}, u32[]{:S(2)}) async-start(bf16[32,104,128]{2,1,0:T(8,128)(2,1)} %get-tuple-element.25), calls=%async_computation | async-start | bytes 1703936 | tf_op jit(solution)/shard_map/all_to_all | solution.py:366
  65.9 3.7 %statistics.1 = (f32[3,256,512]{2,1,0:T(8,128)}, f32[3,256,512]{2,1,0:T(8,128)}, f32[8,128]{1,0:T(8,128)S(1)}) custom-call(s32[1]{0:T(128)} %bitcast.place, f32[8,128]{1,0:T(8,128)S(1)} %get-tuple-element.26.clip, bf16[1536,512]{1,0:T(8,128)(2,1)S(1)} %get-tuple-element.27.blocks, f32[3,256,512]{2,1,0:T(8,128)} %bitcast.17, f32[3,256,512]{2,1,0:T(8,128)} %bitcast.18), custom_call_target="tpu_custom_call" | custom-call | flops 805306368 | bytes 8388608 | tf_op jit(solution)/shard_map/statistics/pallas_call | solution.py:367
  69.6 19.1 %all-to-all-done.back = bf16[32,104,128]{2,1,0:T(8,128)(2,1)S(1)} async-done(((bf16[32,104,128]{2,1,0:T(8,128)(2,1)}), bf16[32,104,128]{2,1,0:T(8,128)(2,1)S(1)}, u32[]{:S(2)}, u32[]{:S(2)}) %all-to-all-start) | async-done | bytes 852000 | tf_op jit(solution)/shard_map/all_to_all | solution.py:366
  88.7 3.4 %finish.1 = f32[48,8192]{1,0:T(8,128)} custom-call(s32[1]{0:T(128)} %bitcast.place, bf16[32,104,128]{2,1,0:T(8,128)(2,1)S(1)} %all-to-all-done.back, f32[8,128]{1,0:T(8,128)S(1)} %get-tuple-element.28.clip, f32[48,8192]{1,0:T(8,128)} %momentum.1), custom_call_target="tpu_custom_call" | custom-call | flops 4194304 | bytes 4194304 | tf_op jit(solution)/shard_map/finish/pallas_call | solution.py:383
Async XLA Ops:
  2.0 20.3 %collective-permute-start = (bf16[200,512]{1,0:T(8,128)(2,1)S(1)}, bf16[200,512]{1,0:T(8,128)(2,1)S(1)}, u32[]{:S(2)}, u32[]{:S(2)}) collective-permute-start(bf16[200,512]{1,0:T(8,128)(2,1)S(1)} %get-tuple-element.17), channel_id=1, source_target_pairs={{0,5},{1,4},{2,7},{3,6},{4,1},{5,0},{6,3},{7,2},{8,13},{9,12},{10,... | collective-permute-start | bytes 614408 | tf_op jit(solution)/shard_map/ppermute | solution.py:29
  8.9 13.4 %collective-permute-start.1 = (bf16[200,512]{1,0:T(8,128)(2,1)S(1)}, bf16[200,512]{1,0:T(8,128)(2,1)S(1)}, u32[]{:S(2)}, u32[]{:S(2)}) collective-permute-start(bf16[200,512]{1,0:T(8,128)(2,1)S(1)} %get-tuple-element.18), channel_id=1, source_target_pairs={{0,2},{1,7},{2,4},{3,1},{4,6},{5,3},{6,0},{7,5},{8,10},{9,15},{10,... | collective-permute-start | bytes 614408 | tf_op jit(solution)/shard_map/ppermute | solution.py:29
  10.3 16.0 %collective-permute-start.2 = (bf16[200,512]{1,0:T(8,128)(2,1)S(1)}, bf16[200,512]{1,0:T(8,128)(2,1)S(1)}, u32[]{:S(2)}, u32[]{:S(2)}) collective-permute-start(bf16[200,512]{1,0:T(8,128)(2,1)S(1)} %get-tuple-element.19), channel_id=1, source_target_pairs={{0,7},{1,2},{2,1},{3,4},{4,3},{5,6},{6,5},{7,0},{8,15},{9,10},{10,... | collective-permute-start | bytes 614408 | tf_op jit(solution)/shard_map/ppermute | solution.py:29
  11.4 40.7 %collective-permute-start.10 = (bf16[2,256,512]{2,1,0:T(8,128)(2,1)S(1)}, bf16[2,256,512]{2,1,0:T(8,128)(2,1)S(1)}, u32[]{:S(2)}, u32[]{:S(2)}) collective-permute-start(bf16[2,256,512]{2,1,0:T(8,128)(2,1)S(1)} %slice_bitcast_fusion), channel_id=1, source_target_pairs={{0,1},{1,0},{2,3},{3,2},{4,5},{5,4},{6,7},{7,6},{8,9},{9,8},{10,11... | collective-permute-start | bytes 1572872 | tf_op jit(solution)/shard_map/ppermute | solution.py:29
  26.4 5.5 %copy-start = (bf16[200,512]{1,0:T(8,128)(2,1)}, bf16[200,512]{1,0:T(8,128)(2,1)S(1)}, u32[]{:S(2)}) copy-start(bf16[200,512]{1,0:T(8,128)(2,1)S(1)} %collective-permute-done.2.refs_2_.earlier) | copy-start | bytes 614404
  26.4 9.3 %collective-permute-start.4 = (bf16[200,512]{1,0:T(8,128)(2,1)S(1)}, bf16[200,512]{1,0:T(8,128)(2,1)S(1)}, u32[]{:S(2)}, u32[]{:S(2)}) collective-permute-start(bf16[200,512]{1,0:T(8,128)(2,1)S(1)} %get-tuple-element.23), channel_id=1, source_target_pairs={{0,16},{1,17},{2,18},{3,19},{4,20},{5,21},{6,22},{7,23},{8,24},{9,... | collective-permute-start | bytes 614408 | tf_op jit(solution)/shard_map/ppermute | solution.py:29
  29.6 8.0 %collective-permute-start.6 = (bf16[200,512]{1,0:T(8,128)(2,1)S(1)}, bf16[200,512]{1,0:T(8,128)(2,1)S(1)}, u32[]{:S(2)}, u32[]{:S(2)}) collective-permute-start(bf16[200,512]{1,0:T(8,128)(2,1)S(1)} %get-tuple-element.21.refs_0_), channel_id=1, source_target_pairs={{0,1},{1,0},{2,3},{3,2},{4,5},{5,4},{6,7},{7,6},{8,9},{9,8},{10,11... | collective-permute-start | bytes 614408 | tf_op jit(solution)/shard_map/ppermute | solution.py:29
  31.3 11.3 %collective-permute-start.7 = (bf16[200,512]{1,0:T(8,128)(2,1)S(1)}, bf16[200,512]{1,0:T(8,128)(2,1)S(1)}, u32[]{:S(2)}, u32[]{:S(2)}) collective-permute-start(bf16[200,512]{1,0:T(8,128)(2,1)S(1)} %get-tuple-element.22), channel_id=1, source_target_pairs={{0,9},{1,8},{2,11},{3,10},{4,13},{5,12},{6,15},{7,14},{8,17},{9,16... | collective-permute-start | bytes 614408 | tf_op jit(solution)/shard_map/ppermute | solution.py:29
  31.6 11.7 %collective-permute-start.3 = (bf16[200,512]{1,0:T(8,128)(2,1)S(1)}, bf16[200,512]{1,0:T(8,128)(2,1)S(1)}, u32[]{:S(2)}, u32[]{:S(2)}) collective-permute-start(bf16[200,512]{1,0:T(8,128)(2,1)S(1)} %get-tuple-element.22), channel_id=1, source_target_pairs={{0,8},{1,9},{2,10},{3,11},{4,12},{5,13},{6,14},{7,15},{8,16},{9,17... | collective-permute-start | bytes 614408 | tf_op jit(solution)/shard_map/ppermute | solution.py:29
  35.8 16.4 %collective-permute-start.11 = (bf16[1,256,512]{2,1,0:T(8,128)(2,1)}, bf16[1,256,512]{2,1,0:T(8,128)(2,1)S(1)}, u32[]{:S(2)}, u32[]{:S(2)}) collective-permute-start(bf16[1,256,512]{2,1,0:T(8,128)(2,1)} %hold.1), channel_id=1, source_target_pairs={{0,1},{1,0},{2,3},{3,2},{4,5},{5,4},{6,7},{7,6},{8,9},{9,8},{10,11... | collective-permute-start | bytes 786440 | tf_op jit(solution)/shard_map/ppermute | solution.py:29
  37.5 14.6 %collective-permute-start.9 = (bf16[200,512]{1,0:T(8,128)(2,1)S(1)}, bf16[200,512]{1,0:T(8,128)(2,1)S(1)}, u32[]{:S(2)}, u32[]{:S(2)}) collective-permute-start(bf16[200,512]{1,0:T(8,128)(2,1)S(1)} %get-tuple-element.24), channel_id=1, source_target_pairs={{0,25},{1,24},{2,27},{3,26},{4,29},{5,28},{6,31},{7,30},{8,1},{9,0... | collective-permute-start | bytes 614408 | tf_op jit(solution)/shard_map/ppermute | solution.py:29
  42.6 9.6 %collective-permute-start.5 = (bf16[200,512]{1,0:T(8,128)(2,1)S(1)}, bf16[200,512]{1,0:T(8,128)(2,1)S(1)}, u32[]{:S(2)}, u32[]{:S(2)}) collective-permute-start(bf16[200,512]{1,0:T(8,128)(2,1)S(1)} %get-tuple-element.24), channel_id=1, source_target_pairs={{0,24},{1,25},{2,26},{3,27},{4,28},{5,29},{6,30},{7,31},{8,0},{9,1... | collective-permute-start | bytes 614408 | tf_op jit(solution)/shard_map/ppermute | solution.py:29
  43.4 11.7 %collective-permute-start.8 = (bf16[200,512]{1,0:T(8,128)(2,1)S(1)}, bf16[200,512]{1,0:T(8,128)(2,1)S(1)}, u32[]{:S(2)}, u32[]{:S(2)}) collective-permute-start(bf16[200,512]{1,0:T(8,128)(2,1)S(1)} %collective-permute-done.4.refs_2_), channel_id=1, source_target_pairs={{0,1},{1,0},{2,3},{3,2},{4,5},{5,4},{6,7},{7,6},{8,9},{9,8},{10,11... | collective-permute-start | bytes 614408 | tf_op jit(solution)/shard_map/ppermute | solution.py:29
  59.1 29.7 %all-to-all-start = ((bf16[32,104,128]{2,1,0:T(8,128)(2,1)}), bf16[32,104,128]{2,1,0:T(8,128)(2,1)S(1)}, u32[]{:S(2)}, u32[]{:S(2)}) async-start(bf16[32,104,128]{2,1,0:T(8,128)(2,1)} %get-tuple-element.25), calls=%async_computation | async-start | bytes 1703936 | tf_op jit(solution)/shard_map/all_to_all | solution.py:366

commit v4 on v3

--- a/solution.py
+++ b/solution.py
@@ -82,15 +82,8 @@
         out[body : body + extra_rows, :] = parts
 
 
-def hold_kernel(root, earlier, out, sem):
-    last = out.shape[0]
-    copy = pltpu.make_async_copy(root.at[pl.ds(root.shape[0] - last, last)], out, sem)
-    copy.start()
-    copy.wait()
-
-
 def pick_kernel(place, *refs):
-    groups, outs = refs[:roles], refs[roles:]
+    groups, outs = refs[:roles], refs[roles + 1 :]
     x = place[0] // ring_z
     body = groups[0].shape[0] - extra_rows
     rows_dev = body // ring_x
@@ -103,31 +96,33 @@
         out[body : body + extra_rows, :] = parts
 
 
+def root_kernel(place, own_root, partner_root, right_root, earlier, roots, right, sem):
+    half = own_root.shape[1]
+    parity = place[0] % 2
+    own_rows, partner_rows = (pl.ds(aligned(side, half), half) for side in (parity, 1 - parity))
+    bring = [
+        pltpu.make_async_copy(own_root, roots.at[:, own_rows], sem.at[0]),
+        pltpu.make_async_copy(partner_root, roots.at[:, partner_rows], sem.at[1]),
+        pltpu.make_async_copy(right_root, right, sem.at[2]),
+    ]
+    for copy in bring:
+        copy.start()
+    for copy in bring:
+        copy.wait()
+
+
 def apply_kernel(clip_limit, place, *refs):
     groups = refs[: 2 * ring_x]
-    own_root, partner_first, partner_last, right_root = refs[8:12]
-    blocks, payload, clip, root_v, right_v, sem = refs[12:]
+    root_v, right_v, blocks, payload, clip = refs[8:]
     me = place[0]
     x, z = me // ring_z, me % ring_z
-    parity = z % 2
-    sign = 1 - 2 * parity
-    row_blocks, half, block_size = own_root.shape
+    sign = 1 - 2 * (z % 2)
+    row_blocks, block_size, half = right_v.shape
     owners, length, _ = payload.shape
     body = length - extra_rows
     group_body = groups[0].shape[0] - extra_rows
     rows_dev = group_body // roles
 
-    own_rows, partner_rows = (pl.ds(aligned(side, half), half) for side in (parity, 1 - parity))
-    early = partner_first.shape[0]
-    first, last = pl.ds(0, early), pl.ds(early, row_blocks - early)
-    bring = [
-        pltpu.make_async_copy(own_root, root_v.at[:, own_rows], sem.at[0]),
-        pltpu.make_async_copy(partner_first, root_v.at[first, partner_rows], sem.at[1]),
-        pltpu.make_async_copy(partner_last, root_v.at[last, partner_rows], sem.at[3]),
-        pltpu.make_async_copy(right_root, right_v, sem.at[2]),
-    ]
-    for copy in bring:
-        copy.start()
     for i, origin in enumerate(origins):
         for d in range(ring_x):
             source = (x + ring_x - d) % ring_x * ring_z + (z + ring_z + sign * origin) % ring_z
@@ -137,8 +132,6 @@
     total_sq = sum(from_parts(group[group_body : group_body + extra_rows, :]) for group in groups)
     clip_factor = jnp.minimum(1.0, clip_limit / (jnp.sqrt(total_sq) + epsilon))
     clip[...] = jnp.broadcast_to(clip_factor[:, :lanes], clip.shape)
-    for copy in bring:
-        copy.wait()
 
     lane = lax.broadcasted_iota(jnp.int32, (1, lanes), 1)
     total = jnp.zeros((1, lanes), jnp.float32)
@@ -211,7 +204,7 @@
 
 def finish_kernel(
     row_blocks, block_size, place, back, clip, momentum, new_momentum,
-    back_v, clip_v, momentum_v, back_sem, clip_sem, in_sem, out_sem,
+    back_v, norm_v, clip_v, momentum_v, back_sem, norm_sem, clip_sem, in_sem, out_sem,
 ):
     me = place[0]
     rows_dev, all_cols = momentum.shape
@@ -222,26 +215,31 @@
     columns = all_cols // owners
     body = length - extra_rows
 
-    get_clip = pltpu.make_async_copy(clip, clip_v, clip_sem)
-    get_clip.start()
+    first_here = [
+        pltpu.make_async_copy(back.at[:, pl.ds(body, extra_rows)], norm_v, norm_sem),
+        pltpu.make_async_copy(clip, clip_v, clip_sem),
+    ]
+    for copy in first_here:
+        copy.start()
     get_back, get_momentum, put_momentum = [], [], []
     for q in range(pieces):
-        some = pl.ds(q * share, share)
-        get_back.append(pltpu.make_async_copy(back.at[some], back_v.at[some], back_sem.at[q]))
-        get_back[-1].start()
-    for q in range(pieces):
-        part = pl.ds(q * width, width)
+        some, part = pl.ds(q * share, share), pl.ds(q * width, width)
+        rows = pl.ds(0, body)
+        get_back.append(
+            pltpu.make_async_copy(back.at[some, rows], back_v.at[some], back_sem.at[q])
+        )
         get_momentum.append(
             pltpu.make_async_copy(momentum.at[:, part], momentum_v.at[:, part], in_sem.at[q])
         )
         put_momentum.append(
             pltpu.make_async_copy(momentum_v.at[:, part], new_momentum.at[:, part], out_sem.at[q])
         )
+        get_back[-1].start()
         get_momentum[-1].start()
-    for copy in [get_clip] + get_back:
+    for copy in first_here:
         copy.wait()
 
-    parts = back_v[:, body : body + extra_rows, :].astype(jnp.float32)
+    parts = norm_v[...].astype(jnp.float32)
     values = parts[:, 0, :] + parts[:, 1, :] + parts[:, 2, :]
     lane = lax.broadcasted_iota(jnp.int32, values.shape, 1)
     source = lax.broadcasted_iota(jnp.int32, values.shape, 0)
@@ -259,6 +257,7 @@
     )
     in_upper = lax.broadcasted_iota(jnp.int32, (rows_dev, lanes), 0) < until
     for q in range(pieces):
+        get_back[q].wait()
         get_momentum[q].wait()
         for s in range(q * share, (q + 1) * share):
             row_scale = jnp.where(in_upper, upper[s : s + 1], lower[s : s + 1])
@@ -306,8 +305,7 @@
     still = lambda z: 0
     to_partner = outward(-1)
 
-    early = row_blocks - 1
-    partner_first = shifted(left_root[:early], 0, to_partner)
+    partner_root = shifted(left_root, 0, to_partner)
     *sent, own = pl.pallas_call(
         cut_kernel,
         out_shape=[group] * roles,
@@ -319,28 +317,32 @@
         name="cut",
     )(place, keep_in_hbm(grad))
     far, same, cross = (shifted(block, 0, outward(n)) for block, n in zip(sent, (3, -2, 1)))
-    last_root = pl.pallas_call(
-        hold_kernel,
-        out_shape=array(row_blocks - early, half, block_size),
-        in_specs=[in_hbm, in_hbm],
-        out_specs=in_vmem,
-        scratch_shapes=[dma],
-        cost_estimate=cost(0, 1),
-        name="hold",
-    )(keep_in_hbm(left_root), cross)
-    partner_last = shifted(last_root, 0, to_partner)
     parts = pl.pallas_call(
         pick_kernel,
         out_shape=[group] * ring_x,
-        in_specs=[smem] + [in_vmem] * roles,
+        in_specs=[smem] + [in_vmem] * roles + [in_hbm],
         out_specs=[in_vmem] * ring_x,
         compiler_params=some_vmem,
         cost_estimate=cost(0, 2),
         name="pick",
-    )(place, far, same, cross, own)
+    )(place, far, same, cross, own, partner_root)
     near = [parts[0]] + [shifted(parts[d], d, still) for d in range(1, ring_x)]
     swapped = [shifted(parts[d], d, to_partner) for d in range(ring_x) if d != 2]
     swapped.insert(2, shifted(near[2], 0, to_partner))
+
+    roots, right = pl.pallas_call(
+        root_kernel,
+        out_shape=[
+            array(row_blocks, block_size, block_size),
+            array(row_blocks, block_size, half),
+        ],
+        in_specs=[smem] + [in_hbm] * 4,
+        out_specs=[in_vmem] * 2,
+        scratch_shapes=[dma((3,))],
+        compiler_params=some_vmem,
+        cost_estimate=cost(0, 4),
+        name="roots",
+    )(place, keep_in_hbm(left_root), partner_root, keep_in_hbm(right_root), near[2])
 
     blocks, payload, clip = pl.pallas_call(
         functools.partial(apply_kernel, clip_limit),
@@ -349,20 +351,12 @@
             array(owners, length, lanes),
             array(8, lanes, dtype=jnp.float32),
         ],
-        in_specs=[smem] + [in_vmem] * (2 * ring_x) + [in_hbm] * 4,
+        in_specs=[smem] + [in_vmem] * (2 * ring_x + 2),
         out_specs=[in_vmem] * 3,
-        scratch_shapes=[
-            pltpu.VMEM((row_blocks, block_size, block_size), jnp.bfloat16),
-            pltpu.VMEM((row_blocks, block_size, half), jnp.bfloat16),
-            dma((4,)),
-        ],
         compiler_params=some_vmem,
         cost_estimate=cost(3 * flops, 6),
         name="apply",
-    )(
-        place, *near, *swapped,
-        keep_in_hbm(left_root), partner_first, partner_last, keep_in_hbm(right_root),
-    )
+    )(place, *near, *swapped, roots, right)
     back = lax.all_to_all(payload, "fsdp", split_axis=0, concat_axis=0, tiled=True)
     new_left, new_right, clip = pl.pallas_call(
         stat_kernel,
@@ -379,20 +373,22 @@
         name="statistics",
     )(place, clip, blocks, keep_in_hbm(left_stat), keep_in_hbm(right_stat))
 
-    quarters = 4
+    pieces = 8
     new_momentum = pl.pallas_call(
         functools.partial(finish_kernel, row_blocks, block_size),
         out_shape=wide,
         in_specs=[smem] + [in_hbm] * 3,
         out_specs=in_hbm,
         scratch_shapes=[
-            pltpu.VMEM((owners, length, lanes), jnp.bfloat16),
+            pltpu.VMEM((owners, length - extra_rows, lanes), jnp.bfloat16),
+            pltpu.VMEM((owners, extra_rows, lanes), jnp.bfloat16),
             pltpu.VMEM((8, lanes), jnp.float32),
             pltpu.VMEM((rows_dev, all_cols), jnp.float32),
-            dma((quarters,)),
+            dma((pieces,)),
             dma,
-            dma((quarters,)),
-            dma((quarters,)),
+            dma,
+            dma((pieces,)),
+            dma((pieces,)),
         ],
         compiler_params=some_vmem,
         cost_estimate=cost(1 << 22, 4),

time: 92.5 us -> 88.9 us (0.961)
  starting transfers between devices: 28 us -> 21.6 us
  waiting for transfers between devices: 48.2 us -> 54.5 us
  Pallas kernels: 14.2 us -> 11.8 us
  local copies, waits for them, and re-layouts: 1.08 us -> 0 us
    ppermute x12 -> x11, waiting for transfers between devices: 29 us -> 35.3 us  [shifted(): return lax.ppermute(block, 'fsdp', route)]
    ppermute x12 -> x11, starting transfers between devices: 21.2 us -> 17.4 us  [shifted(): return lax.ppermute(block, 'fsdp', route)]
    all_to_all x1, starting transfers between devices: 6.79 us -> 4.15 us  [local(): lax.all_to_all(payload, 'fsdp', split_axis=0, concat_axis=0, tiled=True)]
    pallas_call x1, Pallas kernels: 3.95 us -> 2.66 us  [local(): pl.pallas_call(functools.partial(apply_kernel, clip_limit), out_shape=[ar...]
    slice x1 -> x0, local copies, waits for them, and re-layouts: 1.08 us -> none  [local(): partner_first = shifted(left_root[:early], 0, to_partner)]
  transfers between devices with their start and end apart: 13 -> 12, of which waited for: 9 -> 9; matrix products, arithmetic and copies ran while one was open for 1% -> 0% of each run, Pallas kernels for 6% -> 7%
where the time goes in v4:
time: 88.9 us; the launch traced here: 88.5 us
  waiting for transfers between devices  54.5 us (61%)
  starting transfers between devices  21.6 us (24%)
  Pallas kernels  11.8 us (13%)
    ppermute x11, waiting for transfers between devices, shifted(): return lax.ppermute(block, 'fsdp', route)  35.3 us
    all_to_all x1, waiting for transfers between devices, local(): lax.all_to_all(payload, 'fsdp', split_axis=0, concat_axis=0, tiled=True)  19.1 us
    ppermute x11, starting transfers between devices, shifted(): return lax.ppermute(block, 'fsdp', route)  17.4 us
    all_to_all x1, starting transfers between devices, local(): lax.all_to_all(payload, 'fsdp', split_axis=0, concat_axis=0, tiled=True)  4.15 us
    pallas_call x1, Pallas kernels, local(): pl.pallas_call(stat_kernel, out_shape=[stat] * 2 + [array(8, lanes, dtype...  3.75 us
    pallas_call x1, Pallas kernels, local(): pl.pallas_call(functools.partial(apply_kernel, clip_limit), out_shape=[ar...  2.66 us
    pallas_call x1, Pallas kernels, local(): pl.pallas_call(functools.partial(finish_kernel, row_blocks, block_size),...  2.49 us
  transfers between devices with their start and end apart: 12, of which 9 were waited for; matrix products, arithmetic and copies ran while one was open for 0% of the time, Pallas kernels for 7%

profile of v4, /device:TPU:8, one launch (start us, length us, event | category | flops | bytes accessed | tf_op | source)
XLA Modules:
  0.0 88.5 jit_solution(2181444316664303103)
XLA Ops:
  0.6 2.0 %collective-permute-start.3 = (bf16[3,256,512]{2,1,0:T(8,128)(2,1)}, bf16[3,256,512]{2,1,0:T(8,128)(2,1)S(1)}, u32[]{:S(2)}, u32[]{:S(2)}) collective-permute-start(bf16[3,256,512]{2,1,0:T(8,128)(2,1)} %bitcast.13), channel_id=1, source_target_pairs={{0,1},{1,0},{2,3},{3,2},{4,5},{5,4},{6,7},{7,6},{8,9},{9,8},{10,11... | collective-permute-start | bytes 2359304 | tf_op jit(solution)/shard_map/ppermute | solution.py:29
  2.6 1.4 %cut.1 = (bf16[200,512]{1,0:T(8,128)(2,1)S(1)}, bf16[200,512]{1,0:T(8,128)(2,1)S(1)}, bf16[200,512]{1,0:T(8,128)(2,1)S(1)}, bf16[200,512]{1,0:T(8,128)(2,1)S(1)}) custom-call(s32[1]{0:T(128)} %bitcast.place, bf16[48,8192]{1,0:T(8,128)(2,1)} %grad.1), custom_call_target="tpu_custom_call" | custom-call | bytes 1048576 | tf_op jit(solution)/shard_map/cut/pallas_call | solution.py:309
  4.0 5.9 %collective-permute-start = (bf16[200,512]{1,0:T(8,128)(2,1)S(1)}, bf16[200,512]{1,0:T(8,128)(2,1)S(1)}, u32[]{:S(2)}, u32[]{:S(2)}) collective-permute-start(bf16[200,512]{1,0:T(8,128)(2,1)S(1)} %get-tuple-element.19), channel_id=1, source_target_pairs={{0,5},{1,4},{2,7},{3,6},{4,1},{5,0},{6,3},{7,2},{8,13},{9,12},{10,... | collective-permute-start | bytes 614408 | tf_op jit(solution)/shard_map/ppermute | solution.py:29
  9.9 1.5 %collective-permute-start.1 = (bf16[200,512]{1,0:T(8,128)(2,1)S(1)}, bf16[200,512]{1,0:T(8,128)(2,1)S(1)}, u32[]{:S(2)}, u32[]{:S(2)}) collective-permute-start(bf16[200,512]{1,0:T(8,128)(2,1)S(1)} %get-tuple-element.20), channel_id=1, source_target_pairs={{0,2},{1,7},{2,4},{3,1},{4,6},{5,3},{6,0},{7,5},{8,10},{9,15},{10,... | collective-permute-start | bytes 614408 | tf_op jit(solution)/shard_map/ppermute | solution.py:29
  11.4 0.0 collective-permute-start.2
  11.4 8.1 %collective-permute-done.refs_0_ = bf16[200,512]{1,0:T(8,128)(2,1)S(1)} collective-permute-done((bf16[200,512]{1,0:T(8,128)(2,1)S(1)}, bf16[200,512]{1,0:T(8,128)(2,1)S(1)}, u32[]{:S(2)}, u32[]{:S(2)}) %collective-permute-start) | collective-permute-done | bytes 204832 | tf_op jit(solution)/shard_map/ppermute | solution.py:29
  19.5 14.8 %collective-permute-done.1.refs_1_ = bf16[200,512]{1,0:T(8,128)(2,1)S(1)} collective-permute-done((bf16[200,512]{1,0:T(8,128)(2,1)S(1)}, bf16[200,512]{1,0:T(8,128)(2,1)S(1)}, u32[]{:S(2)}, u32[]{:S(2)}) %collective-permute-start.1) | collective-permute-done | bytes 204832 | tf_op jit(solution)/shard_map/ppermute | solution.py:29
  34.3 0.0 collective-permute-done.2.refs_2_
  34.3 0.0 collective-permute-done.3.refs_4_.partner_root
  34.3 0.1 pick.1
  34.4 3.1 %collective-permute-start.5 = (bf16[200,512]{1,0:T(8,128)(2,1)S(1)}, bf16[200,512]{1,0:T(8,128)(2,1)S(1)}, u32[]{:S(2)}, u32[]{:S(2)}) collective-permute-start(bf16[200,512]{1,0:T(8,128)(2,1)S(1)} %get-tuple-element.25), channel_id=1, source_target_pairs={{0,16},{1,17},{2,18},{3,19},{4,20},{5,21},{6,22},{7,23},{8,24},{9,... | collective-permute-start | bytes 614408 | tf_op jit(solution)/shard_map/ppermute | solution.py:29
  37.5 0.0 collective-permute-start.7
  37.5 2.1 %collective-permute-start.8 = (bf16[200,512]{1,0:T(8,128)(2,1)S(1)}, bf16[200,512]{1,0:T(8,128)(2,1)S(1)}, u32[]{:S(2)}, u32[]{:S(2)}) collective-permute-start(bf16[200,512]{1,0:T(8,128)(2,1)S(1)} %get-tuple-element.24), channel_id=1, source_target_pairs={{0,9},{1,8},{2,11},{3,10},{4,13},{5,12},{6,15},{7,14},{8,17},{9,16... | collective-permute-start | bytes 614408 | tf_op jit(solution)/shard_map/ppermute | solution.py:29
  39.5 0.0 collective-permute-start.4
  39.5 2.7 %collective-permute-start.10 = (bf16[200,512]{1,0:T(8,128)(2,1)S(1)}, bf16[200,512]{1,0:T(8,128)(2,1)S(1)}, u32[]{:S(2)}, u32[]{:S(2)}) collective-permute-start(bf16[200,512]{1,0:T(8,128)(2,1)S(1)} %get-tuple-element.26), channel_id=1, source_target_pairs={{0,25},{1,24},{2,27},{3,26},{4,29},{5,28},{6,31},{7,30},{8,1},{9,0... | collective-permute-start | bytes 614408 | tf_op jit(solution)/shard_map/ppermute | solution.py:29
  42.2 3.2 %collective-permute-done.5.earlier.refs_2_ = bf16[200,512]{1,0:T(8,128)(2,1)S(1)} collective-permute-done((bf16[200,512]{1,0:T(8,128)(2,1)S(1)}, bf16[200,512]{1,0:T(8,128)(2,1)S(1)}, u32[]{:S(2)}, u32[]{:S(2)}) %collective-permute-start.5) | collective-permute-done | bytes 204832 | tf_op jit(solution)/shard_map/ppermute | solution.py:29
  45.4 0.0 collective-permute-start.6
  45.4 0.1 collective-permute-done.7.refs_4_
  45.5 0.2 collective-permute-start.9
  45.7 1.4 %roots.1 = (bf16[3,512,512]{2,1,0:T(8,128)(2,1)S(1)}, bf16[3,512,256]{2,1,0:T(8,128)(2,1)S(1)}) custom-call(s32[1]{0:T(128)} %bitcast.place, bf16[3,256,512]{2,1,0:T(8,128)(2,1)} %bitcast.14, bf16[3,256,512]{2,1,0:T(8,128)(2,1)S(1)} %collective-permute-done.3.refs_4_.partner_root, bf16[3,512,256]{2,1,0:T(8,128)(2,1)} %bitcast.15, ...), custom_call_target="tpu_custom_call" | custom-call | bytes 4194304 | tf_op jit(solution)/shard_map/roots/pallas_call | solution.py:333
  47.1 3.4 %collective-permute-done.8.refs_5_ = bf16[200,512]{1,0:T(8,128)(2,1)S(1)} collective-permute-done((bf16[200,512]{1,0:T(8,128)(2,1)S(1)}, bf16[200,512]{1,0:T(8,128)(2,1)S(1)}, u32[]{:S(2)}, u32[]{:S(2)}) %collective-permute-start.8) | collective-permute-done | bytes 204832 | tf_op jit(solution)/shard_map/ppermute | solution.py:29
  50.5 0.6 collective-permute-done.4.refs_1_
  51.0 3.1 %collective-permute-done.10.refs_7_ = bf16[200,512]{1,0:T(8,128)(2,1)S(1)} collective-permute-done((bf16[200,512]{1,0:T(8,128)(2,1)S(1)}, bf16[200,512]{1,0:T(8,128)(2,1)S(1)}, u32[]{:S(2)}, u32[]{:S(2)}) %collective-permute-start.10) | collective-permute-done | bytes 204832 | tf_op jit(solution)/shard_map/ppermute | solution.py:29
  54.1 0.0 collective-permute-done.6.refs_3_
  54.1 2.2 %collective-permute-done.9.refs_6_ = bf16[200,512]{1,0:T(8,128)(2,1)S(1)} collective-permute-done((bf16[200,512]{1,0:T(8,128)(2,1)S(1)}, bf16[200,512]{1,0:T(8,128)(2,1)S(1)}, u32[]{:S(2)}, u32[]{:S(2)}) %collective-permute-start.9) | collective-permute-done | bytes 204832 | tf_op jit(solution)/shard_map/ppermute | solution.py:29
  56.3 2.7 %apply.1 = (bf16[1536,512]{1,0:T(8,128)(2,1)S(1)}, bf16[32,104,128]{2,1,0:T(8,128)(2,1)}, f32[8,128]{1,0:T(8,128)S(1)}) custom-call(s32[1]{0:T(128)} %bitcast.place, bf16[200,512]{1,0:T(8,128)(2,1)S(1)} %get-tuple-element.23.refs_0_, bf16[200,512]{1,0:T(8,128)(2,1)S(1)} %collective-permute-done.4.refs_1_, ...), custom_call_target="tpu_custom_call" | custom-call | flops 1207959552 | bytes 6291456 | tf_op jit(solution)/shard_map/apply/pallas_call | solution.py:347
  59.0 4.2 %all-to-all-start = ((bf16[32,104,128]{2,1,0:T(8,128)(2,1)}), bf16[32,104,128]{2,1,0:T(8,128)(2,1)S(1)}, u32[]{:S(2)}, u32[]{:S(2)}) async-start(bf16[32,104,128]{2,1,0:T(8,128)(2,1)} %get-tuple-element.29), calls=%async_computation | async-start | bytes 1703936 | tf_op jit(solution)/shard_map/all_to_all | solution.py:360
  63.1 3.8 %statistics.1 = (f32[3,256,512]{2,1,0:T(8,128)}, f32[3,256,512]{2,1,0:T(8,128)}, f32[8,128]{1,0:T(8,128)S(1)}) custom-call(s32[1]{0:T(128)} %bitcast.place, f32[8,128]{1,0:T(8,128)S(1)} %get-tuple-element.30.clip, bf16[1536,512]{1,0:T(8,128)(2,1)S(1)} %get-tuple-element.31.blocks, f32[3,256,512]{2,1,0:T(8,128)} %bitcast.11, f32[3,256,512]{2,1,0:T(8,128)} %bitcast.12), custom_call_target="tpu_custom_call" | custom-call | flops 805306368 | bytes 8388608 | tf_op jit(solution)/shard_map/statistics/pallas_call | solution.py:361
  66.9 19.1 %all-to-all-done.back = bf16[32,104,128]{2,1,0:T(8,128)(2,1)S(1)} async-done(((bf16[32,104,128]{2,1,0:T(8,128)(2,1)}), bf16[32,104,128]{2,1,0:T(8,128)(2,1)S(1)}, u32[]{:S(2)}, u32[]{:S(2)}) %all-to-all-start) | async-done | bytes 852000 | tf_op jit(solution)/shard_map/all_to_all | solution.py:360
  86.0 2.5 %finish.1 = f32[48,8192]{1,0:T(8,128)} custom-call(s32[1]{0:T(128)} %bitcast.place, bf16[32,104,128]{2,1,0:T(8,128)(2,1)S(1)} %all-to-all-done.back, f32[8,128]{1,0:T(8,128)S(1)} %get-tuple-element.32.clip, f32[48,8192]{1,0:T(8,128)} %momentum.1), custom_call_target="tpu_custom_call" | custom-call | flops 4194304 | bytes 4194304 | tf_op jit(solution)/shard_map/finish/pallas_call | solution.py:377
Async XLA Ops:
  0.6 33.7 %collective-permute-start.3 = (bf16[3,256,512]{2,1,0:T(8,128)(2,1)}, bf16[3,256,512]{2,1,0:T(8,128)(2,1)S(1)}, u32[]{:S(2)}, u32[]{:S(2)}) collective-permute-start(bf16[3,256,512]{2,1,0:T(8,128)(2,1)} %bitcast.13), channel_id=1, source_target_pairs={{0,1},{1,0},{2,3},{3,2},{4,5},{5,4},{6,7},{7,6},{8,9},{9,8},{10,11... | collective-permute-start | bytes 2359304 | tf_op jit(solution)/shard_map/ppermute | solution.py:29
  4.0 15.5 %collective-permute-start = (bf16[200,512]{1,0:T(8,128)(2,1)S(1)}, bf16[200,512]{1,0:T(8,128)(2,1)S(1)}, u32[]{:S(2)}, u32[]{:S(2)}) collective-permute-start(bf16[200,512]{1,0:T(8,128)(2,1)S(1)} %get-tuple-element.19), channel_id=1, source_target_pairs={{0,5},{1,4},{2,7},{3,6},{4,1},{5,0},{6,3},{7,2},{8,13},{9,12},{10,... | collective-permute-start | bytes 614408 | tf_op jit(solution)/shard_map/ppermute | solution.py:29
  9.9 24.3 %collective-permute-start.1 = (bf16[200,512]{1,0:T(8,128)(2,1)S(1)}, bf16[200,512]{1,0:T(8,128)(2,1)S(1)}, u32[]{:S(2)}, u32[]{:S(2)}) collective-permute-start(bf16[200,512]{1,0:T(8,128)(2,1)S(1)} %get-tuple-element.20), channel_id=1, source_target_pairs={{0,2},{1,7},{2,4},{3,1},{4,6},{5,3},{6,0},{7,5},{8,10},{9,15},{10,... | collective-permute-start | bytes 614408 | tf_op jit(solution)/shard_map/ppermute | solution.py:29
  11.4 22.9 %collective-permute-start.2 = (bf16[200,512]{1,0:T(8,128)(2,1)S(1)}, bf16[200,512]{1,0:T(8,128)(2,1)S(1)}, u32[]{:S(2)}, u32[]{:S(2)}) collective-permute-start(bf16[200,512]{1,0:T(8,128)(2,1)S(1)} %get-tuple-element.21), channel_id=1, source_target_pairs={{0,7},{1,2},{2,1},{3,4},{4,3},{5,6},{6,5},{7,0},{8,15},{9,10},{10,... | collective-permute-start | bytes 614408 | tf_op jit(solution)/shard_map/ppermute | solution.py:29
  34.4 11.1 %collective-permute-start.5 = (bf16[200,512]{1,0:T(8,128)(2,1)S(1)}, bf16[200,512]{1,0:T(8,128)(2,1)S(1)}, u32[]{:S(2)}, u32[]{:S(2)}) collective-permute-start(bf16[200,512]{1,0:T(8,128)(2,1)S(1)} %get-tuple-element.25), channel_id=1, source_target_pairs={{0,16},{1,17},{2,18},{3,19},{4,20},{5,21},{6,22},{7,23},{8,24},{9,... | collective-permute-start | bytes 614408 | tf_op jit(solution)/shard_map/ppermute | solution.py:29
  37.5 8.0 %collective-permute-start.7 = (bf16[200,512]{1,0:T(8,128)(2,1)S(1)}, bf16[200,512]{1,0:T(8,128)(2,1)S(1)}, u32[]{:S(2)}, u32[]{:S(2)}) collective-permute-start(bf16[200,512]{1,0:T(8,128)(2,1)S(1)} %get-tuple-element.23.refs_0_), channel_id=1, source_target_pairs={{0,1},{1,0},{2,3},{3,2},{4,5},{5,4},{6,7},{7,6},{8,9},{9,8},{10,11... | collective-permute-start | bytes 614408 | tf_op jit(solution)/shard_map/ppermute | solution.py:29
  37.5 13.0 %collective-permute-start.8 = (bf16[200,512]{1,0:T(8,128)(2,1)S(1)}, bf16[200,512]{1,0:T(8,128)(2,1)S(1)}, u32[]{:S(2)}, u32[]{:S(2)}) collective-permute-start(bf16[200,512]{1,0:T(8,128)(2,1)S(1)} %get-tuple-element.24), channel_id=1, source_target_pairs={{0,9},{1,8},{2,11},{3,10},{4,13},{5,12},{6,15},{7,14},{8,17},{9,16... | collective-permute-start | bytes 614408 | tf_op jit(solution)/shard_map/ppermute | solution.py:29
  39.5 11.5 %collective-permute-start.4 = (bf16[200,512]{1,0:T(8,128)(2,1)S(1)}, bf16[200,512]{1,0:T(8,128)(2,1)S(1)}, u32[]{:S(2)}, u32[]{:S(2)}) collective-permute-start(bf16[200,512]{1,0:T(8,128)(2,1)S(1)} %get-tuple-element.24), channel_id=1, source_target_pairs={{0,8},{1,9},{2,10},{3,11},{4,12},{5,13},{6,14},{7,15},{8,16},{9,17... | collective-permute-start | bytes 614408 | tf_op jit(solution)/shard_map/ppermute | solution.py:29
  39.5 14.6 %collective-permute-start.10 = (bf16[200,512]{1,0:T(8,128)(2,1)S(1)}, bf16[200,512]{1,0:T(8,128)(2,1)S(1)}, u32[]{:S(2)}, u32[]{:S(2)}) collective-permute-start(bf16[200,512]{1,0:T(8,128)(2,1)S(1)} %get-tuple-element.26), channel_id=1, source_target_pairs={{0,25},{1,24},{2,27},{3,26},{4,29},{5,28},{6,31},{7,30},{8,1},{9,0... | collective-permute-start | bytes 614408 | tf_op jit(solution)/shard_map/ppermute | solution.py:29
  45.4 8.7 %collective-permute-start.6 = (bf16[200,512]{1,0:T(8,128)(2,1)S(1)}, bf16[200,512]{1,0:T(8,128)(2,1)S(1)}, u32[]{:S(2)}, u32[]{:S(2)}) collective-permute-start(bf16[200,512]{1,0:T(8,128)(2,1)S(1)} %get-tuple-element.26), channel_id=1, source_target_pairs={{0,24},{1,25},{2,26},{3,27},{4,28},{5,29},{6,30},{7,31},{8,0},{9,1... | collective-permute-start | bytes 614408 | tf_op jit(solution)/shard_map/ppermute | solution.py:29
  45.5 10.8 %collective-permute-start.9 = (bf16[200,512]{1,0:T(8,128)(2,1)S(1)}, bf16[200,512]{1,0:T(8,128)(2,1)S(1)}, u32[]{:S(2)}, u32[]{:S(2)}) collective-permute-start(bf16[200,512]{1,0:T(8,128)(2,1)S(1)} %collective-permute-done.5.earlier.refs_2_), channel_id=1, source_target_pairs={{0,1},{1,0},{2,3},{3,2},{4,5},{5,4},{6,7},{7,6},{8,9},{9,8},{10,11... | collective-permute-start | bytes 614408 | tf_op jit(solution)/shard_map/ppermute | solution.py:29
  59.0 27.1 %all-to-all-start = ((bf16[32,104,128]{2,1,0:T(8,128)(2,1)}), bf16[32,104,128]{2,1,0:T(8,128)(2,1)S(1)}, u32[]{:S(2)}, u32[]{:S(2)}) async-start(bf16[32,104,128]{2,1,0:T(8,128)(2,1)} %get-tuple-element.29), calls=%async_computation | async-start | bytes 1703936 | tf_op jit(solution)/shard_map/all_to_all | solution.py:360

commit v5 on v4

--- a/solution.py
+++ b/solution.py
@@ -56,8 +56,10 @@
     return jnp.sum(wide, axis=0, keepdims=True)
 
 
-def cut_kernel(place, grad, *rest):
-    outs, sem = rest[:-1], rest[-1]
+def cut_kernel(place, grad, left_root, *rest):
+    outs, early_root, sem, root_sem = rest[:-3], rest[-3], rest[-2], rest[-1]
+    early = pl.ds(0, early_root.shape[0])
+    get_root = pltpu.make_async_copy(left_root.at[early], early_root, root_sem)
     pair, parity = place[0] % ring_z // 2, place[0] % 2
     rows_dev = grad.shape[0]
     width = outs[0].shape[1]
@@ -70,6 +72,7 @@
             rows = pl.ds(x * rows_dev, rows_dev)
             copies.append(pltpu.make_async_copy(grad.at[:, at], out.at[rows], sem.at[len(copies)]))
             copies[-1].start()
+    get_root.start()
     square = jnp.zeros((8, width), jnp.float32)
     for i, copy in enumerate(copies):
         copy.wait()
@@ -80,10 +83,13 @@
     parts = in_parts(jnp.broadcast_to(scalar_sum(square), (1, width)))
     for out in outs:
         out[body : body + extra_rows, :] = parts
+    get_root.wait()
 
 
 def pick_kernel(place, *refs):
-    groups, outs = refs[:roles], refs[roles + 1 :]
+    groups, last_root, outs = refs[:roles], refs[roles], refs[roles + 2 :]
+    half = last_root.shape[0]
+    outs[0][outs[0].shape[0] - half :, :] = last_root[...]
     x = place[0] // ring_z
     body = groups[0].shape[0] - extra_rows
     rows_dev = body // ring_x
@@ -96,14 +102,19 @@
         out[body : body + extra_rows, :] = parts
 
 
-def root_kernel(place, own_root, partner_root, right_root, earlier, roots, right, sem):
-    half = own_root.shape[1]
+def root_kernel(
+    place, own_root, partner_early, message, right_root, earlier, roots, right, sem
+):
+    row_blocks, half, _ = own_root.shape
+    early = row_blocks - 1
+    partner_last = message.at[pl.ds(message.shape[0] - half, half)]
     parity = place[0] % 2
     own_rows, partner_rows = (pl.ds(aligned(side, half), half) for side in (parity, 1 - parity))
     bring = [
         pltpu.make_async_copy(own_root, roots.at[:, own_rows], sem.at[0]),
-        pltpu.make_async_copy(partner_root, roots.at[:, partner_rows], sem.at[1]),
-        pltpu.make_async_copy(right_root, right, sem.at[2]),
+        pltpu.make_async_copy(partner_early, roots.at[pl.ds(0, early), partner_rows], sem.at[1]),
+        pltpu.make_async_copy(partner_last, roots.at[early, partner_rows], sem.at[2]),
+        pltpu.make_async_copy(right_root, right, sem.at[3]),
     ]
     for copy in bring:
         copy.start()
@@ -120,7 +131,7 @@
     row_blocks, block_size, half = right_v.shape
     owners, length, _ = payload.shape
     body = length - extra_rows
-    group_body = groups[0].shape[0] - extra_rows
+    group_body = groups[1].shape[0] - extra_rows
     rows_dev = group_body // roles
 
     for i, origin in enumerate(origins):
@@ -302,30 +313,31 @@
     group = array(ring_x * rows_dev + extra_rows, block_size)
     stat = array(row_blocks, half, block_size, dtype=jnp.float32)
     wide = array(rows_dev, all_cols, dtype=jnp.float32)
+    message_rows = -(-group.shape[0] // 16) * 16 + half
     still = lambda z: 0
     to_partner = outward(-1)
 
-    partner_root = shifted(left_root, 0, to_partner)
-    *sent, own = pl.pallas_call(
+    *sent, own, early_root = pl.pallas_call(
         cut_kernel,
-        out_shape=[group] * roles,
-        in_specs=[smem, in_hbm],
-        out_specs=[in_vmem] * roles,
-        scratch_shapes=[dma((roles * ring_x,))],
+        out_shape=[group] * roles + [array(row_blocks - 1, half, block_size)],
+        in_specs=[smem, in_hbm, in_hbm],
+        out_specs=[in_vmem] * (roles + 1),
+        scratch_shapes=[dma((roles * ring_x,)), dma],
         compiler_params=some_vmem,
         cost_estimate=cost(0, 1),
         name="cut",
-    )(place, keep_in_hbm(grad))
+    )(place, keep_in_hbm(grad), keep_in_hbm(left_root))
+    partner_early = shifted(early_root, 0, to_partner)
     far, same, cross = (shifted(block, 0, outward(n)) for block, n in zip(sent, (3, -2, 1)))
     parts = pl.pallas_call(
         pick_kernel,
-        out_shape=[group] * ring_x,
-        in_specs=[smem] + [in_vmem] * roles + [in_hbm],
+        out_shape=[array(message_rows, block_size)] + [group] * (ring_x - 1),
+        in_specs=[smem] + [in_vmem] * (roles + 1) + [in_hbm],
         out_specs=[in_vmem] * ring_x,
         compiler_params=some_vmem,
         cost_estimate=cost(0, 2),
         name="pick",
-    )(place, far, same, cross, own, partner_root)
+    )(place, far, same, cross, own, left_root[row_blocks - 1], partner_early)
     near = [parts[0]] + [shifted(parts[d], d, still) for d in range(1, ring_x)]
     swapped = [shifted(parts[d], d, to_partner) for d in range(ring_x) if d != 2]
     swapped.insert(2, shifted(near[2], 0, to_partner))
@@ -336,13 +348,15 @@
             array(row_blocks, block_size, block_size),
             array(row_blocks, block_size, half),
         ],
-        in_specs=[smem] + [in_hbm] * 4,
+        in_specs=[smem] + [in_hbm] * 5,
         out_specs=[in_vmem] * 2,
-        scratch_shapes=[dma((3,))],
+        scratch_shapes=[dma((4,))],
         compiler_params=some_vmem,
         cost_estimate=cost(0, 4),
         name="roots",
-    )(place, keep_in_hbm(left_root), partner_root, keep_in_hbm(right_root), near[2])
+    )(
+        place, keep_in_hbm(left_root), partner_early, swapped[0], keep_in_hbm(right_root), near[2]
+    )
 
     blocks, payload, clip = pl.pallas_call(
         functools.partial(apply_kernel, clip_limit),

time: 88.9 us -> 90.2 us (1.015)
  starting transfers between devices: 21.6 us -> 25.4 us
  waiting for transfers between devices: 54.5 us -> 50.7 us
  local copies, waits for them, and re-layouts: 0 us -> 0.97 us
    ppermute x11, waiting for transfers between devices: 35.3 us -> 31.5 us  [shifted(): return lax.ppermute(block, 'fsdp', route)]
    ppermute x11, starting transfers between devices: 17.4 us -> 19.5 us  [shifted(): return lax.ppermute(block, 'fsdp', route)]
    all_to_all x1, starting transfers between devices: 4.15 us -> 5.86 us  [local(): lax.all_to_all(payload, 'fsdp', split_axis=0, concat_axis=0, tiled=True)]
    squeeze x0 -> x1, local copies, waits for them, and re-layouts: none -> 0.97 us  [local(): left_root[row_blocks - 1]]
  transfers between devices with their start and end apart: 12 -> 12, of which waited for: 9 -> 8; matrix products, arithmetic and copies ran while one was open for 0% -> 1% of each run, Pallas kernels for 7% -> 6%
where the time goes in v5:
time: 90.2 us; the launch traced here: 89.7 us
  waiting for transfers between devices  50.7 us (56%)
  starting transfers between devices  25.4 us (28%)
  Pallas kernels  12 us (13%)
  local copies, waits for them, and re-layouts  0.97 us (1%)
    ppermute x11, waiting for transfers between devices, shifted(): return lax.ppermute(block, 'fsdp', route)  31.5 us
    ppermute x11, starting transfers between devices, shifted(): return lax.ppermute(block, 'fsdp', route)  19.5 us
    all_to_all x1, waiting for transfers between devices, local(): lax.all_to_all(payload, 'fsdp', split_axis=0, concat_axis=0, tiled=True)  19.2 us
    all_to_all x1, starting transfers between devices, local(): lax.all_to_all(payload, 'fsdp', split_axis=0, concat_axis=0, tiled=True)  5.86 us
    pallas_call x1, Pallas kernels, local(): pl.pallas_call(stat_kernel, out_shape=[stat] * 2 + [array(8, lanes, dtype...  3.75 us
    pallas_call x1, Pallas kernels, local(): pl.pallas_call(functools.partial(apply_kernel, clip_limit), out_shape=[ar...  2.65 us
    pallas_call x1, Pallas kernels, local(): pl.pallas_call(functools.partial(finish_kernel, row_blocks, block_size),...  2.49 us
  transfers between devices with their start and end apart: 12, of which 8 were waited for; matrix products, arithmetic and copies ran while one was open for 1% of the time, Pallas kernels for 6%

profile of v5, /device:TPU:8, one launch (start us, length us, event | category | flops | bytes accessed | tf_op | source)
XLA Modules:
  0.0 89.7 jit_solution(9590903760275585796)
XLA Ops:
  0.6 1.6 %cut.1 = (bf16[200,512]{1,0:T(8,128)(2,1)S(1)}, bf16[200,512]{1,0:T(8,128)(2,1)S(1)}, bf16[200,512]{1,0:T(8,128)(2,1)S(1)}, bf16[200,512]{1,0:T(8,128)(2,1)S(1)}, bf16[2,256,512]{2,1,0:T(8,128)(2,1)S(1)}) custom-call(s32[1]{0:T(128)} %bitcast.place, bf16[48,8192]{1,0:T(8,128)(2,1)} %grad.1, bf16[3,256,512]{2,1,0:T(8,128)(2,1)} %bitcast.13), custom_call_target="tpu_custom_call" | custom-call | bytes 1048576 | tf_op jit(solution)/shard_map/cut/pallas_call | solution.py:320
  2.2 2.0 %collective-permute-start.3 = (bf16[2,256,512]{2,1,0:T(8,128)(2,1)S(1)}, bf16[2,256,512]{2,1,0:T(8,128)(2,1)S(1)}, u32[]{:S(2)}, u32[]{:S(2)}) collective-permute-start(bf16[2,256,512]{2,1,0:T(8,128)(2,1)S(1)} %get-tuple-element.24), channel_id=1, source_target_pairs={{0,1},{1,0},{2,3},{3,2},{4,5},{5,4},{6,7},{7,6},{8,9},{9,8},{10,11... | collective-permute-start | bytes 1572872 | tf_op jit(solution)/shard_map/ppermute | solution.py:29
  4.2 5.8 %collective-permute-start = (bf16[200,512]{1,0:T(8,128)(2,1)S(1)}, bf16[200,512]{1,0:T(8,128)(2,1)S(1)}, u32[]{:S(2)}, u32[]{:S(2)}) collective-permute-start(bf16[200,512]{1,0:T(8,128)(2,1)S(1)} %get-tuple-element.20), channel_id=1, source_target_pairs={{0,5},{1,4},{2,7},{3,6},{4,1},{5,0},{6,3},{7,2},{8,13},{9,12},{10,... | collective-permute-start | bytes 614408 | tf_op jit(solution)/shard_map/ppermute | solution.py:29
  10.1 1.5 %collective-permute-start.1 = (bf16[200,512]{1,0:T(8,128)(2,1)S(1)}, bf16[200,512]{1,0:T(8,128)(2,1)S(1)}, u32[]{:S(2)}, u32[]{:S(2)}) collective-permute-start(bf16[200,512]{1,0:T(8,128)(2,1)S(1)} %get-tuple-element.21), channel_id=1, source_target_pairs={{0,2},{1,7},{2,4},{3,1},{4,6},{5,3},{6,0},{7,5},{8,10},{9,15},{10,... | collective-permute-start | bytes 614408 | tf_op jit(solution)/shard_map/ppermute | solution.py:29
  11.5 0.0 collective-permute-start.2
  11.5 1.0 %slice_bitcast_fusion.refs_4_ = bf16[256,512]{1,0:T(8,128)(2,1)S(1)} fusion(bf16[3,1,256,512]{3,2,1,0:T(8,128)(2,1)} %param.10), kind=kLoop, calls=%fused_computation | loop fusion | bytes 524288 | tf_op jit(solution)/shard_map/squeeze | solution.py:340
  12.5 11.7 %collective-permute-done.refs_0_ = bf16[200,512]{1,0:T(8,128)(2,1)S(1)} collective-permute-done((bf16[200,512]{1,0:T(8,128)(2,1)S(1)}, bf16[200,512]{1,0:T(8,128)(2,1)S(1)}, u32[]{:S(2)}, u32[]{:S(2)}) %collective-permute-start) | collective-permute-done | bytes 204832 | tf_op jit(solution)/shard_map/ppermute | solution.py:29
  24.2 5.9 %collective-permute-done.1.refs_1_ = bf16[200,512]{1,0:T(8,128)(2,1)S(1)} collective-permute-done((bf16[200,512]{1,0:T(8,128)(2,1)S(1)}, bf16[200,512]{1,0:T(8,128)(2,1)S(1)}, u32[]{:S(2)}, u32[]{:S(2)}) %collective-permute-start.1) | collective-permute-done | bytes 204832 | tf_op jit(solution)/shard_map/ppermute | solution.py:29
  30.0 0.0 collective-permute-done.2.refs_2_
  30.0 0.0 collective-permute-done.3.refs_5_.partner_early
  30.1 0.1 pick.1
  30.1 0.1 collective-permute-start.7
  30.2 3.1 %collective-permute-start.5 = (bf16[200,512]{1,0:T(8,128)(2,1)S(1)}, bf16[200,512]{1,0:T(8,128)(2,1)S(1)}, u32[]{:S(2)}, u32[]{:S(2)}) collective-permute-start(bf16[200,512]{1,0:T(8,128)(2,1)S(1)} %get-tuple-element.27), channel_id=1, source_target_pairs={{0,16},{1,17},{2,18},{3,19},{4,20},{5,21},{6,22},{7,23},{8,24},{9,... | collective-permute-start | bytes 614408 | tf_op jit(solution)/shard_map/ppermute | solution.py:29
  33.3 2.0 %collective-permute-start.8 = (bf16[200,512]{1,0:T(8,128)(2,1)S(1)}, bf16[200,512]{1,0:T(8,128)(2,1)S(1)}, u32[]{:S(2)}, u32[]{:S(2)}) collective-permute-start(bf16[200,512]{1,0:T(8,128)(2,1)S(1)} %get-tuple-element.26), channel_id=1, source_target_pairs={{0,9},{1,8},{2,11},{3,10},{4,13},{5,12},{6,15},{7,14},{8,17},{9,16... | collective-permute-start | bytes 614408 | tf_op jit(solution)/shard_map/ppermute | solution.py:29
  35.3 0.0 collective-permute-start.4
  35.3 2.8 %collective-permute-start.10 = (bf16[200,512]{1,0:T(8,128)(2,1)S(1)}, bf16[200,512]{1,0:T(8,128)(2,1)S(1)}, u32[]{:S(2)}, u32[]{:S(2)}) collective-permute-start(bf16[200,512]{1,0:T(8,128)(2,1)S(1)} %get-tuple-element.28), channel_id=1, source_target_pairs={{0,25},{1,24},{2,27},{3,26},{4,29},{5,28},{6,31},{7,30},{8,1},{9,0... | collective-permute-start | bytes 614408 | tf_op jit(solution)/shard_map/ppermute | solution.py:29
  38.1 0.8 collective-permute-done.5.earlier.refs_2_
  38.9 2.3 %collective-permute-start.6 = (bf16[200,512]{1,0:T(8,128)(2,1)S(1)}, bf16[200,512]{1,0:T(8,128)(2,1)S(1)}, u32[]{:S(2)}, u32[]{:S(2)}) collective-permute-start(bf16[200,512]{1,0:T(8,128)(2,1)S(1)} %get-tuple-element.28), channel_id=1, source_target_pairs={{0,24},{1,25},{2,26},{3,27},{4,28},{5,29},{6,30},{7,31},{8,0},{9,1... | collective-permute-start | bytes 614408 | tf_op jit(solution)/shard_map/ppermute | solution.py:29
  41.1 2.9 %collective-permute-done.7.message.refs_4_ = bf16[464,512]{1,0:T(8,128)(2,1)S(1)} collective-permute-done((bf16[464,512]{1,0:T(8,128)(2,1)S(1)}, bf16[464,512]{1,0:T(8,128)(2,1)S(1)}, u32[]{:S(2)}, u32[]{:S(2)}) %collective-permute-start.7) | collective-permute-done | bytes 475168 | tf_op jit(solution)/shard_map/ppermute | solution.py:29
  44.0 0.0 collective-permute-start.9
  44.0 1.4 %roots.1 = (bf16[3,512,512]{2,1,0:T(8,128)(2,1)S(1)}, bf16[3,512,256]{2,1,0:T(8,128)(2,1)S(1)}) custom-call(s32[1]{0:T(128)} %bitcast.place, bf16[3,256,512]{2,1,0:T(8,128)(2,1)} %bitcast.14, bf16[2,256,512]{2,1,0:T(8,128)(2,1)S(1)} %collective-permute-done.3.refs_5_.partner_early, bf16[464,512]{1,0:T(8,128)(2,1)S(1)} %collective-permute-done.7.message.refs_4_, ...), custom_call_target="tpu_custom_call" | custom-call | bytes 4194304 | tf_op jit(solution)/shard_map/roots/pallas_call | solution.py:345
  45.4 5.2 %collective-permute-done.8.refs_5_ = bf16[200,512]{1,0:T(8,128)(2,1)S(1)} collective-permute-done((bf16[200,512]{1,0:T(8,128)(2,1)S(1)}, bf16[200,512]{1,0:T(8,128)(2,1)S(1)}, u32[]{:S(2)}, u32[]{:S(2)}) %collective-permute-start.8) | collective-permute-done | bytes 204832 | tf_op jit(solution)/shard_map/ppermute | solution.py:29
  50.6 0.0 collective-permute-done.4.refs_1_
  50.6 3.2 %collective-permute-done.10.refs_7_ = bf16[200,512]{1,0:T(8,128)(2,1)S(1)} collective-permute-done((bf16[200,512]{1,0:T(8,128)(2,1)S(1)}, bf16[200,512]{1,0:T(8,128)(2,1)S(1)}, u32[]{:S(2)}, u32[]{:S(2)}) %collective-permute-start.10) | collective-permute-done | bytes 204832 | tf_op jit(solution)/shard_map/ppermute | solution.py:29
  53.8 0.0 collective-permute-done.6.refs_3_
  53.8 2.0 %collective-permute-done.9.refs_6_ = bf16[200,512]{1,0:T(8,128)(2,1)S(1)} collective-permute-done((bf16[200,512]{1,0:T(8,128)(2,1)S(1)}, bf16[200,512]{1,0:T(8,128)(2,1)S(1)}, u32[]{:S(2)}, u32[]{:S(2)}) %collective-permute-start.9) | collective-permute-done | bytes 204832 | tf_op jit(solution)/shard_map/ppermute | solution.py:29
  55.8 2.6 %apply.1 = (bf16[1536,512]{1,0:T(8,128)(2,1)S(1)}, bf16[32,104,128]{2,1,0:T(8,128)(2,1)}, f32[8,128]{1,0:T(8,128)S(1)}) custom-call(s32[1]{0:T(128)} %bitcast.place, bf16[464,512]{1,0:T(8,128)(2,1)S(1)} %get-tuple-element.25.refs_0_, bf16[200,512]{1,0:T(8,128)(2,1)S(1)} %collective-permute-done.4.refs_1_, ...), custom_call_target="tpu_custom_call" | custom-call | flops 1207959552 | bytes 6291456 | tf_op jit(solution)/shard_map/apply/pallas_call | solution.py:361
  58.4 5.9 %all-to-all-start = ((bf16[32,104,128]{2,1,0:T(8,128)(2,1)}), bf16[32,104,128]{2,1,0:T(8,128)(2,1)S(1)}, u32[]{:S(2)}, u32[]{:S(2)}) async-start(bf16[32,104,128]{2,1,0:T(8,128)(2,1)} %get-tuple-element.31), calls=%async_computation | async-start | bytes 1703936 | tf_op jit(solution)/shard_map/all_to_all | solution.py:374
  64.3 3.8 %statistics.1 = (f32[3,256,512]{2,1,0:T(8,128)}, f32[3,256,512]{2,1,0:T(8,128)}, f32[8,128]{1,0:T(8,128)S(1)}) custom-call(s32[1]{0:T(128)} %bitcast.place, f32[8,128]{1,0:T(8,128)S(1)} %get-tuple-element.32.clip, bf16[1536,512]{1,0:T(8,128)(2,1)S(1)} %get-tuple-element.33.blocks, f32[3,256,512]{2,1,0:T(8,128)} %bitcast.15, f32[3,256,512]{2,1,0:T(8,128)} %bitcast.16), custom_call_target="tpu_custom_call" | custom-call | flops 805306368 | bytes 8388608 | tf_op jit(solution)/shard_map/statistics/pallas_call | solution.py:375
  68.0 19.2 %all-to-all-done.back = bf16[32,104,128]{2,1,0:T(8,128)(2,1)S(1)} async-done(((bf16[32,104,128]{2,1,0:T(8,128)(2,1)}), bf16[32,104,128]{2,1,0:T(8,128)(2,1)S(1)}, u32[]{:S(2)}, u32[]{:S(2)}) %all-to-all-start) | async-done | bytes 852000 | tf_op jit(solution)/shard_map/all_to_all | solution.py:374
  87.2 2.5 %finish.1 = f32[48,8192]{1,0:T(8,128)} custom-call(s32[1]{0:T(128)} %bitcast.place, bf16[32,104,128]{2,1,0:T(8,128)(2,1)S(1)} %all-to-all-done.back, f32[8,128]{1,0:T(8,128)S(1)} %get-tuple-element.34.clip, f32[48,8192]{1,0:T(8,128)} %momentum.1), custom_call_target="tpu_custom_call" | custom-call | flops 4194304 | bytes 4194304 | tf_op jit(solution)/shard_map/finish/pallas_call | solution.py:391
Async XLA Ops:
  2.2 27.8 %collective-permute-start.3 = (bf16[2,256,512]{2,1,0:T(8,128)(2,1)S(1)}, bf16[2,256,512]{2,1,0:T(8,128)(2,1)S(1)}, u32[]{:S(2)}, u32[]{:S(2)}) collective-permute-start(bf16[2,256,512]{2,1,0:T(8,128)(2,1)S(1)} %get-tuple-element.24), channel_id=1, source_target_pairs={{0,1},{1,0},{2,3},{3,2},{4,5},{5,4},{6,7},{7,6},{8,9},{9,8},{10,11... | collective-permute-start | bytes 1572872 | tf_op jit(solution)/shard_map/ppermute | solution.py:29
  4.2 19.9 %collective-permute-start = (bf16[200,512]{1,0:T(8,128)(2,1)S(1)}, bf16[200,512]{1,0:T(8,128)(2,1)S(1)}, u32[]{:S(2)}, u32[]{:S(2)}) collective-permute-start(bf16[200,512]{1,0:T(8,128)(2,1)S(1)} %get-tuple-element.20), channel_id=1, source_target_pairs={{0,5},{1,4},{2,7},{3,6},{4,1},{5,0},{6,3},{7,2},{8,13},{9,12},{10,... | collective-permute-start | bytes 614408 | tf_op jit(solution)/shard_map/ppermute | solution.py:29
  10.1 20.0 %collective-permute-start.1 = (bf16[200,512]{1,0:T(8,128)(2,1)S(1)}, bf16[200,512]{1,0:T(8,128)(2,1)S(1)}, u32[]{:S(2)}, u32[]{:S(2)}) collective-permute-start(bf16[200,512]{1,0:T(8,128)(2,1)S(1)} %get-tuple-element.21), channel_id=1, source_target_pairs={{0,2},{1,7},{2,4},{3,1},{4,6},{5,3},{6,0},{7,5},{8,10},{9,15},{10,... | collective-permute-start | bytes 614408 | tf_op jit(solution)/shard_map/ppermute | solution.py:29
  11.5 18.5 %collective-permute-start.2 = (bf16[200,512]{1,0:T(8,128)(2,1)S(1)}, bf16[200,512]{1,0:T(8,128)(2,1)S(1)}, u32[]{:S(2)}, u32[]{:S(2)}) collective-permute-start(bf16[200,512]{1,0:T(8,128)(2,1)S(1)} %get-tuple-element.22), channel_id=1, source_target_pairs={{0,7},{1,2},{2,1},{3,4},{4,3},{5,6},{6,5},{7,0},{8,15},{9,10},{10,... | collective-permute-start | bytes 614408 | tf_op jit(solution)/shard_map/ppermute | solution.py:29
  30.1 13.9 %collective-permute-start.7 = (bf16[464,512]{1,0:T(8,128)(2,1)S(1)}, bf16[464,512]{1,0:T(8,128)(2,1)S(1)}, u32[]{:S(2)}, u32[]{:S(2)}) collective-permute-start(bf16[464,512]{1,0:T(8,128)(2,1)S(1)} %get-tuple-element.25.refs_0_), channel_id=1, source_target_pairs={{0,1},{1,0},{2,3},{3,2},{4,5},{5,4},{6,7},{7,6},{8,9},{9,8},{10,11... | collective-permute-start | bytes 1425416 | tf_op jit(solution)/shard_map/ppermute | solution.py:29
  30.2 8.6 %collective-permute-start.5 = (bf16[200,512]{1,0:T(8,128)(2,1)S(1)}, bf16[200,512]{1,0:T(8,128)(2,1)S(1)}, u32[]{:S(2)}, u32[]{:S(2)}) collective-permute-start(bf16[200,512]{1,0:T(8,128)(2,1)S(1)} %get-tuple-element.27), channel_id=1, source_target_pairs={{0,16},{1,17},{2,18},{3,19},{4,20},{5,21},{6,22},{7,23},{8,24},{9,... | collective-permute-start | bytes 614408 | tf_op jit(solution)/shard_map/ppermute | solution.py:29
  33.3 17.3 %collective-permute-start.8 = (bf16[200,512]{1,0:T(8,128)(2,1)S(1)}, bf16[200,512]{1,0:T(8,128)(2,1)S(1)}, u32[]{:S(2)}, u32[]{:S(2)}) collective-permute-start(bf16[200,512]{1,0:T(8,128)(2,1)S(1)} %get-tuple-element.26), channel_id=1, source_target_pairs={{0,9},{1,8},{2,11},{3,10},{4,13},{5,12},{6,15},{7,14},{8,17},{9,16... | collective-permute-start | bytes 614408 | tf_op jit(solution)/shard_map/ppermute | solution.py:29
  35.3 15.3 %collective-permute-start.4 = (bf16[200,512]{1,0:T(8,128)(2,1)S(1)}, bf16[200,512]{1,0:T(8,128)(2,1)S(1)}, u32[]{:S(2)}, u32[]{:S(2)}) collective-permute-start(bf16[200,512]{1,0:T(8,128)(2,1)S(1)} %get-tuple-element.26), channel_id=1, source_target_pairs={{0,8},{1,9},{2,10},{3,11},{4,12},{5,13},{6,14},{7,15},{8,16},{9,17... | collective-permute-start | bytes 614408 | tf_op jit(solution)/shard_map/ppermute | solution.py:29
  35.3 18.5 %collective-permute-start.10 = (bf16[200,512]{1,0:T(8,128)(2,1)S(1)}, bf16[200,512]{1,0:T(8,128)(2,1)S(1)}, u32[]{:S(2)}, u32[]{:S(2)}) collective-permute-start(bf16[200,512]{1,0:T(8,128)(2,1)S(1)} %get-tuple-element.28), channel_id=1, source_target_pairs={{0,25},{1,24},{2,27},{3,26},{4,29},{5,28},{6,31},{7,30},{8,1},{9,0... | collective-permute-start | bytes 614408 | tf_op jit(solution)/shard_map/ppermute | solution.py:29
  38.9 14.9 %collective-permute-start.6 = (bf16[200,512]{1,0:T(8,128)(2,1)S(1)}, bf16[200,512]{1,0:T(8,128)(2,1)S(1)}, u32[]{:S(2)}, u32[]{:S(2)}) collective-permute-start(bf16[200,512]{1,0:T(8,128)(2,1)S(1)} %get-tuple-element.28), channel_id=1, source_target_pairs={{0,24},{1,25},{2,26},{3,27},{4,28},{5,29},{6,30},{7,31},{8,0},{9,1... | collective-permute-start | bytes 614408 | tf_op jit(solution)/shard_map/ppermute | solution.py:29
  44.0 11.8 %collective-permute-start.9 = (bf16[200,512]{1,0:T(8,128)(2,1)S(1)}, bf16[200,512]{1,0:T(8,128)(2,1)S(1)}, u32[]{:S(2)}, u32[]{:S(2)}) collective-permute-start(bf16[200,512]{1,0:T(8,128)(2,1)S(1)} %collective-permute-done.5.earlier.refs_2_), channel_id=1, source_target_pairs={{0,1},{1,0},{2,3},{3,2},{4,5},{5,4},{6,7},{7,6},{8,9},{9,8},{10,11... | collective-permute-start | bytes 614408 | tf_op jit(solution)/shard_map/ppermute | solution.py:29
  58.4 28.8 %all-to-all-start = ((bf16[32,104,128]{2,1,0:T(8,128)(2,1)}), bf16[32,104,128]{2,1,0:T(8,128)(2,1)S(1)}, u32[]{:S(2)}, u32[]{:S(2)}) async-start(bf16[32,104,128]{2,1,0:T(8,128)(2,1)} %get-tuple-element.31), calls=%async_computation | async-start | bytes 1703936 | tf_op jit(solution)/shard_map/all_to_all | solution.py:374

commit v6 on v4

--- a/solution.py
+++ b/solution.py
@@ -327,9 +327,9 @@
         name="pick",
     )(place, far, same, cross, own, partner_root)
     near = [parts[0]] + [shifted(parts[d], d, still) for d in range(1, ring_x)]
-    swapped = [shifted(parts[d], d, to_partner) for d in range(ring_x) if d != 2]
-    swapped.insert(2, shifted(near[2], 0, to_partner))
-
+    swapped = [shifted(parts[0], 0, to_partner)]
+    swapped += [shifted(near[d], 0, to_partner) for d in (1, 2)]
+    swapped.append(shifted(parts[3], 3, to_partner))
     roots, right = pl.pallas_call(
         root_kernel,
         out_shape=[

time: 88.9 us -> 90.6 us (1.019)
  waiting for transfers between devices: 54.5 us -> 57.1 us
    ppermute x11, waiting for transfers between devices: 35.3 us -> 38 us  [shifted(): return lax.ppermute(block, 'fsdp', route)]
  transfers between devices with their start and end apart: 12 -> 12, of which waited for: 9 -> 8; matrix products, arithmetic and copies ran while one was open for 0% -> 0% of each run, Pallas kernels for 7% -> 7%
where the time goes in v6:
time: 90.6 us; the launch traced here: 90.3 us
  waiting for transfers between devices  57.1 us (63%)
  starting transfers between devices  20.8 us (23%)
  Pallas kernels  11.8 us (13%)
    ppermute x11, waiting for transfers between devices, shifted(): return lax.ppermute(block, 'fsdp', route)  38 us
    all_to_all x1, waiting for transfers between devices, local(): lax.all_to_all(payload, 'fsdp', split_axis=0, concat_axis=0, tiled=True)  19.1 us
    ppermute x11, starting transfers between devices, shifted(): return lax.ppermute(block, 'fsdp', route)  16.6 us
    all_to_all x1, starting transfers between devices, local(): lax.all_to_all(payload, 'fsdp', split_axis=0, concat_axis=0, tiled=True)  4.19 us
    pallas_call x1, Pallas kernels, local(): pl.pallas_call(stat_kernel, out_shape=[stat] * 2 + [array(8, lanes, dtype...  3.75 us
    pallas_call x1, Pallas kernels, local(): pl.pallas_call(functools.partial(apply_kernel, clip_limit), out_shape=[ar...  2.66 us
    pallas_call x1, Pallas kernels, local(): pl.pallas_call(functools.partial(finish_kernel, row_blocks, block_size),...  2.49 us
  transfers between devices with their start and end apart: 12, of which 8 were waited for; matrix products, arithmetic and copies ran while one was open for 0% of the time, Pallas kernels for 7%

profile of v6, /device:TPU:8, one launch (start us, length us, event | category | flops | bytes accessed | tf_op | source)
XLA Modules:
  0.0 90.3 jit_solution(8595579081920080033)
XLA Ops:
  0.6 2.0 %collective-permute-start.3 = (bf16[3,256,512]{2,1,0:T(8,128)(2,1)}, bf16[3,256,512]{2,1,0:T(8,128)(2,1)S(1)}, u32[]{:S(2)}, u32[]{:S(2)}) collective-permute-start(bf16[3,256,512]{2,1,0:T(8,128)(2,1)} %bitcast.13), channel_id=1, source_target_pairs={{0,1},{1,0},{2,3},{3,2},{4,5},{5,4},{6,7},{7,6},{8,9},{9,8},{10,11... | collective-permute-start | bytes 2359304 | tf_op jit(solution)/shard_map/ppermute | solution.py:29
  2.6 1.4 %cut.1 = (bf16[200,512]{1,0:T(8,128)(2,1)S(1)}, bf16[200,512]{1,0:T(8,128)(2,1)S(1)}, bf16[200,512]{1,0:T(8,128)(2,1)S(1)}, bf16[200,512]{1,0:T(8,128)(2,1)S(1)}) custom-call(s32[1]{0:T(128)} %bitcast.place, bf16[48,8192]{1,0:T(8,128)(2,1)} %grad.1), custom_call_target="tpu_custom_call" | custom-call | bytes 1048576 | tf_op jit(solution)/shard_map/cut/pallas_call | solution.py:309
  4.0 5.9 %collective-permute-start = (bf16[200,512]{1,0:T(8,128)(2,1)S(1)}, bf16[200,512]{1,0:T(8,128)(2,1)S(1)}, u32[]{:S(2)}, u32[]{:S(2)}) collective-permute-start(bf16[200,512]{1,0:T(8,128)(2,1)S(1)} %get-tuple-element.19), channel_id=1, source_target_pairs={{0,5},{1,4},{2,7},{3,6},{4,1},{5,0},{6,3},{7,2},{8,13},{9,12},{10,... | collective-permute-start | bytes 614408 | tf_op jit(solution)/shard_map/ppermute | solution.py:29
  9.9 1.5 %collective-permute-start.1 = (bf16[200,512]{1,0:T(8,128)(2,1)S(1)}, bf16[200,512]{1,0:T(8,128)(2,1)S(1)}, u32[]{:S(2)}, u32[]{:S(2)}) collective-permute-start(bf16[200,512]{1,0:T(8,128)(2,1)S(1)} %get-tuple-element.20), channel_id=1, source_target_pairs={{0,2},{1,7},{2,4},{3,1},{4,6},{5,3},{6,0},{7,5},{8,10},{9,15},{10,... | collective-permute-start | bytes 614408 | tf_op jit(solution)/shard_map/ppermute | solution.py:29
  11.4 0.0 collective-permute-start.2
  11.4 8.1 %collective-permute-done.refs_0_ = bf16[200,512]{1,0:T(8,128)(2,1)S(1)} collective-permute-done((bf16[200,512]{1,0:T(8,128)(2,1)S(1)}, bf16[200,512]{1,0:T(8,128)(2,1)S(1)}, u32[]{:S(2)}, u32[]{:S(2)}) %collective-permute-start) | collective-permute-done | bytes 204832 | tf_op jit(solution)/shard_map/ppermute | solution.py:29
  19.5 14.8 %collective-permute-done.1.refs_1_ = bf16[200,512]{1,0:T(8,128)(2,1)S(1)} collective-permute-done((bf16[200,512]{1,0:T(8,128)(2,1)S(1)}, bf16[200,512]{1,0:T(8,128)(2,1)S(1)}, u32[]{:S(2)}, u32[]{:S(2)}) %collective-permute-start.1) | collective-permute-done | bytes 204832 | tf_op jit(solution)/shard_map/ppermute | solution.py:29
  34.3 0.0 collective-permute-done.2.refs_2_
  34.3 0.0 collective-permute-done.3.refs_4_.partner_root
  34.3 0.1 pick.1
  34.4 1.6 %collective-permute-start.4 = (bf16[200,512]{1,0:T(8,128)(2,1)S(1)}, bf16[200,512]{1,0:T(8,128)(2,1)S(1)}, u32[]{:S(2)}, u32[]{:S(2)}) collective-permute-start(bf16[200,512]{1,0:T(8,128)(2,1)S(1)} %get-tuple-element.24), channel_id=1, source_target_pairs={{0,8},{1,9},{2,10},{3,11},{4,12},{5,13},{6,14},{7,15},{8,16},{9,17... | collective-permute-start | bytes 614408 | tf_op jit(solution)/shard_map/ppermute | solution.py:29
  35.9 2.7 %collective-permute-start.5 = (bf16[200,512]{1,0:T(8,128)(2,1)S(1)}, bf16[200,512]{1,0:T(8,128)(2,1)S(1)}, u32[]{:S(2)}, u32[]{:S(2)}) collective-permute-start(bf16[200,512]{1,0:T(8,128)(2,1)S(1)} %get-tuple-element.25), channel_id=1, source_target_pairs={{0,16},{1,17},{2,18},{3,19},{4,20},{5,21},{6,22},{7,23},{8,24},{9,... | collective-permute-start | bytes 614408 | tf_op jit(solution)/shard_map/ppermute | solution.py:29
  38.7 0.0 collective-permute-start.10
  38.7 1.4 %collective-permute-start.6 = (bf16[200,512]{1,0:T(8,128)(2,1)S(1)}, bf16[200,512]{1,0:T(8,128)(2,1)S(1)}, u32[]{:S(2)}, u32[]{:S(2)}) collective-permute-start(bf16[200,512]{1,0:T(8,128)(2,1)S(1)} %get-tuple-element.26), channel_id=1, source_target_pairs={{0,24},{1,25},{2,26},{3,27},{4,28},{5,29},{6,30},{7,31},{8,0},{9,1... | collective-permute-start | bytes 614408 | tf_op jit(solution)/shard_map/ppermute | solution.py:29
  40.1 1.5 %collective-permute-start.7 = (bf16[200,512]{1,0:T(8,128)(2,1)S(1)}, bf16[200,512]{1,0:T(8,128)(2,1)S(1)}, u32[]{:S(2)}, u32[]{:S(2)}) collective-permute-start(bf16[200,512]{1,0:T(8,128)(2,1)S(1)} %get-tuple-element.23.refs_0_), channel_id=1, source_target_pairs={{0,1},{1,0},{2,3},{3,2},{4,5},{5,4},{6,7},{7,6},{8,9},{9,8},{10,11... | collective-permute-start | bytes 614408 | tf_op jit(solution)/shard_map/ppermute | solution.py:29
  41.6 1.1 %collective-permute-done.4.refs_1_ = bf16[200,512]{1,0:T(8,128)(2,1)S(1)} collective-permute-done((bf16[200,512]{1,0:T(8,128)(2,1)S(1)}, bf16[200,512]{1,0:T(8,128)(2,1)S(1)}, u32[]{:S(2)}, u32[]{:S(2)}) %collective-permute-start.4) | collective-permute-done | bytes 204832 | tf_op jit(solution)/shard_map/ppermute | solution.py:29
  42.7 0.0 collective-permute-start.8
  42.7 4.3 %collective-permute-done.5.earlier.refs_2_ = bf16[200,512]{1,0:T(8,128)(2,1)S(1)} collective-permute-done((bf16[200,512]{1,0:T(8,128)(2,1)S(1)}, bf16[200,512]{1,0:T(8,128)(2,1)S(1)}, u32[]{:S(2)}, u32[]{:S(2)}) %collective-permute-start.5) | collective-permute-done | bytes 204832 | tf_op jit(solution)/shard_map/ppermute | solution.py:29
  47.0 0.0 collective-permute-start.9
  47.0 1.4 %roots.1 = (bf16[3,512,512]{2,1,0:T(8,128)(2,1)S(1)}, bf16[3,512,256]{2,1,0:T(8,128)(2,1)S(1)}) custom-call(s32[1]{0:T(128)} %bitcast.place, bf16[3,256,512]{2,1,0:T(8,128)(2,1)} %bitcast.14, bf16[3,256,512]{2,1,0:T(8,128)(2,1)S(1)} %collective-permute-done.3.refs_4_.partner_root, bf16[3,512,256]{2,1,0:T(8,128)(2,1)} %bitcast.15, ...), custom_call_target="tpu_custom_call" | custom-call | bytes 4194304 | tf_op jit(solution)/shard_map/roots/pallas_call | solution.py:333
  48.4 3.5 %collective-permute-done.7.refs_4_ = bf16[200,512]{1,0:T(8,128)(2,1)S(1)} collective-permute-done((bf16[200,512]{1,0:T(8,128)(2,1)S(1)}, bf16[200,512]{1,0:T(8,128)(2,1)S(1)}, u32[]{:S(2)}, u32[]{:S(2)}) %collective-permute-start.7) | collective-permute-done | bytes 204832 | tf_op jit(solution)/shard_map/ppermute | solution.py:29
  51.9 0.0 collective-permute-done.10.refs_7_
  51.9 0.0 collective-permute-done.6.refs_3_
  51.9 4.0 %collective-permute-done.8.refs_5_ = bf16[200,512]{1,0:T(8,128)(2,1)S(1)} collective-permute-done((bf16[200,512]{1,0:T(8,128)(2,1)S(1)}, bf16[200,512]{1,0:T(8,128)(2,1)S(1)}, u32[]{:S(2)}, u32[]{:S(2)}) %collective-permute-start.8) | collective-permute-done | bytes 204832 | tf_op jit(solution)/shard_map/ppermute | solution.py:29
  55.9 2.2 %collective-permute-done.9.refs_6_ = bf16[200,512]{1,0:T(8,128)(2,1)S(1)} collective-permute-done((bf16[200,512]{1,0:T(8,128)(2,1)S(1)}, bf16[200,512]{1,0:T(8,128)(2,1)S(1)}, u32[]{:S(2)}, u32[]{:S(2)}) %collective-permute-start.9) | collective-permute-done | bytes 204832 | tf_op jit(solution)/shard_map/ppermute | solution.py:29
  58.1 2.7 %apply.1 = (bf16[1536,512]{1,0:T(8,128)(2,1)S(1)}, bf16[32,104,128]{2,1,0:T(8,128)(2,1)}, f32[8,128]{1,0:T(8,128)S(1)}) custom-call(s32[1]{0:T(128)} %bitcast.place, bf16[200,512]{1,0:T(8,128)(2,1)S(1)} %get-tuple-element.23.refs_0_, bf16[200,512]{1,0:T(8,128)(2,1)S(1)} %collective-permute-done.4.refs_1_, ...), custom_call_target="tpu_custom_call" | custom-call | flops 1207959552 | bytes 6291456 | tf_op jit(solution)/shard_map/apply/pallas_call | solution.py:347
  60.8 4.2 %all-to-all-start = ((bf16[32,104,128]{2,1,0:T(8,128)(2,1)}), bf16[32,104,128]{2,1,0:T(8,128)(2,1)S(1)}, u32[]{:S(2)}, u32[]{:S(2)}) async-start(bf16[32,104,128]{2,1,0:T(8,128)(2,1)} %get-tuple-element.29), calls=%async_computation | async-start | bytes 1703936 | tf_op jit(solution)/shard_map/all_to_all | solution.py:360
  65.0 3.8 %statistics.1 = (f32[3,256,512]{2,1,0:T(8,128)}, f32[3,256,512]{2,1,0:T(8,128)}, f32[8,128]{1,0:T(8,128)S(1)}) custom-call(s32[1]{0:T(128)} %bitcast.place, f32[8,128]{1,0:T(8,128)S(1)} %get-tuple-element.30.clip, bf16[1536,512]{1,0:T(8,128)(2,1)S(1)} %get-tuple-element.31.blocks, f32[3,256,512]{2,1,0:T(8,128)} %bitcast.11, f32[3,256,512]{2,1,0:T(8,128)} %bitcast.12), custom_call_target="tpu_custom_call" | custom-call | flops 805306368 | bytes 8388608 | tf_op jit(solution)/shard_map/statistics/pallas_call | solution.py:361
  68.7 19.1 %all-to-all-done.back = bf16[32,104,128]{2,1,0:T(8,128)(2,1)S(1)} async-done(((bf16[32,104,128]{2,1,0:T(8,128)(2,1)}), bf16[32,104,128]{2,1,0:T(8,128)(2,1)S(1)}, u32[]{:S(2)}, u32[]{:S(2)}) %all-to-all-start) | async-done | bytes 852000 | tf_op jit(solution)/shard_map/all_to_all | solution.py:360
  87.8 2.5 %finish.1 = f32[48,8192]{1,0:T(8,128)} custom-call(s32[1]{0:T(128)} %bitcast.place, bf16[32,104,128]{2,1,0:T(8,128)(2,1)S(1)} %all-to-all-done.back, f32[8,128]{1,0:T(8,128)S(1)} %get-tuple-element.32.clip, f32[48,8192]{1,0:T(8,128)} %momentum.1), custom_call_target="tpu_custom_call" | custom-call | flops 4194304 | bytes 4194304 | tf_op jit(solution)/shard_map/finish/pallas_call | solution.py:377
Async XLA Ops:
  0.6 33.7 %collective-permute-start.3 = (bf16[3,256,512]{2,1,0:T(8,128)(2,1)}, bf16[3,256,512]{2,1,0:T(8,128)(2,1)S(1)}, u32[]{:S(2)}, u32[]{:S(2)}) collective-permute-start(bf16[3,256,512]{2,1,0:T(8,128)(2,1)} %bitcast.13), channel_id=1, source_target_pairs={{0,1},{1,0},{2,3},{3,2},{4,5},{5,4},{6,7},{7,6},{8,9},{9,8},{10,11... | collective-permute-start | bytes 2359304 | tf_op jit(solution)/shard_map/ppermute | solution.py:29
  4.0 15.5 %collective-permute-start = (bf16[200,512]{1,0:T(8,128)(2,1)S(1)}, bf16[200,512]{1,0:T(8,128)(2,1)S(1)}, u32[]{:S(2)}, u32[]{:S(2)}) collective-permute-start(bf16[200,512]{1,0:T(8,128)(2,1)S(1)} %get-tuple-element.19), channel_id=1, source_target_pairs={{0,5},{1,4},{2,7},{3,6},{4,1},{5,0},{6,3},{7,2},{8,13},{9,12},{10,... | collective-permute-start | bytes 614408 | tf_op jit(solution)/shard_map/ppermute | solution.py:29
  9.9 24.3 %collective-permute-start.1 = (bf16[200,512]{1,0:T(8,128)(2,1)S(1)}, bf16[200,512]{1,0:T(8,128)(2,1)S(1)}, u32[]{:S(2)}, u32[]{:S(2)}) collective-permute-start(bf16[200,512]{1,0:T(8,128)(2,1)S(1)} %get-tuple-element.20), channel_id=1, source_target_pairs={{0,2},{1,7},{2,4},{3,1},{4,6},{5,3},{6,0},{7,5},{8,10},{9,15},{10,... | collective-permute-start | bytes 614408 | tf_op jit(solution)/shard_map/ppermute | solution.py:29
  11.4 22.9 %collective-permute-start.2 = (bf16[200,512]{1,0:T(8,128)(2,1)S(1)}, bf16[200,512]{1,0:T(8,128)(2,1)S(1)}, u32[]{:S(2)}, u32[]{:S(2)}) collective-permute-start(bf16[200,512]{1,0:T(8,128)(2,1)S(1)} %get-tuple-element.21), channel_id=1, source_target_pairs={{0,7},{1,2},{2,1},{3,4},{4,3},{5,6},{6,5},{7,0},{8,15},{9,10},{10,... | collective-permute-start | bytes 614408 | tf_op jit(solution)/shard_map/ppermute | solution.py:29
  34.4 8.3 %collective-permute-start.4 = (bf16[200,512]{1,0:T(8,128)(2,1)S(1)}, bf16[200,512]{1,0:T(8,128)(2,1)S(1)}, u32[]{:S(2)}, u32[]{:S(2)}) collective-permute-start(bf16[200,512]{1,0:T(8,128)(2,1)S(1)} %get-tuple-element.24), channel_id=1, source_target_pairs={{0,8},{1,9},{2,10},{3,11},{4,12},{5,13},{6,14},{7,15},{8,16},{9,17... | collective-permute-start | bytes 614408 | tf_op jit(solution)/shard_map/ppermute | solution.py:29
  35.9 11.0 %collective-permute-start.5 = (bf16[200,512]{1,0:T(8,128)(2,1)S(1)}, bf16[200,512]{1,0:T(8,128)(2,1)S(1)}, u32[]{:S(2)}, u32[]{:S(2)}) collective-permute-start(bf16[200,512]{1,0:T(8,128)(2,1)S(1)} %get-tuple-element.25), channel_id=1, source_target_pairs={{0,16},{1,17},{2,18},{3,19},{4,20},{5,21},{6,22},{7,23},{8,24},{9,... | collective-permute-start | bytes 614408 | tf_op jit(solution)/shard_map/ppermute | solution.py:29
  38.7 13.3 %collective-permute-start.10 = (bf16[200,512]{1,0:T(8,128)(2,1)S(1)}, bf16[200,512]{1,0:T(8,128)(2,1)S(1)}, u32[]{:S(2)}, u32[]{:S(2)}) collective-permute-start(bf16[200,512]{1,0:T(8,128)(2,1)S(1)} %get-tuple-element.26), channel_id=1, source_target_pairs={{0,25},{1,24},{2,27},{3,26},{4,29},{5,28},{6,31},{7,30},{8,1},{9,0... | collective-permute-start | bytes 614408 | tf_op jit(solution)/shard_map/ppermute | solution.py:29
  38.7 13.3 %collective-permute-start.6 = (bf16[200,512]{1,0:T(8,128)(2,1)S(1)}, bf16[200,512]{1,0:T(8,128)(2,1)S(1)}, u32[]{:S(2)}, u32[]{:S(2)}) collective-permute-start(bf16[200,512]{1,0:T(8,128)(2,1)S(1)} %get-tuple-element.26), channel_id=1, source_target_pairs={{0,24},{1,25},{2,26},{3,27},{4,28},{5,29},{6,30},{7,31},{8,0},{9,1... | collective-permute-start | bytes 614408 | tf_op jit(solution)/shard_map/ppermute | solution.py:29
  40.1 11.8 %collective-permute-start.7 = (bf16[200,512]{1,0:T(8,128)(2,1)S(1)}, bf16[200,512]{1,0:T(8,128)(2,1)S(1)}, u32[]{:S(2)}, u32[]{:S(2)}) collective-permute-start(bf16[200,512]{1,0:T(8,128)(2,1)S(1)} %get-tuple-element.23.refs_0_), channel_id=1, source_target_pairs={{0,1},{1,0},{2,3},{3,2},{4,5},{5,4},{6,7},{7,6},{8,9},{9,8},{10,11... | collective-permute-start | bytes 614408 | tf_op jit(solution)/shard_map/ppermute | solution.py:29
  42.7 13.2 %collective-permute-start.8 = (bf16[200,512]{1,0:T(8,128)(2,1)S(1)}, bf16[200,512]{1,0:T(8,128)(2,1)S(1)}, u32[]{:S(2)}, u32[]{:S(2)}) collective-permute-start(bf16[200,512]{1,0:T(8,128)(2,1)S(1)} %collective-permute-done.4.refs_1_), channel_id=1, source_target_pairs={{0,1},{1,0},{2,3},{3,2},{4,5},{5,4},{6,7},{7,6},{8,9},{9,8},{10,11... | collective-permute-start | bytes 614408 | tf_op jit(solution)/shard_map/ppermute | solution.py:29
  47.0 11.1 %collective-permute-start.9 = (bf16[200,512]{1,0:T(8,128)(2,1)S(1)}, bf16[200,512]{1,0:T(8,128)(2,1)S(1)}, u32[]{:S(2)}, u32[]{:S(2)}) collective-permute-start(bf16[200,512]{1,0:T(8,128)(2,1)S(1)} %collective-permute-done.5.earlier.refs_2_), channel_id=1, source_target_pairs={{0,1},{1,0},{2,3},{3,2},{4,5},{5,4},{6,7},{7,6},{8,9},{9,8},{10,11... | collective-permute-start | bytes 614408 | tf_op jit(solution)/shard_map/ppermute | solution.py:29
  60.8 27.0 %all-to-all-start = ((bf16[32,104,128]{2,1,0:T(8,128)(2,1)}), bf16[32,104,128]{2,1,0:T(8,128)(2,1)S(1)}, u32[]{:S(2)}, u32[]{:S(2)}) async-start(bf16[32,104,128]{2,1,0:T(8,128)(2,1)} %get-tuple-element.29), calls=%async_computation | async-start | bytes 1703936 | tf_op jit(solution)/shard_map/all_to_all | solution.py:360
